TPU v7x, 32 devices: a whole 2x2x4 slice. The times are simulated.
32 devices in a mesh: dp: 2 (over core), seq: 16 (over z, y, x).
Axes of the slice: x: 2, y: 2, z: 4, core: 2. Of those that a mesh axis runs over, the one named last changes fastest.
Arguments:
- byte_ids: int32 [32, 4096], P('dp', 'seq'), may hold values from 0 to 255
- lengths: int32 [32], P('dp'), may hold values from 1024 to 4096, as said below
- embedding: float32 [256, 768], replicated, may hold values from -6 to 6
- conv_weight: float32 [4, 768], replicated, may hold values from -3 to 3
- conv_bias: float32 [768], replicated, may hold values from -3 to 3
- score_weight: float32 [768], replicated, may hold values from -0.5 to 0.5
- cotangent: float32 [32, 2048, 768], P('dp', 'seq'), may hold values from -6 to 6
Outputs:
- latent: float32 [32, 2048, 768], P('dp', 'seq')
- grad_embedding: float32 [256, 768], replicated
- grad_conv_weight: float32 [4, 768], replicated
- grad_conv_bias: float32 [768], replicated
- grad_score_weight: float32 [768], replicated
Inputs may be any that keep to these rules, and one draw needn't show every extreme that they name: `lengths`: among the 16 rows of each index of dp one has length 4096 and one has length 1024, which ones drawn from the seed.
All inputs are finite; a program needn't handle non-finite values.
Results may differ from a plain program's by a relative error of at most 0.0003.
Values sent between devices are 32-bit elements; how exact they have to be, the bound alone decides.
No kernel may reach another device: no remote copies, remote signals or barrier semaphores. Data moves between devices by JAX's collectives and lax.ppermute only.
A program may use at most 448 MiB of HBM per device.

v0:
```python
import jax
import jax.numpy as jnp
from jax import lax
from jax.sharding import PartitionSpec as P

HIGH = lax.Precision.HIGHEST


def with_halo(block, sides, width):
    for axis, dim in sides:
        count = lax.axis_size(axis)
        forward = [(i, i + 1) for i in range(count - 1)]
        backward = [(target, source) for source, target in forward]
        low = lax.ppermute(
            lax.slice_in_dim(block, block.shape[dim] - width, None, axis=dim), axis, forward
        )
        high = lax.ppermute(lax.slice_in_dim(block, 0, width, axis=dim), axis, backward)
        block = jnp.concatenate([low, block, high], axis=dim)
    return block


def one_hot_rows(ids, vocab):
    flat = ids.reshape(-1)
    return (flat[:, None] == jnp.arange(vocab)[None, :]).astype(jnp.float32)


def lookup(ids, table):
    picked = jnp.dot(one_hot_rows(ids, table.shape[0]), table, precision=HIGH)
    return picked.reshape(ids.shape + (table.shape[1],))


def live_mask(first, count, lengths):
    positions = first + jnp.arange(count)
    inside = (positions[None, :] >= 0) & (positions[None, :] < lengths[:, None])
    return inside.astype(jnp.float32)[:, :, None]


def convolve(x_wide, weight, bias, mask):
    count = x_wide.shape[1] - 4
    total = bias[None, None, :] + sum(
        (weight[k][None, None, :] * x_wide[:, k : k + count] for k in range(4))
    )
    return mask * total


def pool_mix(c_wide, scorer, start):
    core = c_wide[:, 2:-2]
    rows, span, width = core.shape
    pair = jnp.repeat(jnp.mean(core.reshape(rows, span // 2, 2, width), axis=2), 2, axis=1)
    quad = jnp.repeat(jnp.mean(core.reshape(rows, span // 4, 4, width), axis=2), 4, axis=1)
    offset = (start + jnp.arange(span)) % 3
    triple = jnp.zeros_like(core)
    for shift_by in range(-2, 3):
        coef = ((shift_by >= -offset) & (shift_by <= 2 - offset)).astype(jnp.float32) / 3.0
        triple = triple + coef[None, :, None] * c_wide[:, 2 + shift_by : 2 + shift_by + span]
    stack = jnp.stack([core, pair, triple, quad])
    scores = jnp.dot(stack, scorer, precision=HIGH)
    weights = jax.nn.softmax(scores, axis=0)
    mixed = jnp.sum(weights[..., None] * stack, axis=0)
    return jnp.mean(mixed.reshape(rows, span // 2, 2, width), axis=2)


def return_rims(grad_wide, returned):
    core = grad_wide[:, 2:-2]
    core = core.at[:, :2].add(returned[:, :2])
    return core.at[:, -2:].add(returned[:, -2:])


def per_device(byte_ids, lengths, embedding, conv_weight, conv_bias, score_weight, cotangent):
    rows, span = byte_ids.shape
    start = lax.axis_index("seq") * span
    core_mask = live_mask(start, span, lengths)
    x_core = lookup(byte_ids, embedding) * core_mask
    x_wide = with_halo(x_core, (("seq", 1),), 2)

    def first_piece(x_in, weight, bias):
        return convolve(x_in, weight, bias, core_mask)

    c_core, first_back = jax.vjp(first_piece, x_wide, conv_weight, conv_bias)
    c_wide = with_halo(c_core, (("seq", 1),), 2)

    def second_piece(c_in, scorer):
        return pool_mix(c_in, scorer, start)

    latent, second_back = jax.vjp(second_piece, c_wide, score_weight)
    d_cwide, grad_score = second_back(cotangent)
    conv_edges = jnp.concatenate([d_cwide[:, :2], d_cwide[:, -2:]], axis=1)
    conv_back = with_halo(conv_edges, (("seq", 1),), 2)
    d_core = return_rims(d_cwide, conv_back)
    d_xwide, grad_weight, grad_bias = first_back(d_core)
    embed_edges = jnp.concatenate([d_xwide[:, :2], d_xwide[:, -2:]], axis=1)
    embed_back = with_halo(embed_edges, (("seq", 1),), 2)
    d_embedded = return_rims(d_xwide, embed_back) * core_mask
    grad_table = jnp.dot(
        one_hot_rows(byte_ids, embedding.shape[0]).T,
        d_embedded.reshape(-1, d_embedded.shape[2]),
        precision=HIGH,
    )
    terms = (grad_table, grad_weight, grad_bias, grad_score)
    summed = lax.psum((terms[0], terms[1], terms[2], terms[3]), ("dp", "seq"))
    return (latent, summed[0], summed[1], summed[2], summed[3])


def solution(mesh):
    placed = (P("dp", "seq"), P("dp"), P(), P(), P(), P(), P("dp", "seq", None))
    return jax.shard_map(
        per_device,
        mesh=mesh,
        in_specs=placed,
        out_specs=(P("dp", "seq", None), P(), P(), P(), P()),
        check_vma=False,
    )
```

profile of v0, /device:TPU:0, one launch (start us, length us, event | category | flops | bytes accessed | tf_op | source)
XLA Modules:
  0.0 847.0 jit_solution(10907904348559611445)
XLA Ops:
  44.9 15.8 %reshape.293 = f32[16,256,768]{2,1,0:T(8,128)} reshape(f32[16,128,2,768]{3,2,1,0:T(2,128)} %broadcast_in_dim.26) | data formatting | bytes 25165824 | tf_op jit(solution)/shard_map/transpose(jvp())/reshape | solution.py:60
  60.8 22.3 %add_multiply_fusion = f32[16,256,768]{2,1,0:T(8,128)S(1)} fusion(f32[16,256,768]{2,1,0:T(8,128)} %broadcast_multiply_fusion.1, f32[16,2,768]{2,1,0:T(2,128)S(1)} %collective-permute-done, f32[16,2,768]{2,1,0:T(2,128)S(1)} %collective-permute-done.1, f32[768]{0:T(1024)S(1)} %get-tuple-element.65, f32[768]{0:T(1024)S(1)} %get-tuple-element.66, ...), kind=kLoop, calls=%fused_computation.37 | loop fusion | flops 37748736 | bytes 25394176 | tf_op jit(solution)/shard_map/jvp()/mul | solution.py:43
  102.3 15.1 %reshape.288 = f32[16,128,2,768]{3,2,1,0:T(2,128)} reshape(f32[16,256,768]{2,1,0:T(8,128)} %copy-done.2) | data formatting | bytes 25165824 | tf_op jit(solution)/shard_map/jvp()/reshape | solution.py:49
  135.6 19.3 %reduce_sum.121 = f32[16,128,768]{2,1,0:T(8,128)} reduce(f32[16,128,2,768]{3,2,1,0:T(2,128)} %reshape.288, f32[]{:T(128)} %constant.139.clone.1), dimensions={2}, to_apply=%region_0.0 | reduce | flops 1572864 | bytes 18874372 | tf_op jit(solution)/shard_map/jvp()/reduce_sum | solution.py:49
  167.5 14.8 %reshape.291 = f32[1,16,256,768]{3,2,1,0:T(8,128)} reshape(f32[16,64,4,768]{3,2,1,0:T(4,128)} %broadcast_in_dim.25) | data formatting | bytes 25165824 | tf_op jit(solution)/shard_map/jvp()/stack;jvp()/reshape | solution.py:56
  191.4 15.7 %reshape.289 = f32[1,16,256,768]{3,2,1,0:T(8,128)} reshape(f32[16,128,2,768]{3,2,1,0:T(2,128)} %broadcast_in_dim.24) | data formatting | bytes 25165824 | tf_op jit(solution)/shard_map/jvp()/stack;jvp()/reshape | solution.py:56
  207.2 29.1 %fusion.4 = f32[1,16,256,768]{3,2,1,0:T(8,128)} fusion(f32[16,256,768]{2,1,0:T(8,128)} %copy-done.2, f32[16,2,768]{2,1,0:T(2,128)S(1)} %collective-permute-done.3, f32[16,2,768]{2,1,0:T(2,128)S(1)} %collective-permute-done.2, f32[256]{0:T(256)S(1)} %get-tuple-element.90, f32[256]{0:T(256)S(1)} %get-tuple-element.91, f32[256]{0:T(256)S(1)} %get-tuple-element.92, ...), kind=kLoop, calls=%fused_computation.16 | loop fusion | flops 40894464 | bytes 25367552 | tf_op jit(solution)/shard_map/jvp()/stack | solution.py:56
  236.2 47.0 %fusion.31 = f32[1,4,16,256]{3,0,2,1:T(1,128)S(1)} fusion(f32[768,1,1,1]{0,1,2,3:T(1,128)S(1)} %reshape.297, f32[1,16,256,768]{3,2,1,0:T(8,128)} %reshape.291, f32[1,16,256,768]{3,2,1,0:T(8,128)} %fusion.4, f32[1,16,256,768]{3,2,1,0:T(8,128)S(1)} %copy-done.4, f32[1,16,256,768]{3,2,1,0:T(8,128)} %bitcast.55), kind=kOutput, calls=%fused_computation.86 | convolution fusion | flops 188743680 | bytes 50400256 | tf_op jit(solution)/shard_map/jvp()/dot_general | solution.py:57
  283.4 25.2 %multiply_reduce_fusion = (f32[4,16,256]{2,1,0:T(8,128)S(1)}, f32[16,256,768]{2,1,0:T(8,128)}) fusion(f32[16,256,768]{2,1,0:T(8,128)} %reshape.293, f32[1,16,256,768]{3,2,1,0:T(8,128)} %reshape.291, f32[1,16,256,768]{3,2,1,0:T(8,128)} %fusion.4, f32[1,16,256,768]{3,2,1,0:T(8,128)} %reshape.289, f32[1,16,256,768]{3,2,1,0:T(8,128)} %bitcast.56, ...), kind=kLoop, calls=%fused_computation.2 | loop fusion | flops 84918272 | bytes 75628544 | tf_op jit(solution)/shard_map/transpose(jvp())/reduce_sum | solution.py:59
  308.6 21.5 %multiply_add_fusion = f32[4,16,256,768]{3,2,1,0:T(8,128)} fusion(f32[768]{0:T(1024)S(1)} %copy-done.22, f32[4,16,256]{2,1,0:T(8,128)S(1)} %add_multiply_fusion.1, f32[16,256,768]{2,1,0:T(8,128)} %reshape.293, f32[4,16,256]{2,1,0:T(8,128)S(1)} %broadcast_divide_fusion), kind=kLoop, calls=%fused_computation.1 | loop fusion | flops 37748736 | bytes 63048704 | tf_op jit(solution)/shard_map/transpose(jvp())/add_any | solution.py:57
  330.1 18.5 %fusion.35 = (f32[1,16,256,768]{3,2,1,0:T(8,128)}, f32[1,16,256,768]{3,2,1,0:T(8,128)}) fusion(f32[4,16,256,768]{3,2,1,0:T(8,128)} %multiply_add_fusion), kind=kLoop, calls=%fused_computation.102 | loop fusion | bytes 50331648 | tf_op jit(solution)/shard_map/transpose(jvp())/unstack | solution.py:56
  348.6 14.7 %unstack.29 = f32[16,64,4,768]{3,2,1,0:T(4,128)} reshape(f32[1,16,256,768]{3,2,1,0:T(8,128)} %get-tuple-element.80) | data formatting | bytes 25165824 | tf_op jit(solution)/shard_map/transpose(jvp())/reshape;transpose(jvp())/unstack | solution.py:50
  383.3 14.8 %reshape.294 = f32[16,256,768]{2,1,0:T(8,128)} reshape(f32[16,64,4,768]{3,2,1,0:T(4,128)} %broadcast_in_dim.57) | data formatting | bytes 25165824 | tf_op jit(solution)/shard_map/transpose(jvp())/reshape | solution.py:50
  398.2 15.1 %unstack.31 = f32[16,128,2,768]{3,2,1,0:T(2,128)} reshape(f32[1,16,256,768]{3,2,1,0:T(8,128)} %get-tuple-element.81) | data formatting | bytes 25165824 | tf_op jit(solution)/shard_map/transpose(jvp())/reshape;transpose(jvp())/unstack | solution.py:49
  413.3 19.3 %reduce_sum.135 = f32[16,128,768]{2,1,0:T(8,128)} reduce(f32[16,128,2,768]{3,2,1,0:T(2,128)} %unstack.31, f32[]{:T(128)} %constant.139.clone.1), dimensions={2}, to_apply=%region_9.10 | reduce | flops 1572864 | bytes 18874372 | tf_op jit(solution)/shard_map/transpose(jvp())/reduce_sum | solution.py:49
  442.6 15.7 %reshape.295 = f32[16,256,768]{2,1,0:T(8,128)} reshape(f32[16,128,2,768]{3,2,1,0:T(2,128)} %broadcast_in_dim.58) | data formatting | bytes 25165824 | tf_op jit(solution)/shard_map/transpose(jvp())/reshape | solution.py:49
  458.3 37.5 %fusion.18 = (f32[16,256,768]{2,1,0:T(8,128)S(1)}, f32[16,256,768]{2,1,0:T(8,128)}, f32[16,256,768]{2,1,0:T(8,128)}, f32[16,256,768]{2,1,0:T(8,128)}, f32[16,256,768]{2,1,0:T(8,128)}, /*index=5*/f32[16,256,768]{2,1,0:T(8,128)}) fusion(f32[4,16,256,768]{3,2,1,0:T(8,128)} %multiply_add_fusion, f32[256]{0:T(256)S(1)} %get-tuple-element.90, ...), kind=kLoop, calls=%fused_computation.42 | loop fusion | flops 22020096 | bytes 125834240 | tf_op jit(solution)/shard_map/transpose(jvp())/mul | solution.py:55
  501.7 29.5 %pad_add_fusion.1 = f32[16,260,768]{2,1,0:T(8,128)} fusion(f32[16,256,768]{2,1,0:T(8,128)} %get-tuple-element.79, f32[16,256,768]{2,1,0:T(8,128)} %get-tuple-element.78, f32[16,256,768]{2,1,0:T(8,128)} %get-tuple-element.77, f32[16,256,768]{2,1,0:T(8,128)} %get-tuple-element.76, f32[16,256,768]{2,1,0:T(8,128)} %get-tuple-element.75, f32[16,256,768]{2,1,0:T(8,128)} %copy-done.3), kind=kLoop, calls=%fused_computation.11 | loop fusion | flops 15974400 | bytes 88276992 | tf_op jit(solution)/shard_map/transpose(jvp())/add_any | solution.py:47
  531.2 27.6 %fusion.23 = f32[768]{0:T(1024)S(1)} fusion(f32[4,16,256,1]{2,1,0,3:T(8,128)S(1)} %bitcast.62, f32[1,16,256,768]{3,2,1,0:T(8,128)} %reshape.291, f32[1,16,256,768]{3,2,1,0:T(8,128)} %fusion.4, f32[1,16,256,768]{3,2,1,0:T(8,128)} %reshape.289, f32[1,16,256,768]{3,2,1,0:T(8,128)} %bitcast.57), kind=kOutput, calls=%fused_computation.62 | convolution fusion | flops 188743680 | bytes 50400256 | tf_op jit(solution)/shard_map/transpose(jvp())/dot_general | solution.py:57
  563.4 15.8 %bitcast_reduce_fusion = f32[16,128,768]{2,0,1:T(8,128)} fusion(f32[16,256,768]{2,1,0:T(8,128)} %get-tuple-element.54), kind=kLoop, calls=%fused_computation.32 | loop fusion | flops 1572864 | bytes 18874368 | tf_op jit(solution)/shard_map/jvp()/reduce_sum | solution.py:60
  595.3 41.2 %multiply_reduce_fusion.6 = (f32[768]{0:T(1024)S(1)}, f32[768]{0:T(1024)S(1)}, f32[768]{0:T(1024)S(1)}, f32[768]{0:T(1024)S(1)}, f32[768]{0:T(1024)S(1)}, /*inde...) fusion(f32[16,256,768]{2,1,0:T(8,128)} %fusion.26, ...), kind=kLoop, calls=%fused_computation.43 | loop fusion | flops 56619264 | bytes 88321024 | tf_op jit(solution)/shard_map/transpose(jvp())/reduce_sum | solution.py:40
  642.4 22.4 %pad_add_fusion = f32[16,260,768]{2,1,0:T(8,128)} fusion(f32[16,256,768]{2,1,0:T(8,128)} %get-tuple-element.82, f32[16,256,768]{2,1,0:T(8,128)} %get-tuple-element.83, f32[16,256,768]{2,1,0:T(8,128)} %get-tuple-element.84, f32[16,256,768]{2,1,0:T(8,128)} %get-tuple-element.85), kind=kLoop, calls=%fused_computation.10 | loop fusion | flops 9584640 | bytes 63111168 | tf_op jit(solution)/shard_map/transpose(jvp())/add_any | solution.py:41
  713.1 46.1 %all-reduce.14 = (f32[4,768]{1,0:T(4,128)}, f32[768]{0:T(1024)}, f32[768]{0:T(1024)}) all-reduce(f32[4,768]{1,0:T(4,128)S(1)} %pad_add_fusion.6, f32[768]{0:T(1024)S(1)} %get-tuple-element.58, f32[768]{0:T(1024)S(1)} %fusion.23), channel_id=1, replica_groups=mesh['dp'=2,'seq'=16] {'dp','seq'}, use_global_device_ids=true, to_apply=%region_15.16 | all-reduce | flops 4608 | bytes 36864 | tf_op jit(solution)/shard_map/psum | solution.py:100
  759.2 78.7 %all-reduce.17.cloned.1.call-done = f32[256,768]{1,0:T(8,128)} async-done(((f32[256,768]{1,0:T(8,128)}), f32[256,768]{1,0:T(8,128)}) %all-reduce.17.cloned.1.call-update) | async-done | bytes 786448 | tf_op jit(solution)/shard_map/psum | solution.py:100
  (120 shorter events, 209.5 us)
Async XLA Ops:
  7.2 9.6 %copy-start.25 = (s32[16]{0:T(128)S(1)}, s32[16]{0:T(128)}, u32[]{:S(2)}) copy-start(s32[16]{0:T(128)} %param.16) | copy-start | bytes 196
  7.2 830.7 %all-reduce.17.cloned.1.call-start = ((), (), s32[]{:S(2)}) async-start(), calls=%async_computation | async-start | bytes 1572864 | tf_op jit(solution)/shard_map/psum | solution.py:100
  16.9 43.9 %copy-start.8 = (f32[16,256]{1,0:T(8,128)}, f32[16,256]{1,0:T(8,128)S(1)}, u32[]{:S(2)}) copy-start(f32[16,256]{1,0:T(8,128)S(1)} %and_convert_fusion) | copy-start | bytes 49156
  16.9 18.0 %copy-start.22 = (f32[768]{0:T(1024)S(1)}, f32[768]{0:T(1024)}, u32[]{:S(2)}) copy-start(f32[768]{0:T(1024)} %param.20) | copy-start | bytes 9220
  16.9 18.0 %copy-start.23 = (f32[4,768]{1,0:T(4,128)S(1)}, f32[4,768]{1,0:T(4,128)}, u32[]{:S(2)}) copy-start(f32[4,768]{1,0:T(4,128)} %param.18) | copy-start | bytes 36868
  28.0 32.7 %collective-permute-start.1 = (f32[16,2,768]{2,1,0:T(2,128)S(1)}, f32[16,2,768]{2,1,0:T(2,128)S(1)}, u32[]{:S(2)}, u32[]{:S(2)}) collective-permute-start(f32[16,2,768]{2,1,0:T(2,128)S(1)} %get-tuple-element.88), channel_id=1, source_target_pairs={{1,0},{2,1},{3,2},{4,3},{5,4},{6,5},{7,6},{8,7},{9,8},{10,9},{11,1... | collective-permute-start | bytes 294920 | tf_op jit(solution)/shard_map/ppermute | solution.py:17
  29.3 31.5 %collective-permute-start = (f32[16,2,768]{2,1,0:T(2,128)S(1)}, f32[16,2,768]{2,1,0:T(2,128)S(1)}, u32[]{:S(2)}, u32[]{:S(2)}) collective-permute-start(f32[16,2,768]{2,1,0:T(2,128)S(1)} %get-tuple-element.89), channel_id=1, source_target_pairs={{0,1},{1,2},{2,3},{3,4},{4,5},{5,6},{6,7},{7,8},{8,9},{9,10},{10,1... | collective-permute-start | bytes 294920 | tf_op jit(solution)/shard_map/ppermute | solution.py:14
  34.9 25.9 %copy-start.14 = (f32[768]{0:T(1024)}, f32[768]{0:T(1024)S(1)}, u32[]{:S(2)}) copy-start(f32[768]{0:T(1024)S(1)} %get-tuple-element.63) | copy-start | bytes 9220
  34.9 25.9 %copy-start.16 = (f32[768]{0:T(1024)}, f32[768]{0:T(1024)S(1)}, u32[]{:S(2)}) copy-start(f32[768]{0:T(1024)S(1)} %get-tuple-element.64) | copy-start | bytes 9220
  34.9 25.9 %copy-start.18 = (f32[768]{0:T(1024)}, f32[768]{0:T(1024)S(1)}, u32[]{:S(2)}) copy-start(f32[768]{0:T(1024)S(1)} %get-tuple-element.65) | copy-start | bytes 9220
  34.9 25.9 %copy-start.20 = (f32[768]{0:T(1024)}, f32[768]{0:T(1024)S(1)}, u32[]{:S(2)}) copy-start(f32[768]{0:T(1024)S(1)} %get-tuple-element.66) | copy-start | bytes 9220
  44.9 15.9 %copy-start.24 = (f32[768]{0:T(1024)S(1)}, f32[768]{0:T(1024)}, u32[]{:S(2)}) copy-start(f32[768]{0:T(1024)} %param.19) | copy-start | bytes 9220
  60.7 22.4 %copy-start.10 = (f32[16,2,768]{2,1,0:T(2,128)}, f32[16,2,768]{2,1,0:T(2,128)S(1)}, u32[]{:S(2)}) copy-start(f32[16,2,768]{2,1,0:T(2,128)S(1)} %collective-permute-done.1) | copy-start | bytes 294916
  60.8 22.4 %copy-start.12 = (f32[16,2,768]{2,1,0:T(2,128)}, f32[16,2,768]{2,1,0:T(2,128)S(1)}, u32[]{:S(2)}) copy-start(f32[16,2,768]{2,1,0:T(2,128)S(1)} %collective-permute-done) | copy-start | bytes 294916
  117.4 89.8 %collective-permute-start.2 = (f32[16,2,768]{2,1,0:T(2,128)S(1)}, f32[16,2,768]{2,1,0:T(2,128)S(1)}, u32[]{:S(2)}, u32[]{:S(2)}) collective-permute-start(f32[16,2,768]{2,1,0:T(2,128)S(1)} %get-tuple-element.86), channel_id=1, source_target_pairs={{0,1},{1,2},{2,3},{3,4},{4,5},{5,6},{6,7},{7,8},{8,9},{9,10},{10,1... | collective-permute-start | bytes 294920 | tf_op jit(solution)/shard_map/ppermute | solution.py:14
  122.2 85.0 %collective-permute-start.3 = (f32[16,2,768]{2,1,0:T(2,128)S(1)}, f32[16,2,768]{2,1,0:T(2,128)S(1)}, u32[]{:S(2)}, u32[]{:S(2)}) collective-permute-start(f32[16,2,768]{2,1,0:T(2,128)S(1)} %get-tuple-element.87), channel_id=1, source_target_pairs={{1,0},{2,1},{3,2},{4,3},{5,4},{6,5},{7,6},{8,7},{9,8},{10,9},{11,1... | collective-permute-start | bytes 294920 | tf_op jit(solution)/shard_map/ppermute | solution.py:17
  154.9 6.2 copy-start.5
  207.2 29.1 %copy-start.4 = (f32[1,16,256,768]{3,2,1,0:T(8,128)S(1)}, f32[1,16,256,768]{3,2,1,0:T(8,128)}, u32[]{:S(2)}) copy-start(f32[1,16,256,768]{3,2,1,0:T(8,128)} %reshape.289) | copy-start | bytes 37748740
  558.8 32.3 %collective-permute-start.4 = (f32[16,2,768]{2,1,0:T(2,128)S(1)}, f32[16,2,768]{2,1,0:T(2,128)S(1)}, u32[]{:S(2)}, u32[]{:S(2)}) collective-permute-start(f32[16,2,768]{2,1,0:T(2,128)S(1)} %get-tuple-element.71), channel_id=1, source_target_pairs={{0,1},{1,2},{2,3},{3,4},{4,5},{5,6},{6,7},{7,8},{8,9},{9,10},{10,1... | collective-permute-start | bytes 294920 | tf_op jit(solution)/shard_map/ppermute | solution.py:14
  579.2 14.4 %collective-permute-start.5 = (f32[16,2,768]{2,1,0:T(2,128)S(1)}, f32[16,2,768]{2,1,0:T(2,128)S(1)}, u32[]{:S(2)}, u32[]{:S(2)}) collective-permute-start(f32[16,2,768]{2,1,0:T(2,128)S(1)} %get-tuple-element.70), channel_id=1, source_target_pairs={{1,0},{2,1},{3,2},{4,3},{5,4},{6,5},{7,6},{8,7},{9,8},{10,9},{11,1... | collective-permute-start | bytes 294920 | tf_op jit(solution)/shard_map/ppermute | solution.py:17
  637.9 39.0 %collective-permute-start.6 = (f32[16,2,768]{2,1,0:T(2,128)S(1)}, f32[16,2,768]{2,1,0:T(2,128)S(1)}, u32[]{:S(2)}, u32[]{:S(2)}) collective-permute-start(f32[16,2,768]{2,1,0:T(2,128)S(1)} %get-tuple-element.73), channel_id=1, source_target_pairs={{0,1},{1,2},{2,3},{3,4},{4,5},{5,6},{6,7},{7,8},{8,9},{9,10},{10,1... | collective-permute-start | bytes 294920 | tf_op jit(solution)/shard_map/ppermute | solution.py:14
  664.8 14.2 %collective-permute-start.7 = (f32[16,2,768]{2,1,0:T(2,128)S(1)}, f32[16,2,768]{2,1,0:T(2,128)S(1)}, u32[]{:S(2)}, u32[]{:S(2)}) collective-permute-start(f32[16,2,768]{2,1,0:T(2,128)S(1)} %get-tuple-element.72), channel_id=1, source_target_pairs={{1,0},{2,1},{3,2},{4,3},{5,4},{6,5},{7,6},{8,7},{9,8},{10,9},{11,1... | collective-permute-start | bytes 294920 | tf_op jit(solution)/shard_map/ppermute | solution.py:17
  680.7 10.1 %copy-start.7 = (s32[2,2,8,128]{3,1,2,0:T(2,128)S(1)}, s32[2,2,8,128]{3,1,2,0:T(2,128)}, u32[]{:S(2)}) copy-start(s32[2,2,8,128]{3,1,2,0:T(2,128)} %copy-done.6) | copy-start | bytes 49156
  690.8 149.1 %copy-start.1 = (f32[256,768]{1,0:T(8,128)S(1)}, f32[256,768]{1,0:T(8,128)}, u32[]{:S(2)}) copy-start(f32[256,768]{1,0:T(8,128)} %param.17) | copy-start | bytes 2359300
  (11 other events, 40.3 us)
Sparse Core Ops, SparseCore 0:
  703.4 134.4 all-reduce.16
where the time goes:
time: 860 us; the launch traced here: 847 us
  other arithmetic  363 us (42%)
  local copies, waits for them, and re-layouts  224 us (26%)
  matrix products  95.2 us (11%)
  waiting for transfers between devices  78.7 us (9%)
  blocking collectives  46.1 us (5%)
  starting transfers between devices  25 us (3%)
  between operations  14.8 us (2%)
    psum x1, waiting for transfers between devices, per_device(): summed = lax.psum((terms[0], terms[1], terms[2], terms[3]), ('dp', 'seq'))  78.7 us
    dot_general x2, matrix products, pool_mix(): scores = jnp.dot(stack, scorer, precision=HIGH)  74.6 us
    psum x1, blocking collectives, per_device(): summed = lax.psum((terms[0], terms[1], terms[2], terms[3]), ('dp', 'seq'))  46.1 us
    reduce_sum x1, other arithmetic, convolve(): bias[None, None, :]  41.2 us
    mul x1, other arithmetic, pool_mix(): coef[None, :, None] * c_wide[:, 2 + shift_by:2 + shift_by + span]  37.5 us
    reshape x2, local copies, waits for them, and re-layouts, pool_mix(): core.reshape(rows, span // 2, 2, width)  30.8 us
    reshape x2, local copies, waits for them, and re-layouts, pool_mix(): stack = jnp.stack([core, pair, triple, quad])  30.5 us
    add_any x1, other arithmetic, pool_mix(): core = c_wide[:, 2:-2]  29.5 us
  transfers between devices with their start and end apart: 9, of which 1 were waited for; matrix products, arithmetic and copies ran while one was open for 22% of the time, Pallas kernels for 0%

commit v1 on v0

v1 whole, which is shorter than its diff:
```python
import functools

import jax
import jax.numpy as jnp
from jax import lax
from jax.experimental import pallas as pl
from jax.experimental.pallas import tpu as pltpu
from jax.sharding import PartitionSpec as P

F32, BF16, I32 = jnp.float32, jnp.bfloat16, jnp.int32
HIGH = lax.Precision.HIGHEST
ROWS = 16
TAPS = 4
RELS = (-2, -1, 0, 1, 2, 3)
VMEM = pltpu.CompilerParams(vmem_limit_bytes=60 * 1024 * 1024)
NT = (((1,), (1,)), ((), ()))
TN = (((0,), (0,)), ((), ()))


def lanes(shape):
    return lax.broadcasted_iota(I32, shape, 1)


def pick(x, index):
    return jnp.take_along_axis(x, index, axis=1, mode="promise_in_bounds")


def split(x):
    high = x.astype(BF16)
    return high, (x - high.astype(F32)).astype(BF16)


def dot(a, b, dims=(((1,), (0,)), ((), ()))):
    return lax.dot_general(a, b, dims, preferred_element_type=F32)


def ahead(x):
    lane = lanes(x.shape) % 8
    below = pltpu.roll(x, x.shape[0] - 1, 0)
    return jnp.where(lane == 7, pltpu.roll(below, 7, 1), pltpu.roll(x, 127, 1))


def behind(x):
    lane = lanes(x.shape) % 8
    above = pltpu.roll(x, 1, 0)
    return jnp.where(lane == 0, pltpu.roll(above, 121, 1), pltpu.roll(x, 1, 1))


def geometry(shape, start, len_ref):
    lane = lanes(shape)
    window = lax.broadcasted_iota(I32, shape, 0) - 8
    even = start + 16 * window + 2 * (lane % 8)
    length = jnp.zeros(shape, I32)
    for r in range(ROWS):
        length = jnp.where(lane // 8 == r, len_ref[r], length)
    return even, length


def alive(pos, length):
    return (pos >= 0) & (pos < length)


def members(even, parity):
    offset = (even + parity) % 3
    left = (even // 2) % 2 == 0
    out = [[((parity,), None)], [((0, 1), None)], [], []]
    for o in range(3):
        out[2].append((tuple(parity - o + i for i in range(3)), offset == o))
    out[3] = [((0, 1, 2, 3), left), ((-2, -1, 0, 1), ~left)]
    return out


def to_chunks(xe, xo, g):
    lane = lanes(xe.shape)
    place = (lane // 8 + 12) % 16
    index = g * 64 + (lane % 8) * 8 + place // 2
    y = jnp.where(place % 2 == 0, pick(xe, index), pick(xo, index))
    return jnp.where(lane < 32, pltpu.roll(y, 1, 0), y)[8:]


def prep_kernel(e_ref, w_ref, b_ref, s_ref, t_ref):
    scaled = w_ref[...] * s_ref[...]
    wide = jnp.concatenate([scaled, jnp.zeros_like(scaled)], axis=0)
    t = lax.dot_general(wide, e_ref[...], NT, precision=HIGH, preferred_element_type=F32)
    b0 = jnp.sum(b_ref[...] * s_ref[...], axis=1, keepdims=True)
    row = lax.broadcasted_iota(I32, t.shape, 0)
    t_ref[...] = jnp.where(row == TAPS, b0, t)


def weigh(start, len_ref, ids_scr, t_ref):
    shape = (ids_scr.shape[0], 128)
    lane = lanes(shape)
    even, length = geometry(shape, start, len_ref)
    live = [alive(even, length), alive(even + 1, length)]
    ids, terms = [], []
    for e in range(2):
        index = ((lane // 8) % 8) * 16 + 2 * (lane % 8) + e
        found = jnp.where(
            lane < 64, pick(ids_scr[:, :128], index), pick(ids_scr[:, 128:], index)
        )
        taps = []
        for k in range(TAPS):
            value = jnp.zeros(shape, F32)
            for half in range(t_ref.shape[1] // 128):
                row = jnp.broadcast_to(t_ref[k : k + 1, half * 128 : half * 128 + 128], shape)
                here = (found >= half * 128) & (found < half * 128 + 128)
                value = jnp.where(here, pick(row, found & 127), value)
            taps.append(jnp.where(live[e], value, 0.0))
        terms.append(taps)
        ids.append(jnp.where(live[e], found, -1))
    b0 = t_ref[TAPS : TAPS + 1, :128]
    (ae, ao) = terms
    ce = jnp.where(live[0], b0 + behind(ae[0] + ao[1]) + ae[2] + ao[3], 0.0)
    co = jnp.where(live[1], b0 + behind(ao[0]) + ae[1] + ao[2] + ahead(ae[3]), 0.0)
    at = {-2: behind(ce), -1: behind(co), 0: ce, 1: co, 2: ahead(ce), 3: ahead(co)}
    weights = []
    for e in range(2):
        scores = []
        for b, cases in enumerate(members(even, e)):
            total = None
            for rels, where in cases:
                part = sum(at[r] for r in rels)
                total = part if total is None else jnp.where(where, part, total)
            scores.append(total * (1.0 / (b + 1)))
        top = functools.reduce(jnp.maximum, scores)
        parts = [jnp.exp(s - top) for s in scores]
        norm = sum(parts)
        weights.append([p / norm for p in parts])
    return ids, weights, even, length


def spread(values, even):
    out = {r: 0.0 for r in RELS}
    for e in range(2):
        for b, cases in enumerate(members(even, e)):
            share = values[e][b] * (1.0 / (b + 1))
            for rels, where in cases:
                part = share if where is None else jnp.where(where, share, 0.0)
                for r in rels:
                    out[r] = out[r] + part
    return out


def banded(bands_ref, g, w, count):
    shape = (160, 128)
    row = lax.broadcasted_iota(I32, shape, 0)
    lane = lanes(shape)
    rel = jnp.where(row % 8 == (lane % 64) // 8, row // 8 - 2 - 2 * (lane % 8), 99)
    out = jnp.zeros(shape, F32)
    for i, r in enumerate(RELS):
        line = bands_ref[pl.ds((g * len(RELS) + i) * count + w, 1), :]
        out = jnp.where(rel == r, line, out)
    high = out.astype(BF16).astype(F32)
    return jnp.where(lane < 64, high, out - high).astype(BF16)


def store_bands(bands, bands_ref, count):
    lane = lanes(bands[0].shape)
    for i, r in enumerate(RELS):
        turned = pltpu.roll(bands[r], 64, 1)
        for g in range(2):
            both = jnp.where((lane < 64) == (g == 0), bands[r], turned)
            at = (g * len(RELS) + i) * count
            bands_ref[at : at + count, :] = both[8 : 8 + count]


def one_hot_t(line, vocab):
    return jnp.where(
        lax.broadcasted_iota(I32, (vocab, 128), 0) == line, 1.0, 0.0
    ).astype(BF16)


def window_grads(ct_ref, hl, d_ref, d_base, g, w):
    wide = jnp.concatenate([hl, hl], axis=1)
    width = ct_ref.shape[2]
    base = pl.multiple_of(d_base + 128 * w + 48, 16)
    for n in range(0, width, 256):
        ct = ct_ref[pl.ds(g * 8, 8), pl.ds(pl.multiple_of(8 * w, 8), 8), n : n + 256]
        high, low = split(ct.reshape(64, 256))
        grads = dot(wide, jnp.concatenate([high, high, low, low], axis=0))
        d_ref[pl.ds(base, 32), n : n + 256] += grads[:32]
        d_ref[pl.ds(base + 32, 128), n : n + 256] = grads[32:]


def table_kernel(
    start_ref, len_ref, ids_ref, left_ref, right_ref, t_ref, w_ref, ct_ref,
    grad_ref, weights_ref, chunks_ref,
    ids_scr, bands_ref, d_ref, oh_ref, high_ref, low_ref,
):
    count = ids_ref.shape[0]
    chunks = count + 1
    vocab = t_ref.shape[1]
    start = start_ref[0]
    ids_scr[...] = jnp.zeros_like(ids_scr)
    ids_scr[7:8] = left_ref[...]
    ids_scr[8 : 8 + count] = ids_ref[...]
    ids_scr[8 + count : 9 + count] = right_ref[...]
    ids, weights, even, length = weigh(start, len_ref, ids_scr, t_ref)
    for e in range(2):
        for b in range(4):
            weights_ref[e * 4 + b] = weights[e][b]
    bands = spread(weights, even)
    for r in RELS:
        bands[r] = jnp.where(alive(even + r, length), 0.5 * bands[r], 0.0)
    store_bands(bands, bands_ref, count)
    per = chunks_ref.shape[0] // 2
    for g in range(2):
        chunks_ref[g * per : g * per + per, :] = to_chunks(ids[0], ids[1], g)
    rows = d_ref.shape[0] // 2
    for g in range(2):
        d_ref[g * rows : g * rows + 80, :] = jnp.zeros((80, d_ref.shape[1]), F32)
        d_ref[(g + 1) * rows - 64 : (g + 1) * rows, :] = jnp.zeros((64, d_ref.shape[1]), F32)

    def table_part(g, c, size):
        d_at = pl.multiple_of(g * rows + 128 * c + 24, 8)
        to = pl.multiple_of((g * chunks + c) * 128, 128)
        for i in range(0, size, 16):
            near = [d_ref[pl.ds(d_at + i + 8 * k, 16), :] for k in range(TAPS)]
            total = sum(w_ref[3 - k : 4 - k, :] * near[k] for k in range(TAPS))
            high, low = split(total)
            high_ref[pl.ds(to + i, 16), :] = high
            low_ref[pl.ds(to + i, 16), :] = low
        for i in range(size, 128, 16):
            zero = jnp.zeros((16, d_ref.shape[1]), BF16)
            high_ref[pl.ds(to + i, 16), :] = zero
            low_ref[pl.ds(to + i, 16), :] = zero
        oh_ref[:, pl.ds(to, 128)] = one_hot_t(chunks_ref[pl.ds(g * per + c, 1), :], vocab)

    for g in range(2):

        @pl.loop(0, count)
        def _(w):
            hl = banded(bands_ref, g, w, count)
            window_grads(ct_ref, hl, d_ref, g * rows, g, w)
            table_part(g, w, 128)

        table_part(g, count, 64)

    for n in range(0, grad_ref.shape[1], 256):
        grad_ref[:, n : n + 256] = dot(oh_ref[...], high_ref[:, n : n + 256]) + dot(
            oh_ref[...], low_ref[:, n : n + 256]
        )


def mix_kernel(
    start_ref, len_ref, weights_ref, chunks_ref, e_ref, w_ref, b_ref, ct_ref,
    latent_ref, small_ref,
    bands_ref, d_ref, oh_ref, x_ref, high_ref, low_ref, near_ref, q_ref,
):
    padded = weights_ref.shape[1]
    count = ct_ref.shape[1] // 8
    chunks = count + 1
    vocab, width = e_ref.shape
    start = start_ref[0]
    even, length = geometry((padded, 128), start, len_ref)
    weights = [[weights_ref[e * 4 + b] for b in range(4)] for e in range(2)]
    bands = spread(weights, even)
    for r in RELS:
        bands[r] = jnp.where(alive(even + r, length), 0.5 * bands[r], 0.0)
    store_bands(bands, bands_ref, count)
    per = chunks_ref.shape[0] // 2
    e_high, e_low = split(e_ref[...])
    d_ref[0:80, :] = jnp.zeros((80, width), F32)
    small_ref[...] = jnp.zeros_like(small_ref)
    near_ref[...] = jnp.zeros_like(near_ref)
    shape = (160, 128)
    row, lane = lax.broadcasted_iota(I32, shape, 0), lanes(shape)

    for g in range(2):
        d_ref[48:80, :] = jnp.zeros((32, width), F32)

        @pl.loop(0, chunks)
        def _(c):
            oh = one_hot_t(chunks_ref[pl.ds(g * per + c, 1), :], vocab)
            oh_ref[:, pl.ds(pl.multiple_of((g * chunks + c) * 128, 128), 128)] = oh
            to = pl.multiple_of(c * 128, 128)
            for n in range(0, width, 256):
                x_ref[pl.ds(to, 128), n : n + 256] = dot(oh, e_high[:, n : n + 256], TN) + dot(
                    oh, e_low[:, n : n + 256], TN
                )

        @pl.loop(0, count)
        def _(w):
            hl = banded(bands_ref, g, w, count)
            window_grads(ct_ref, hl, d_ref, 0, g, w)

        def conv_part(c, size):
            at = pl.multiple_of(c * 128, 128)
            sums = [jnp.zeros((8, width), F32) for _ in range(TAPS + 1)]
            for i in range(0, size, 16):
                d = d_ref[pl.ds(at + 48 + i, 16), :]
                total = b_ref[...]
                sums[TAPS] = sums[TAPS] + d[:8] + d[8:]
                for k in range(TAPS):
                    x = x_ref[pl.ds(at + i + 8 * k, 16), :]
                    total = total + w_ref[k : k + 1, :] * x
                    p = d * x
                    sums[k] = sums[k] + p[:8] + p[8:]
                high, low = split(total)
                high_ref[pl.ds(at + i, 16), :] = high
                low_ref[pl.ds(at + i, 16), :] = low
            for k in range(TAPS + 1):
                small_ref[k : k + 1, :] += jnp.sum(sums[k], axis=0, keepdims=True)

        @pl.loop(0, count)
        def _(c):
            conv_part(c, 128)

        conv_part(count, 32)

        @pl.loop(0, count)
        def _(w):
            hl = banded(bands_ref, g, w, count)
            band = hl.astype(F32).T.astype(BF16)
            at = pl.multiple_of(w * 128, 128)
            u_at = pl.multiple_of(8 * w, 8)
            for n in range(0, width, 256):
                both = dot(band, high_ref[pl.ds(at, 160), n : n + 256])
                rest = dot(band[:64], low_ref[pl.ds(at, 160), n : n + 256])
                out = both[:64] + both[64:] + rest
                latent_ref[pl.ds(g * 8, 8), pl.ds(u_at, 8), n : n + 256] = out.reshape(8, 8, 256)
            ct = ct_ref[pl.ds(g * 8, 8), pl.ds(u_at, 8), :].reshape(64, width)
            ct = jnp.concatenate(split(ct), axis=0)
            product = dot(high_ref[pl.ds(at, 160), :], ct, NT) + dot(
                low_ref[pl.ds(at, 160), :], ct, NT
            )
            rel = jnp.where(row % 8 == (lane % 64) // 8, row // 8 - 2 - 2 * (lane % 8), 99)
            for i, r in enumerate(RELS):
                line = jnp.sum(jnp.where(rel == r, product, 0.0), axis=0, keepdims=True)
                line = line + pltpu.roll(line, 64, 1)
                keep = (lanes((1, 128)) < 64) == (g == 0)
                near_ref[i, pl.ds(8 + w, 1), :] = jnp.where(
                    keep, line, near_ref[i, pl.ds(8 + w, 1), :]
                )

    near = {}
    for i, r in enumerate(RELS):
        near[r] = jnp.where(alive(even + r, length), 0.5 * near_ref[i], 0.0)
    d_scores = []
    for e in range(2):
        d_weights = []
        for b, cases in enumerate(members(even, e)):
            total = None
            for rels, where in cases:
                part = sum(near[r] for r in rels)
                total = part if total is None else jnp.where(where, part, total)
            d_weights.append(total * (1.0 / (b + 1)))
        mean = sum(weights[e][b] * d_weights[b] for b in range(4))
        d_scores.append([weights[e][b] * (d_weights[b] - mean) for b in range(4)])
    own = lax.broadcasted_iota(I32, (padded, 128), 0) - 8
    own = (own >= 0) & (own < count)
    q = spread(d_scores, even)
    for r in RELS:
        q[r] = jnp.where(own & alive(even + r, length), q[r], 0.0)
    qe = q[0] + behind(q[2]) + ahead(q[-2])
    qo = q[1] + behind(q[3]) + ahead(q[-1])
    q_sum = jnp.sum(jnp.sum(qe + qo, axis=0, keepdims=True), axis=1, keepdims=True)
    shifted = [
        (ahead(qe), ahead(qo)),
        (qo, ahead(qe)),
        (qe, qo),
        (behind(qo), qe),
    ]
    q_ref[...] = jnp.zeros_like(q_ref)
    for g in range(2):
        for k in range(TAPS):
            flat = to_chunks(*shifted[k], g)
            for c in range(chunks):
                at = (g * chunks + c) * 128
                q_ref[k : k + 1, at : at + 128] = flat[c : c + 1]
    q1, rest = q_ref[...].astype(BF16), q_ref[...]
    rest = rest - q1.astype(F32)
    q2 = rest.astype(BF16)
    q3 = (rest - q2.astype(F32)).astype(BF16)
    hist = dot(jnp.concatenate([q1, q2, q3], axis=0), oh_ref[...], NT)
    hist = hist[:8] + hist[8:16] + hist[16:]
    for k in range(TAPS):
        at = k * vocab
        small_ref[5 + at // width : 6 + at // width, at % width : at % width + vocab] = hist[k : k + 1]
    at = TAPS * vocab
    small_ref[5 + at // width : 6 + at // width, at % width : at % width + 128] = (
        jnp.broadcast_to(q_sum, (1, 128))
    )


def final_kernel(sum_ref, small_ref, e_ref, w_ref, b_ref, s_ref, ge_ref, gw_ref, gb_ref, gs_ref):
    vocab, width = e_ref.shape
    hist = []
    for k in range(TAPS):
        at = k * vocab
        hist.append(small_ref[5 + at // width : 6 + at // width, at % width : at % width + vocab])
    at = TAPS * vocab
    q_sum = small_ref[5 + at // width : 6 + at // width, at % width : at % width + 1]
    zero = jnp.zeros((8 - TAPS, vocab), F32)
    hist = jnp.concatenate(hist + [zero], axis=0)
    scaled = w_ref[...] * s_ref[...]
    scaled = jnp.concatenate([scaled, jnp.zeros((8 - TAPS, width), F32)], axis=0)
    ge_ref[...] = sum_ref[...] + lax.dot_general(
        hist, scaled, TN, precision=HIGH, preferred_element_type=F32
    )
    looked = jnp.dot(hist, e_ref[...], precision=HIGH, preferred_element_type=F32)[:TAPS]
    gw_ref[...] = small_ref[0:TAPS, :] + looked * s_ref[...]
    gb_ref[...] = small_ref[TAPS : TAPS + 1, :] + q_sum * s_ref[...]
    gs_ref[...] = q_sum * b_ref[...] + jnp.sum(looked * w_ref[...], axis=0, keepdims=True)


def partners(axis, mask):
    return [(i, i ^ mask) for i in range(lax.axis_size(axis))]


def part(v, index, size):
    return lax.dynamic_slice_in_dim(v, index * size, size, 0)


def scatter_sum(v, axis, low, bits):
    group = 1 << bits
    size = v.shape[0] // group
    me = (lax.axis_index(axis) >> low) & (group - 1)
    total = part(v, me, size)
    for m in range(1, group):
        total = total + lax.ppermute(part(v, me ^ m, size), axis, partners(axis, m << low))
    return total


def exchange_sum(v, axis, low, bits):
    return v + sum(
        lax.ppermute(v, axis, partners(axis, m << low)) for m in range(1, 1 << bits)
    )


def gather_back(v, small, axis, low, bits):
    group = 1 << bits
    size = v.shape[0]
    me = (lax.axis_index(axis) >> low) & (group - 1)
    both = jnp.concatenate([v, small], axis=0)
    out = jnp.zeros((group * size,) + v.shape[1:], v.dtype)
    out = lax.dynamic_update_slice_in_dim(out, v, me * size, 0)
    for m in range(1, group):
        got = lax.ppermute(both, axis, partners(axis, m << low))
        out = lax.dynamic_update_slice_in_dim(out, got[:size], (me ^ m) * size, 0)
        small = small + got[size:]
    return out, small


def per_device(byte_ids, lengths, embedding, conv_weight, conv_bias, score_weight, cotangent):
    rows, span = byte_ids.shape
    vocab, width = embedding.shape
    count = span // 16
    chunks = count + 1
    per = -(-chunks // 8) * 8
    padded = 8 + per
    half = span // 2
    seq = lax.axis_size("seq")
    start = (lax.axis_index("seq") * span).reshape(1)
    bias, scorer = conv_bias.reshape(1, width), score_weight.reshape(1, width)

    ids = byte_ids.reshape(rows, count, 16).transpose(1, 0, 2).reshape(count, rows * 16)
    up = [(i, i + 1) for i in range(seq - 1)]
    left = lax.ppermute(ids[-1:], "seq", up)
    right = lax.ppermute(ids[:1], "seq", [(j, i) for i, j in up])
    vm = pl.BlockSpec(memory_space=pltpu.VMEM)
    sm = pl.BlockSpec(memory_space=pltpu.SMEM)
    table_scores = pl.pallas_call(
        prep_kernel,
        out_shape=jax.ShapeDtypeStruct((8, vocab), F32),
        in_specs=[vm] * 4,
        out_specs=vm,
        name="prep",
    )(embedding, conv_weight, bias, scorer)

    d_rows = (span + 16) * 8
    grad_table, weights, id_chunks = pl.pallas_call(
        table_kernel,
        out_shape=(
            jax.ShapeDtypeStruct((vocab, width), F32),
            jax.ShapeDtypeStruct((8, padded, 128), F32),
            jax.ShapeDtypeStruct((2 * per, 128), I32),
        ),
        in_specs=[sm, sm] + [vm] * 6,
        out_specs=(vm, vm, vm),
        scratch_shapes=[
            pltpu.VMEM((padded, 256), I32),
            pltpu.VMEM((12 * count, 128), F32),
            pltpu.VMEM((2 * d_rows, width), F32),
            pltpu.VMEM((vocab, 2 * chunks * 128), BF16),
            pltpu.VMEM((2 * chunks * 128, width), BF16),
            pltpu.VMEM((2 * chunks * 128, width), BF16),
        ],
        compiler_params=VMEM,
        name="table_grad",
    )(start, lengths, ids, left, right, table_scores, conv_weight, cotangent)

    latent, small = pl.pallas_call(
        mix_kernel,
        out_shape=(
            jax.ShapeDtypeStruct((rows, half, width), F32),
            jax.ShapeDtypeStruct((8, width), F32),
        ),
        in_specs=[sm, sm] + [vm] * 6,
        out_specs=(vm, vm),
        scratch_shapes=[
            pltpu.VMEM((12 * count, 128), F32),
            pltpu.VMEM((d_rows, width), F32),
            pltpu.VMEM((vocab, 2 * chunks * 128), BF16),
            pltpu.VMEM((chunks * 128, width), F32),
            pltpu.VMEM((chunks * 128, width), BF16),
            pltpu.VMEM((chunks * 128, width), BF16),
            pltpu.VMEM((6, padded, 128), F32),
            pltpu.VMEM((8, 2 * chunks * 128), F32),
        ],
        compiler_params=VMEM,
        name="mix",
    )(start, lengths, weights, id_chunks, embedding, conv_weight, bias, cotangent)

    bits = seq.bit_length() - 1
    groups = [("seq", low, min(2, bits - low)) for low in range(0, bits, 2)]
    stages = [("dp", 0, lax.axis_size("dp").bit_length() - 1)] + groups[:-1]
    total = grad_table
    for stage in stages:
        total = scatter_sum(total, *stage)
    size = total.shape[0]
    both = exchange_sum(jnp.concatenate([total, small], axis=0), *groups[-1])
    total, small = both[:size], both[size:]
    for stage in reversed(stages):
        total, small = gather_back(total, small, *stage)

    grad_e, grad_w, grad_b, grad_s = pl.pallas_call(
        final_kernel,
        out_shape=(
            jax.ShapeDtypeStruct((vocab, width), F32),
            jax.ShapeDtypeStruct((TAPS, width), F32),
            jax.ShapeDtypeStruct((1, width), F32),
            jax.ShapeDtypeStruct((1, width), F32),
        ),
        in_specs=[vm] * 6,
        out_specs=(vm,) * 4,
        name="final",
    )(total, small, embedding, conv_weight, bias, scorer)
    return latent, grad_e, grad_w, grad_b.reshape(width), grad_s.reshape(width)


def solution(mesh):
    placed = (P("dp", "seq"), P("dp"), P(), P(), P(), P(), P("dp", "seq", None))
    return jax.shard_map(
        per_device,
        mesh=mesh,
        in_specs=placed,
        out_specs=(P("dp", "seq", None), P(), P(), P(), P()),
        check_vma=False,
    )
```

time: 860 us -> 132 us (0.15); the launches traced: 847 us -> 132 us
  other arithmetic: 363 us -> 5.78 us
  local copies, waits for them, and re-layouts: 224 us -> 7 us
  matrix products: 95.2 us -> 0 us
  Pallas kernels: 0 us -> 81 us
  waiting for transfers between devices: 78.7 us -> 16.3 us
  blocking collectives: 46.1 us -> 0 us
  between operations: 14.8 us -> 0.85 us
    reduce_sum x9 -> x0, other arithmetic: 144 us -> none  [the longest x1 41.2 us: convolve(): bias[None, None, :]]
    reshape x7 -> x5, local copies, waits for them, and re-layouts: 107 us -> 4.1 us  [the longest x2 2.53 us: per_device(): bias, scorer = (conv_bias.reshape(1, width), score_weight.reshape(1, width))]
    dot_general x4 -> x0, matrix products: 95.2 us -> none  [the longest x2 74.6 us: pool_mix(): scores = jnp.dot(stack, scorer, precision=HIGH)]
    pallas_call x0 -> x4, Pallas kernels: none -> 81 us  [the longest x1 53.6 us: per_device(): pl.pallas_call(mix_kernel, out_shape=(jax.ShapeDtypeStruct((rows, half, w...]
    mul x5 -> x0, other arithmetic: 79.8 us -> none  [the longest x1 37.5 us: pool_mix(): coef[None, :, None] * c_wide[:, 2 + shift_by:2 + shift_by + span]]
    psum x1 -> x0, waiting for transfers between devices: 78.7 us -> none  [per_device(): summed = lax.psum((terms[0], terms[1], terms[2], terms[3]), ('dp', 'seq'))]
    add_any x4 -> x0, other arithmetic: 73.5 us -> none  [the longest x1 29.5 us: pool_mix(): core = c_wide[:, 2:-2]]
    another operation x3 -> x0, local copies, waits for them, and re-layouts: 48.2 us -> none  [the longest x1 18.5 us: pool_mix(): stack = jnp.stack([core, pair, triple, quad])]
  transfers between devices with their start and end apart: 9 -> 13, of which waited for: 1 -> 6; matrix products, arithmetic and copies ran while one was open for 22% -> 3% of each run, Pallas kernels for 0% -> 43%
where the time goes in v1:
time: 132 us
  Pallas kernels  81 us (61%)
  starting transfers between devices  20.6 us (16%)
  waiting for transfers between devices  16.3 us (12%)
  local copies, waits for them, and re-layouts  7 us (5%)
  other arithmetic  5.78 us (4%)
    pallas_call x1, Pallas kernels, per_device(): pl.pallas_call(mix_kernel, out_shape=(jax.ShapeDtypeStruct((rows, half, w...  53.6 us
    pallas_call x1, Pallas kernels, per_device(): pl.pallas_call(table_kernel, out_shape=(jax.ShapeDtypeStruct((vocab, widt...  21.6 us
    ppermute x3, waiting for transfers between devices, exchange_sum(): lax.ppermute(v, axis, partners(axis, m << low))  9.17 us
    ppermute x3, starting transfers between devices, exchange_sum(): lax.ppermute(v, axis, partners(axis, m << low))  5.71 us
    ppermute x4, waiting for transfers between devices, gather_back(): got = lax.ppermute(both, axis, partners(axis, m << low))  5.44 us
    ppermute x4, starting transfers between devices, scatter_sum(): lax.ppermute(part(v, me ^ m, size), axis, partners(axis, m << low))  5.17 us
    ppermute x1, starting transfers between devices, per_device(): left = lax.ppermute(ids[-1:], 'seq', up)  4.83 us
    ppermute x4, starting transfers between devices, gather_back(): got = lax.ppermute(both, axis, partners(axis, m << low))  3.62 us
  transfers between devices with their start and end apart: 13, of which 6 were waited for; matrix products, arithmetic and copies ran while one was open for 3% of the time, Pallas kernels for 43%

profile of v1, /device:TPU:0, one launch (start us, length us, event | category | flops | bytes accessed | tf_op | source)
XLA Modules:
  0.0 131.5 jit_solution(16933606701784408121)
XLA Ops:
  0.6 0.8 reshape.34
  1.6 4.8 %collective-permute-start = (s32[1,256]{1,0:T(1,128)S(1)}, s32[1,256]{1,0:T(1,128)S(1)}, u32[]{:S(2)}, u32[]{:S(2)}) collective-permute-start(s32[1,256]{1,0:T(1,128)S(1)} %slice.44), channel_id=1, source_target_pairs={{0,1},{1,2},{2,3},{3,4},{4,5},{5,6},{6,7},{7,8},{8,9},{9,10},{10,1... | collective-permute-start | bytes 3080 | tf_op jit(solution)/shard_map/ppermute | solution.py:459
  6.5 1.3 collective-permute-start.1
  8.5 1.3 reshape.36.b_ref
  9.8 1.3 reshape.37.s_ref
  11.1 2.5 %prep.1.t_ref = f32[8,256]{1,0:T(8,128)} custom-call(f32[256,768]{1,0:T(8,128)} %e_ref.5, f32[4,768]{1,0:T(4,128)} %w_ref.7, f32[1,768]{1,0:T(1,128)} %reshape.36.b_ref, f32[1,768]{1,0:T(1,128)} %reshape.37.s_ref), custom_call_target="tpu_custom_call" | custom-call | tf_op jit(solution)/shard_map/prep/pallas_call | solution.py:463
  14.1 21.6 %table_grad.1 = (f32[256,768]{1,0:T(8,128)}, f32[8,32,128]{2,1,0:T(8,128)}, s32[48,128]{1,0:T(8,128)}) custom-call(s32[1]{0:T(128)} %bitcast.start_ref, s32[16]{0:T(128)} %len_ref.3, s32[16,256]{1,0:T(8,128)} %reshape.35.ids_ref, s32[1,256]{1,0:T(1,128)} %copy-done.1, s32[1,256]{1,0:T(1,128)} %copy-done.2, f32[8,256]{1,0:T(8,128)} %prep.1.t_ref, ...), custom_call_target="tpu_custom_call" | custom-call | tf_op jit(solution)/shard_map/table_grad/pallas_call | solution.py:472
  35.8 1.0 constant_dynamic-slice_fusion.3
  36.9 1.7 %collective-permute-done.2 = f32[128,768]{1,0:T(8,128)S(1)} collective-permute-done((f32[128,768]{1,0:T(8,128)S(1)}, f32[128,768]{1,0:T(8,128)S(1)}, u32[]{:S(2)}, u32[]{:S(2)}) %collective-permute-start.2) | collective-permute-done | bytes 393248 | tf_op jit(solution)/shard_map/ppermute | solution.py:421
  38.6 1.0 dynamic-slice_add_fusion
  39.7 2.7 %collective-permute-start.3 = (f32[32,768]{1,0:T(8,128)S(1)}, f32[32,768]{1,0:T(8,128)S(1)}, u32[]{:S(2)}, u32[]{:S(2)}) collective-permute-start(f32[32,768]{1,0:T(8,128)S(1)} %get-tuple-element.23), channel_id=1, source_target_pairs={{0,1},{1,0},{2,3},{3,2},{4,5},{5,4},{6,7},{7,6},{8,9},{9,8},{10,11... | collective-permute-start | bytes 294920 | tf_op jit(solution)/shard_map/ppermute | solution.py:421
  42.4 2.4 %collective-permute-start.5 = (f32[32,768]{1,0:T(8,128)S(1)}, f32[32,768]{1,0:T(8,128)S(1)}, u32[]{:S(2)}, u32[]{:S(2)}) collective-permute-start(f32[32,768]{1,0:T(8,128)S(1)} %get-tuple-element.24), channel_id=1, source_target_pairs={{0,3},{1,2},{2,1},{3,0},{4,7},{5,6},{6,5},{7,4},{8,11},{9,10},{10,... | collective-permute-start | bytes 294920 | tf_op jit(solution)/shard_map/ppermute | solution.py:421
  44.8 53.6 %mix.1 = (f32[16,128,768]{2,1,0:T(8,128)}, f32[8,768]{1,0:T(8,128)}) custom-call(s32[1]{0:T(128)} %bitcast.start_ref, s32[16]{0:T(128)} %len_ref.3, f32[8,32,128]{2,1,0:T(8,128)} %get-tuple-element.14.weights_ref, s32[48,128]{1,0:T(8,128)} %get-tuple-element.15.chunks_ref, f32[256,768]{1,0:T(8,128)} %e_ref.5, f32[4,768]{1,0:T(4,128)} %w_ref.7, ...), custom_call_target="tpu_custom_call" | custom-call | tf_op jit(solution)/shard_map/mix/pallas_call | solution.py:493
  99.2 5.1 %collective-permute-start.8 = (f32[40,768]{1,0:T(8,128)S(1)}, f32[40,768]{1,0:T(8,128)S(1)}, u32[]{:S(2)}, u32[]{:S(2)}) collective-permute-start(f32[40,768]{1,0:T(8,128)S(1)} %pad_maximum_fusion.1), channel_id=1, source_target_pairs={{0,12},{1,13},{2,14},{3,15},{4,8},{5,9},{6,10},{7,11},{8,4},{9,5},... | collective-permute-start | bytes 368648 | tf_op jit(solution)/shard_map/ppermute | solution.py:427
  104.9 3.6 %collective-permute-done.8 = f32[40,768]{1,0:T(8,128)S(1)} collective-permute-done((f32[40,768]{1,0:T(8,128)S(1)}, f32[40,768]{1,0:T(8,128)S(1)}, u32[]{:S(2)}, u32[]{:S(2)}) %collective-permute-start.8) | collective-permute-done | bytes 122912 | tf_op jit(solution)/shard_map/ppermute | solution.py:427
  108.6 5.5 %collective-permute-done.7 = f32[40,768]{1,0:T(8,128)S(1)} collective-permute-done((f32[40,768]{1,0:T(8,128)S(1)}, f32[40,768]{1,0:T(8,128)S(1)}, u32[]{:S(2)}, u32[]{:S(2)}) %collective-permute-start.7) | collective-permute-done | bytes 122912 | tf_op jit(solution)/shard_map/ppermute | solution.py:427
  115.6 1.1 collective-permute-start.10
  116.7 1.7 %collective-permute-start.9 = (f32[40,768]{1,0:T(8,128)S(1)}, f32[40,768]{1,0:T(8,128)S(1)}, u32[]{:S(2)}, u32[]{:S(2)}) collective-permute-start(f32[40,768]{1,0:T(8,128)S(1)} %add_add_fusion), channel_id=1, source_target_pairs={{0,1},{1,0},{2,3},{3,2},{4,5},{5,4},{6,7},{7,6},{8,9},{9,8},{10,11... | collective-permute-start | bytes 368648 | tf_op jit(solution)/shard_map/ppermute | solution.py:439
  118.5 3.5 %collective-permute-done.9 = f32[40,768]{1,0:T(8,128)S(1)} collective-permute-done((f32[40,768]{1,0:T(8,128)S(1)}, f32[40,768]{1,0:T(8,128)S(1)}, u32[]{:S(2)}, u32[]{:S(2)}) %collective-permute-start.9) | collective-permute-done | bytes 122912 | tf_op jit(solution)/shard_map/ppermute | solution.py:439
  122.6 1.6 %collective-permute-done.12 = f32[136,768]{1,0:T(8,128)S(1)} collective-permute-done((f32[136,768]{1,0:T(8,128)S(1)}, f32[136,768]{1,0:T(8,128)S(1)}, u32[]{:S(2)}, u32[]{:S(2)}) %collective-permute-start.12) | collective-permute-done | bytes 417824 | tf_op jit(solution)/shard_map/ppermute | solution.py:439
  124.9 0.9 copy-done
  125.8 3.2 %final.1 = (f32[256,768]{1,0:T(8,128)}, f32[4,768]{1,0:T(4,128)}, f32[1,768]{1,0:T(1,128)}, f32[1,768]{1,0:T(1,128)}) custom-call(f32[256,768]{1,0:T(8,128)} %copy-done, f32[8,768]{1,0:T(8,128)} %slice_add_fusion.small_ref, f32[256,768]{1,0:T(8,128)} %e_ref.5, f32[4,768]{1,0:T(4,128)} %w_ref.7, f32[1,768]{1,0:T(1,128)} %reshape.36.b_ref, f32[1,768]{1,0:T(1,128)} %reshape.37.s_ref), custom_call_target="tpu_custom_call" | custom-call | tf_op jit(solution)/shard_map/final/pallas_call | solution.py:527
  129.0 1.3 reduce
  130.3 1.3 reduce.1
  (39 shorter events, 5.8 us)
Async XLA Ops:
  1.6 12.0 %collective-permute-start = (s32[1,256]{1,0:T(1,128)S(1)}, s32[1,256]{1,0:T(1,128)S(1)}, u32[]{:S(2)}, u32[]{:S(2)}) collective-permute-start(s32[1,256]{1,0:T(1,128)S(1)} %slice.44), channel_id=1, source_target_pairs={{0,1},{1,2},{2,3},{3,4},{4,5},{5,6},{6,7},{7,8},{8,9},{9,10},{10,1... | collective-permute-start | bytes 3080 | tf_op jit(solution)/shard_map/ppermute | solution.py:459
  6.5 7.0 %collective-permute-start.1 = (s32[1,256]{1,0:T(1,128)S(1)}, s32[1,256]{1,0:T(1,128)S(1)}, u32[]{:S(2)}, u32[]{:S(2)}) collective-permute-start(s32[1,256]{1,0:T(1,128)S(1)} %slice.46), channel_id=1, source_target_pairs={{1,0},{2,1},{3,2},{4,3},{5,4},{6,5},{7,6},{8,7},{9,8},{10,9},{11,1... | collective-permute-start | bytes 3080 | tf_op jit(solution)/shard_map/ppermute | solution.py:460
  13.5 0.6 copy-start.1
  13.6 0.6 copy-start.2
  36.8 1.8 %collective-permute-start.2 = (f32[128,768]{1,0:T(8,128)S(1)}, f32[128,768]{1,0:T(8,128)S(1)}, u32[]{:S(2)}, u32[]{:S(2)}) collective-permute-start(f32[128,768]{1,0:T(8,128)S(1)} %constant_dynamic-slice_fusion.3), channel_id=1, source_target_pairs={{0,16},{16,0},{1,17},{17,1},{2,18},{18,2},{3,19},{19,3},{4,20},{20... | collective-permute-start | bytes 1179656 | tf_op jit(solution)/shard_map/ppermute | solution.py:421
  39.7 58.7 %collective-permute-start.3 = (f32[32,768]{1,0:T(8,128)S(1)}, f32[32,768]{1,0:T(8,128)S(1)}, u32[]{:S(2)}, u32[]{:S(2)}) collective-permute-start(f32[32,768]{1,0:T(8,128)S(1)} %get-tuple-element.23), channel_id=1, source_target_pairs={{0,1},{1,0},{2,3},{3,2},{4,5},{5,4},{6,7},{7,6},{8,9},{9,8},{10,11... | collective-permute-start | bytes 294920 | tf_op jit(solution)/shard_map/ppermute | solution.py:421
  42.4 56.0 %collective-permute-start.5 = (f32[32,768]{1,0:T(8,128)S(1)}, f32[32,768]{1,0:T(8,128)S(1)}, u32[]{:S(2)}, u32[]{:S(2)}) collective-permute-start(f32[32,768]{1,0:T(8,128)S(1)} %get-tuple-element.24), channel_id=1, source_target_pairs={{0,3},{1,2},{2,1},{3,0},{4,7},{5,6},{6,5},{7,4},{8,11},{9,10},{10,... | collective-permute-start | bytes 294920 | tf_op jit(solution)/shard_map/ppermute | solution.py:421
  44.8 53.7 %collective-permute-start.4 = (f32[32,768]{1,0:T(8,128)S(1)}, f32[32,768]{1,0:T(8,128)S(1)}, u32[]{:S(2)}, u32[]{:S(2)}) collective-permute-start(f32[32,768]{1,0:T(8,128)S(1)} %get-tuple-element.25), channel_id=1, source_target_pairs={{0,2},{1,3},{2,0},{3,1},{4,6},{5,7},{6,4},{7,5},{8,10},{9,11},{10,... | collective-permute-start | bytes 294920 | tf_op jit(solution)/shard_map/ppermute | solution.py:421
  99.2 9.4 %collective-permute-start.8 = (f32[40,768]{1,0:T(8,128)S(1)}, f32[40,768]{1,0:T(8,128)S(1)}, u32[]{:S(2)}, u32[]{:S(2)}) collective-permute-start(f32[40,768]{1,0:T(8,128)S(1)} %pad_maximum_fusion.1), channel_id=1, source_target_pairs={{0,12},{1,13},{2,14},{3,15},{4,8},{5,9},{6,10},{7,11},{8,4},{9,5},... | collective-permute-start | bytes 368648 | tf_op jit(solution)/shard_map/ppermute | solution.py:427
  104.3 9.8 %collective-permute-start.7 = (f32[40,768]{1,0:T(8,128)S(1)}, f32[40,768]{1,0:T(8,128)S(1)}, u32[]{:S(2)}, u32[]{:S(2)}) collective-permute-start(f32[40,768]{1,0:T(8,128)S(1)} %pad_maximum_fusion.1), channel_id=1, source_target_pairs={{0,8},{1,9},{2,10},{3,11},{4,12},{5,13},{6,14},{7,15},{8,0},{9,1},... | collective-permute-start | bytes 368648 | tf_op jit(solution)/shard_map/ppermute | solution.py:427
  104.3 9.8 %collective-permute-start.6 = (f32[40,768]{1,0:T(8,128)S(1)}, f32[40,768]{1,0:T(8,128)S(1)}, u32[]{:S(2)}, u32[]{:S(2)}) collective-permute-start(f32[40,768]{1,0:T(8,128)S(1)} %pad_maximum_fusion.1), channel_id=1, source_target_pairs={{0,4},{1,5},{2,6},{3,7},{4,0},{5,1},{6,2},{7,3},{8,12},{9,13},{10,... | collective-permute-start | bytes 368648 | tf_op jit(solution)/shard_map/ppermute | solution.py:427
  114.9 7.1 %collective-permute-start.11 = (f32[40,768]{1,0:T(8,128)S(1)}, f32[40,768]{1,0:T(8,128)S(1)}, u32[]{:S(2)}, u32[]{:S(2)}) collective-permute-start(f32[40,768]{1,0:T(8,128)S(1)} %add_add_fusion), channel_id=1, source_target_pairs={{0,3},{1,2},{2,1},{3,0},{4,7},{5,6},{6,5},{7,4},{8,11},{9,10},{10,... | collective-permute-start | bytes 368648 | tf_op jit(solution)/shard_map/ppermute | solution.py:439
  115.6 6.7 %collective-permute-start.10 = (f32[40,768]{1,0:T(8,128)S(1)}, f32[40,768]{1,0:T(8,128)S(1)}, u32[]{:S(2)}, u32[]{:S(2)}) collective-permute-start(f32[40,768]{1,0:T(8,128)S(1)} %add_add_fusion), channel_id=1, source_target_pairs={{0,2},{1,3},{2,0},{3,1},{4,6},{5,7},{6,4},{7,5},{8,10},{9,11},{10,... | collective-permute-start | bytes 368648 | tf_op jit(solution)/shard_map/ppermute | solution.py:439
  116.7 5.2 %collective-permute-start.9 = (f32[40,768]{1,0:T(8,128)S(1)}, f32[40,768]{1,0:T(8,128)S(1)}, u32[]{:S(2)}, u32[]{:S(2)}) collective-permute-start(f32[40,768]{1,0:T(8,128)S(1)} %add_add_fusion), channel_id=1, source_target_pairs={{0,1},{1,0},{2,3},{3,2},{4,5},{5,4},{6,7},{7,6},{8,9},{9,8},{10,11... | collective-permute-start | bytes 368648 | tf_op jit(solution)/shard_map/ppermute | solution.py:439
  122.4 1.8 %collective-permute-start.12 = (f32[136,768]{1,0:T(8,128)S(1)}, f32[136,768]{1,0:T(8,128)S(1)}, u32[]{:S(2)}, u32[]{:S(2)}) collective-permute-start(f32[136,768]{1,0:T(8,128)S(1)} %pad_maximum_fusion), channel_id=1, source_target_pairs={{0,16},{16,0},{1,17},{17,1},{2,18},{18,2},{3,19},{19,3},{4,20},{20... | collective-permute-start | bytes 1253384 | tf_op jit(solution)/shard_map/ppermute | solution.py:439
  124.8 0.9 copy-start

commit v2 on v1

v2 whole, which is shorter than its diff:
```python
import functools

import jax
import jax.numpy as jnp
from jax import lax
from jax.experimental import pallas as pl
from jax.experimental.pallas import tpu as pltpu
from jax.sharding import PartitionSpec as P

F32, BF16, I32 = jnp.float32, jnp.bfloat16, jnp.int32
HIGH = lax.Precision.HIGHEST
ROWS = 16
TAPS = 4
TABLE_BATCH, MIX_BATCH, LATENT_BATCH = 4, 2, 4
RING = 10
RELS = (-2, -1, 0, 1, 2, 3)
NT = (((1,), (1,)), ((), ()))
TN = (((0,), (0,)), ((), ()))


def lanes(shape):
    return lax.broadcasted_iota(I32, shape, 1)


def line(ref):
    return ref[...].reshape(1, ref.shape[0])


def pick(x, index):
    return jnp.take_along_axis(x, index, axis=1, mode="promise_in_bounds")


def split(x):
    high = x.astype(BF16)
    return high, (x - high.astype(F32)).astype(BF16)


def dot(a, b, dims=(((1,), (0,)), ((), ()))):
    return lax.dot_general(a, b, dims, preferred_element_type=F32)


def ahead(x):
    lane = lanes(x.shape) % 8
    below = pltpu.roll(x, x.shape[0] - 1, 0)
    return jnp.where(lane == 7, pltpu.roll(below, 7, 1), pltpu.roll(x, 127, 1))


def behind(x):
    lane = lanes(x.shape) % 8
    above = pltpu.roll(x, 1, 0)
    return jnp.where(lane == 0, pltpu.roll(above, 121, 1), pltpu.roll(x, 1, 1))


def geometry(shape, start, len_ref):
    lane = lanes(shape)
    window = lax.broadcasted_iota(I32, shape, 0) - 8
    even = start + 16 * window + 2 * (lane % 8)
    length = jnp.zeros(shape, I32)
    for r in range(ROWS):
        length = jnp.where(lane // 8 == r, len_ref[r], length)
    return even, length


def alive(pos, length):
    return (pos >= 0) & (pos < length)


def members(even, parity):
    offset = (even + parity) % 3
    left = (even // 2) % 2 == 0
    out = [[((parity,), None)], [((0, 1), None)], [], []]
    for o in range(3):
        out[2].append((tuple(parity - o + i for i in range(3)), offset == o))
    out[3] = [((0, 1, 2, 3), left), ((-2, -1, 0, 1), ~left)]
    return out


def to_chunks(xe, xo, g):
    lane = lanes(xe.shape)
    place = (lane // 8 + 12) % 16
    index = g * 64 + (lane % 8) * 8 + place // 2
    y = jnp.where(place % 2 == 0, pick(xe, index), pick(xo, index))
    return jnp.where(lane < 32, pltpu.roll(y, 1, 0), y)[8:]


def prep_kernel(e_ref, w_ref, b_ref, s_ref, ct_hbm, t_ref, high_ref, low_ref, ct_ref, sem):
    copy = pltpu.make_async_copy(ct_hbm, ct_ref, sem)
    copy.start()
    scaled = w_ref[...] * line(s_ref)
    wide = jnp.concatenate([scaled, jnp.zeros_like(scaled)], axis=0)
    t = lax.dot_general(wide, e_ref[...], NT, precision=HIGH, preferred_element_type=F32)
    b0 = jnp.sum(line(b_ref) * line(s_ref), axis=1, keepdims=True)
    row = lax.broadcasted_iota(I32, t.shape, 0)
    t_ref[...] = jnp.where(row == TAPS, b0, t)
    high_ref[...], low_ref[...] = split(e_ref[...])
    copy.wait()


def regroup(ids_ref, ids_scr, first, windows):
    for a in range(0, len(windows), 8):
        some = windows[a : a + 8]
        shape = (8, 128)
        lane = lanes(shape)
        window = lax.broadcasted_iota(I32, shape, 0) + some[0]
        column = 16 * some[0] // 128 * 128
        width = min(128, ids_ref.shape[1] - column)
        index = jnp.clip(16 * window + lane % 16 - column, 0, width - 1)
        for g in range(2):
            out = jnp.zeros(shape, I32)
            for r in range(8):
                row = ids_ref[g * 8 + r : g * 8 + r + 1, column : column + width]
                if width < 128:
                    row = jnp.concatenate([row, jnp.zeros((1, 128 - width), I32)], axis=1)
                found = pick(jnp.broadcast_to(row, shape), index)
                out = jnp.where(lane // 16 == r, found, out)
            at = first + a
            ids_scr[at : at + len(some), g * 128 : g * 128 + 128] = out[: len(some)]


def weigh(start, len_ref, ids_scr, t_ref):
    shape = (ids_scr.shape[0], 128)
    lane = lanes(shape)
    even, length = geometry(shape, start, len_ref)
    live = [alive(even, length), alive(even + 1, length)]
    ids, terms = [], []
    for e in range(2):
        index = ((lane // 8) % 8) * 16 + 2 * (lane % 8) + e
        found = jnp.where(
            lane < 64, pick(ids_scr[:, :128], index), pick(ids_scr[:, 128:], index)
        )
        taps = []
        for k in range(TAPS):
            value = jnp.zeros(shape, F32)
            for half in range(t_ref.shape[1] // 128):
                row = jnp.broadcast_to(t_ref[k : k + 1, half * 128 : half * 128 + 128], shape)
                here = (found >= half * 128) & (found < half * 128 + 128)
                value = jnp.where(here, pick(row, found & 127), value)
            taps.append(jnp.where(live[e], value, 0.0))
        terms.append(taps)
        ids.append(jnp.where(live[e], found, -1))
    b0 = t_ref[TAPS : TAPS + 1, :128]
    (ae, ao) = terms
    ce = jnp.where(live[0], b0 + behind(ae[0] + ao[1]) + ae[2] + ao[3], 0.0)
    co = jnp.where(live[1], b0 + behind(ao[0]) + ae[1] + ao[2] + ahead(ae[3]), 0.0)
    at = {-2: behind(ce), -1: behind(co), 0: ce, 1: co, 2: ahead(ce), 3: ahead(co)}
    weights = []
    for e in range(2):
        scores = []
        for b, cases in enumerate(members(even, e)):
            total = None
            for rels, where in cases:
                part = sum(at[r] for r in rels)
                total = part if total is None else jnp.where(where, part, total)
            scores.append(total * (1.0 / (b + 1)))
        top = functools.reduce(jnp.maximum, scores)
        parts = [jnp.exp(s - top) for s in scores]
        norm = sum(parts)
        weights.append([p / norm for p in parts])
    return ids, weights, even, length


def spread(values, even):
    out = {r: 0.0 for r in RELS}
    for e in range(2):
        for b, cases in enumerate(members(even, e)):
            share = values[e][b] * (1.0 / (b + 1))
            for rels, where in cases:
                part = share if where is None else jnp.where(where, share, 0.0)
                for r in rels:
                    out[r] = out[r] + part
    return out


def diagonals():
    shape = (8, 128)
    row, lane = lax.broadcasted_iota(I32, shape, 0), lanes(shape)
    same = row == (lane % 64) // 8
    return [same & (lane % 8 == u) for u in range(8)]


def banded(bands_ref, g, w, count, diagonal):
    lane = lanes((8, 128))
    tiles = [jnp.zeros((8, 128), F32) for _ in range(20)]
    for i, r in enumerate(RELS):
        line = bands_ref[pl.ds((g * len(RELS) + i) * count + w, 1), :]
        high = line.astype(BF16).astype(F32)
        line = jnp.where(lanes((1, 128)) < 64, high, line - high)
        line = jnp.broadcast_to(line, (8, 128))
        for u in range(8):
            at = 2 * u + 2 + r
            tiles[at] = jnp.where(diagonal[u], line, tiles[at])
    return jnp.concatenate(tiles, axis=0).astype(BF16)


def store_bands(bands, bands_ref, count):
    lane = lanes(bands[0].shape)
    for i, r in enumerate(RELS):
        turned = pltpu.roll(bands[r], 64, 1)
        for g in range(2):
            both = jnp.where((lane < 64) == (g == 0), bands[r], turned)
            at = (g * len(RELS) + i) * count
            bands_ref[at : at + count, :] = both[8 : 8 + count]


def one_hot_t(ids, vocab):
    return jnp.where(
        lax.broadcasted_iota(I32, (vocab, 128), 0) == ids, 1.0, 0.0
    ).astype(BF16)


def weave(*parts):
    order = [((i + 0.5) / len(p), k, step) for k, p in enumerate(parts) for i, step in enumerate(p)]
    for _, _, step in sorted(order, key=lambda item: item[:2]):
        step()


def run_stages(stages, lags):
    for slot in range(len(stages[0]) + max(lags)):
        now = [(items, slot - lag) for items, lag in zip(stages, lags)]
        weave(*[items[t] for items, t in now if 0 <= t < len(items)])


def batches(count, size):
    return [(g, list(range(b, b + size))) for g in range(2) for b in range(0, count, size)]


def window_grads(ct_ref, hl, d_ref, w, n):
    wide = jnp.concatenate([hl, hl], axis=1)
    at = 128 * w + 48
    high, low = split(ct_ref[:, 8 * w : 8 * w + 8, n : n + 256].reshape(64, 256))
    grads = dot(wide, jnp.concatenate([high, high, low, low], axis=0))
    d_ref[at : at + 32, n : n + 256] += grads[:32]
    d_ref[at + 32 : at + 160, n : n + 256] = grads[32:]


def table_kernel(
    start_ref, len_ref, ids_ref, left_ref, right_ref, t_ref, w_ref, ct_ref,
    grad_ref, weights_ref, chunks_ref, hl0, hl1,
    ids_scr, bands_ref, *scratch,
):
    d_refs, oh_refs, high_refs, low_refs = (scratch[2 * i : 2 * i + 2] for i in range(4))
    hl_refs = (hl0, hl1)
    count = ids_ref.shape[1] // 16
    chunks = count + 1
    vocab = t_ref.shape[1]
    start = start_ref[0]
    ids_scr[...] = jnp.zeros_like(ids_scr)
    regroup(left_ref, ids_scr, 7, [count - 1])
    regroup(ids_ref, ids_scr, 8, list(range(count)))
    regroup(right_ref, ids_scr, 8 + count, [0])
    ids, weights, even, length = weigh(start, len_ref, ids_scr, t_ref)
    for e in range(2):
        for b in range(4):
            weights_ref[e * 4 + b] = weights[e][b]
    bands = spread(weights, even)
    for r in RELS:
        bands[r] = jnp.where(alive(even + r, length), 0.5 * bands[r], 0.0)
    store_bands(bands, bands_ref, count)
    per = chunks_ref.shape[0] // 2
    for g in range(2):
        chunks_ref[g * per : g * per + per, :] = to_chunks(ids[0], ids[1], g)
    width = w_ref.shape[1]
    for d_ref in d_refs:
        d_ref[:80, :] = jnp.zeros((80, width), F32)
        d_ref[-64:, :] = jnp.zeros((64, width), F32)

    diagonal = diagonals()

    def grad_steps(g, w):
        made = []

        def step(n):
            if not made:
                made.append(banded(bands_ref, g, w, count, diagonal))
                hl_refs[g][w * 160 : w * 160 + 160, :] = made[0]
            window_grads(ct_ref.at[g * 8 : g * 8 + 8], made[0], d_refs[g], w, n)

        return [functools.partial(step, n) for n in range(0, width, 256)]

    def part_steps(g, c):
        d_ref, oh_ref, high_ref, low_ref = (x[g] for x in (d_refs, oh_refs, high_refs, low_refs))
        to = c * 128
        size = 128 if c < count else 64

        def mark():
            ids = chunks_ref[g * per + c : g * per + c + 1, :]
            oh_ref[:, to : to + 128] = one_hot_t(ids, vocab)
            if size < 128:
                zero = jnp.zeros((128 - size, width), BF16)
                high_ref[to + size : to + 128, :] = zero
                low_ref[to + size : to + 128, :] = zero

        def step(n):
            cols = slice(n, n + 128)
            taps = [jnp.broadcast_to(w_ref[k : k + 1, cols], (64, 128)) for k in range(TAPS)]
            for i in range(0, size, 64):
                near = d_ref[to + 24 + i : to + 112 + i, cols]
                total = sum(taps[3 - k] * near[8 * k : 8 * k + 64] for k in range(TAPS))
                high, low = split(total)
                high_ref[to + i : to + i + 64, cols] = high
                low_ref[to + i : to + i + 64, cols] = low

        return [mark] + [functools.partial(step, n) for n in range(0, width, 128)]

    def sum_steps(g, cs):
        at = slice(cs[0] * 128, cs[-1] * 128 + 128)

        def step(n):
            cols = slice(n, n + 256)
            oh = oh_refs[g][:, at]
            total = dot(oh, high_refs[g][at, cols]) + dot(oh, low_refs[g][at, cols])
            if g == 0 and cs[0] == 0:
                grad_ref[:, cols] = total
            else:
                grad_ref[:, cols] += total

        return [functools.partial(step, n) for n in range(0, width, 256)]

    stages = [[], [], []]
    for g, ws in batches(count, min(TABLE_BATCH, count)):
        cs = ws + [count] * (ws[-1] == count - 1)
        stages[0].append(sum((grad_steps(g, w) for w in ws), []))
        stages[1].append(sum((part_steps(g, c) for c in cs), []))
        stages[2].append(sum_steps(g, cs))
    run_stages(stages, (0, 1, 2))


def near_kernel(
    start_ref, len_ref, weights_ref, chunks_ref, e_high, e_low, w_ref, b_ref, s_ref, hl0, hl1, ct_hbm,
    small_ref, high0, low0, high1, low1,
    near_ref, q_ref, sums_ref, oh0, oh1, d0, d1, x_ref, ct_ref, sem,
):
    copy = pltpu.make_async_copy(ct_hbm, ct_ref, sem)
    copy.start()
    oh_refs, d_refs, hl_refs = (oh0, oh1), (d0, d1), (hl0, hl1)
    high_refs, low_refs = (high0, high1), (low0, low1)
    padded = weights_ref.shape[1]
    count = ct_ref.shape[1] // 8
    chunks = count + 1
    vocab, width = e_high.shape
    start = start_ref[0]
    per = chunks_ref.shape[0] // 2
    small_ref[...] = jnp.zeros_like(small_ref)
    near_ref[...] = jnp.zeros_like(near_ref)
    sums_ref[...] = jnp.zeros_like(sums_ref)
    diagonal = diagonals()
    for d_ref in d_refs:
        d_ref[48:80, :] = jnp.zeros((32, width), F32)
    bias = line(b_ref)
    turned = chunks_ref[...].astype(F32).T

    def slot(g, c):
        return (g * chunks + c) % RING * 128

    def bytes_at(g, c, first, size, cols):
        here = min(128 - first, size)
        at = slot(g, c) + first
        x = x_ref[at : at + here, cols]
        if here == size:
            return x
        at = slot(g, c + 1)
        return jnp.concatenate([x, x_ref[at : at + size - here, cols]], axis=0)

    def look_up_steps(g, cs):
        at = slice(cs[0] * 128, cs[-1] * 128 + 128)

        def mark(c):
            column = jnp.broadcast_to(turned[:, g * per + c : g * per + c + 1], (128, vocab))
            found = jnp.where(column == lanes((128, vocab)).astype(F32), 1.0, 0.0)
            oh_refs[g][c * 128 : c * 128 + 128, :] = found.astype(BF16)

        def step(n):
            cols = slice(n, n + 256)
            oh = oh_refs[g][at, :]
            x = dot(oh, e_high[:, cols]) + dot(oh, e_low[:, cols])
            for i, c in enumerate(cs):
                to = slot(g, c)
                x_ref[to : to + 128, cols] = x[i * 128 : i * 128 + 128]

        return [functools.partial(mark, c) for c in cs] + [
            functools.partial(step, n) for n in range(0, width, 256)
        ]

    def grad_steps(g, w):
        def step(n):
            hl = hl_refs[g][w * 160 : w * 160 + 160, :]
            window_grads(ct_ref.at[g * 8 : g * 8 + 8], hl, d_refs[g], w, n)

        return [functools.partial(step, n) for n in range(0, width, 256)]

    def conv_steps(g, c):
        at = c * 128
        size = 128 if c < count else 32
        step_size = min(size, 64)

        def step(n):
            cols = slice(n, n + 128)
            taps = [jnp.broadcast_to(w_ref[k : k + 1, cols], (step_size, 128)) for k in range(TAPS)]
            first = jnp.broadcast_to(bias[:, cols], (step_size, 128))
            sums = [sums_ref[8 * k : 8 * k + 8, cols] for k in range(TAPS + 1)]
            for i in range(at, at + size, step_size):
                d = d_refs[g][i + 48 : i + 48 + step_size, cols]
                x = bytes_at(g, c, i - at, step_size + 24, cols)
                total = first
                products = [d]
                for k in range(TAPS):
                    near = x[8 * k : 8 * k + step_size]
                    total = total + taps[k] * near
                    products.append(d * near)
                for k, p in enumerate(products):
                    sums[k] = sums[k] + p.reshape(step_size // 8, 8, 128).sum(0)
                high, low = split(total)
                high_refs[g][i : i + step_size, cols] = high
                low_refs[g][i : i + step_size, cols] = low
            for k in range(TAPS + 1):
                sums_ref[8 * k : 8 * k + 8, cols] = sums[k]

        return [functools.partial(step, n) for n in range(0, width, 128)]

    def meet_steps(g, w):
        at = slice(w * 128, w * 128 + 160)

        def meet():
            ct = ct_ref[g * 8 : g * 8 + 8, 8 * w : 8 * w + 8, :].reshape(64, width)
            ct = jnp.concatenate(split(ct), axis=0)
            product = dot(high_refs[g][at, :], ct, NT) + dot(low_refs[g][at, :], ct, NT)
            for i, r in enumerate(RELS):
                total = jnp.zeros((8, 128), F32)
                for u in range(8):
                    row = 8 * (2 * u + 2 + r)
                    total = total + jnp.where(diagonal[u], product[row : row + 8], 0.0)
                found = jnp.sum(total, axis=0, keepdims=True)
                found = found + pltpu.roll(found, 64, 1)
                near_ref[i, 8 + w : 9 + w, g * 64 : g * 64 + 64] = found[:, g * 64 : g * 64 + 64]

        return [meet]

    stages = [[], [], [], []]
    for g, ws in batches(count, MIX_BATCH):
        cs = ws + [count] * (ws[-1] == count - 1)
        stages[0].append(look_up_steps(g, cs))
        stages[1].append(sum((grad_steps(g, w) for w in ws), []))
        stages[2].append(sum((conv_steps(g, c) for c in cs), []))
        stages[3].append(sum((meet_steps(g, w) for w in ws), []))
    stages[1][0].insert(0, copy.wait)
    run_stages(stages, (0, 1, 2, 4))

    for k in range(TAPS + 1):
        total = jnp.sum(sums_ref[8 * k : 8 * k + 8, :], axis=0, keepdims=True)
        to = (k + TAPS) % (TAPS + 1)
        small_ref[to : to + 1, :] = total
    even, length = geometry((padded, 128), start, len_ref)
    weights = [[weights_ref[e * 4 + b] for b in range(4)] for e in range(2)]
    near = {}
    for i, r in enumerate(RELS):
        near[r] = jnp.where(alive(even + r, length), 0.5 * near_ref[i], 0.0)
    d_scores = []
    for e in range(2):
        d_weights = []
        for b, cases in enumerate(members(even, e)):
            total = None
            for rels, where in cases:
                part = sum(near[r] for r in rels)
                total = part if total is None else jnp.where(where, part, total)
            d_weights.append(total * (1.0 / (b + 1)))
        mean = sum(weights[e][b] * d_weights[b] for b in range(4))
        d_scores.append([weights[e][b] * (d_weights[b] - mean) for b in range(4)])
    own = lax.broadcasted_iota(I32, (padded, 128), 0) - 8
    own = (own >= 0) & (own < count)
    q = spread(d_scores, even)
    for r in RELS:
        q[r] = jnp.where(own & alive(even + r, length), q[r], 0.0)
    qe = q[0] + behind(q[2]) + ahead(q[-2])
    qo = q[1] + behind(q[3]) + ahead(q[-1])
    q_sum = jnp.sum(jnp.sum(qe + qo, axis=0, keepdims=True), axis=1, keepdims=True)
    shifted = [
        (ahead(qe), ahead(qo)),
        (qo, ahead(qe)),
        (qe, qo),
        (behind(qo), qe),
    ]
    q_ref[...] = jnp.zeros_like(q_ref)
    for g in range(2):
        for k in range(TAPS):
            flat = to_chunks(*shifted[k], g)
            for c in range(chunks):
                at = (g * chunks + c) * 128
                q_ref[k : k + 1, at : at + 128] = flat[c : c + 1]
    q1, rest = q_ref[...].astype(BF16), q_ref[...]
    rest = rest - q1.astype(F32)
    q2 = rest.astype(BF16)
    q3 = (rest - q2.astype(F32)).astype(BF16)
    q = jnp.concatenate([q1, q2, q3], axis=0)
    xs = chunks * 128
    hist = dot(q[:, :xs], oh_refs[0][...]) + dot(q[:, xs:], oh_refs[1][...])
    hist = hist[:8] + hist[8:16] + hist[16:]
    h_high, h_low = split(hist)
    looked = dot(jnp.concatenate([h_high, h_low], axis=0), e_high[...])
    looked = looked[:8] + looked[8:] + dot(h_high, e_low[...])
    for k in range(TAPS):
        small_ref[k : k + 1, :] += looked[k : k + 1] * line(s_ref)
        at = k * vocab
        small_ref[6 + at // width : 7 + at // width, at % width : at % width + vocab] = hist[k : k + 1]
    small_ref[TAPS : TAPS + 1, :] += q_sum * line(s_ref)
    small_ref[5:6, :] = q_sum * bias + jnp.sum(
        looked[:TAPS] * w_ref[...], axis=0, keepdims=True
    )


def latent_kernel(high0, low0, high1, low1, hl0, hl1, out_ref, latent_ref, sems):
    half, width = latent_ref.shape[1:]
    size = min(LATENT_BATCH, half // 8)
    copies = []
    for g, (high_ref, low_ref, hl_ref) in enumerate(((high0, low0, hl0), (high1, low1, hl1))):
        for w in range(half // 8):
            band = hl_ref[w * 160 : w * 160 + 160, :].astype(F32).T.astype(BF16)
            at = slice(w * 128, w * 128 + 160)
            for n in range(0, width, 256):
                both = dot(band, high_ref[at, n : n + 256])
                rest = dot(band[:64], low_ref[at, n : n + 256])
                out = both[:64] + both[64:] + rest
                latent_ref[g * 8 : g * 8 + 8, 8 * w : 8 * w + 8, n : n + 256] = out.reshape(8, 8, 256)
            if (w + 1) % size == 0:
                done = (pl.ds(g * 8, 8), pl.ds(8 * (w + 1 - size), 8 * size))
                copy = pltpu.make_async_copy(
                    latent_ref.at[done], out_ref.at[done], sems.at[len(copies)]
                )
                copy.start()
                copies.append(copy)
    for copy in copies:
        copy.wait()


def final_kernel(sum_ref, small_ref, w_ref, s_ref, ge_ref, gw_ref, gb_ref, gs_ref):
    vocab, width = sum_ref.shape
    hist = []
    for k in range(TAPS):
        at = k * vocab
        hist.append(small_ref[6 + at // width : 7 + at // width, at % width : at % width + vocab])
    hist = jnp.concatenate(hist + [jnp.zeros((8 - TAPS, vocab), F32)], axis=0).T
    scaled = w_ref[...] * line(s_ref)
    columns = [jnp.broadcast_to(hist[:, k : k + 1], (vocab, 128)) for k in range(TAPS)]
    for n in range(0, width, 128):
        cols = slice(n, n + 128)
        ge_ref[:, cols] = sum_ref[:, cols] + sum(
            columns[k] * scaled[k : k + 1, cols] for k in range(TAPS)
        )
    gw_ref[...] = small_ref[0:TAPS, :]
    gb_ref[...] = small_ref[TAPS : TAPS + 1, :].reshape(width)
    gs_ref[...] = small_ref[TAPS + 1 : TAPS + 2, :].reshape(width)


def in_vmem(*arrays):
    return [pltpu.with_memory_space_constraint(a, pltpu.VMEM) for a in arrays]


def in_hbm(*arrays):
    return [pltpu.with_memory_space_constraint(a, pltpu.HBM) for a in arrays]


def limit(megabytes):
    return pltpu.CompilerParams(vmem_limit_bytes=megabytes * 1024 * 1024)


def cost(flops, moved):
    return pl.CostEstimate(flops=flops, bytes_accessed=moved, transcendentals=0)


def vm(n):
    return [pl.BlockSpec(memory_space=pltpu.VMEM)] * n


def sm(n):
    return [pl.BlockSpec(memory_space=pltpu.SMEM)] * n


def sizes(span):
    count = span // 16
    chunks = count + 1
    per = -(-chunks // 8) * 8
    return count, chunks, per, (span + 16) * 8


def prep_call(*params):
    vocab, width = params[0].shape
    return pl.pallas_call(
        prep_kernel,
        out_shape=(
            pltpu.VMEM((8, vocab), F32),
            pltpu.VMEM((vocab, width), BF16),
            pltpu.VMEM((vocab, width), BF16),
            pltpu.VMEM(params[-1].shape, F32),
        ),
        in_specs=vm(4) + [pl.BlockSpec(memory_space=pl.ANY)],
        out_specs=vm(4),
        scratch_shapes=[pltpu.SemaphoreType.DMA(())],
        compiler_params=limit(4),
        cost_estimate=cost(10**8, 10**6),
        name="prep",
    )(*in_hbm(*params))


def table_call(start, lengths, ids, left, right, table_scores, conv_weight, cotangent):
    rows, half, width = cotangent.shape
    count, chunks, per, d_rows = sizes(2 * half)
    vocab = table_scores.shape[1]
    return pl.pallas_call(
        table_kernel,
        out_shape=(
            pltpu.VMEM((vocab, width), F32),
            pltpu.VMEM((8, 8 + per, 128), F32),
            pltpu.VMEM((2 * per, 128), I32),
            pltpu.VMEM((160 * count, 128), BF16),
            pltpu.VMEM((160 * count, 128), BF16),
        ),
        in_specs=sm(2) + vm(6),
        out_specs=vm(5),
        scratch_shapes=[
            pltpu.VMEM((8 + per, 256), I32),
            pltpu.VMEM((12 * count, 128), F32),
        ]
        + [pltpu.VMEM((d_rows, width), F32)] * 2
        + [pltpu.VMEM((vocab, chunks * 128), BF16)] * 2
        + [pltpu.VMEM((chunks * 128, width), BF16)] * 4,
        compiler_params=limit(34),
        cost_estimate=cost(8 * 10**9, 2 * 10**7),
        name="table_grad",
    )(
        start, lengths, *in_hbm(ids), *in_vmem(left, right, table_scores),
        *in_hbm(conv_weight), *in_vmem(cotangent),
    )


def near_call(start, lengths, weights, id_chunks, e_high, e_low, conv_weight, bias, scorer, hl0, hl1, ct):
    rows, half, width = ct.shape
    count, chunks, per, d_rows = sizes(2 * half)
    vocab = e_high.shape[0]
    return pl.pallas_call(
        near_kernel,
        out_shape=[pltpu.VMEM((8, width), F32)] + [pltpu.VMEM((chunks * 128, width), BF16)] * 4,
        in_specs=sm(2) + vm(9) + [pl.BlockSpec(memory_space=pl.ANY)],
        out_specs=vm(5),
        scratch_shapes=[
            pltpu.VMEM((6, 8 + per, 128), F32),
            pltpu.VMEM((8, 2 * chunks * 128), F32),
            pltpu.VMEM((8 * (TAPS + 1), width), F32),
        ]
        + [pltpu.VMEM((chunks * 128, vocab), BF16)] * 2
        + [pltpu.VMEM((d_rows, width), F32)] * 2
        + [
            pltpu.VMEM((RING * 128, width), F32),
            pltpu.VMEM(ct.shape, F32),
            pltpu.SemaphoreType.DMA(()),
        ],
        compiler_params=limit(30),
        cost_estimate=cost(16 * 10**9, 4 * 10**7),
        name="near",
    )(
        start, lengths, *in_vmem(weights, id_chunks, e_high, e_low),
        *in_hbm(conv_weight, bias, scorer), *in_vmem(hl0, hl1), *in_hbm(ct),
    )


def latent_call(kept, shape):
    rows, half, width = shape
    count = half // 8
    return pl.pallas_call(
        latent_kernel,
        out_shape=jax.ShapeDtypeStruct(shape, F32),
        in_specs=vm(6),
        out_specs=pl.BlockSpec(memory_space=pl.ANY),
        scratch_shapes=[
            pltpu.VMEM(shape, F32),
            pltpu.SemaphoreType.DMA((2 * (count // min(LATENT_BATCH, count)),)),
        ],
        compiler_params=limit(8),
        cost_estimate=cost(4 * 10**9, 10**7),
        name="latent",
    )(*in_vmem(*kept))


def partners(axis, mask):
    return [(i, i ^ mask) for i in range(lax.axis_size(axis))]


def part(v, index, size):
    return lax.dynamic_slice_in_dim(v, index * size, size, 0)


def scatter_sum(v, axis, low, bits):
    group = 1 << bits
    size = v.shape[0] // group
    me = (lax.axis_index(axis) >> low) & (group - 1)
    total = part(v, me, size)
    for m in range(1, group):
        total = total + lax.ppermute(part(v, me ^ m, size), axis, partners(axis, m << low))
    return total


def exchange_sum(v, axis, low, bits):
    return v + sum(
        lax.ppermute(v, axis, partners(axis, m << low)) for m in range(1, 1 << bits)
    )


def gather_back(v, small, axis, low, bits):
    group = 1 << bits
    size = v.shape[0]
    me = (lax.axis_index(axis) >> low) & (group - 1)
    both = jnp.concatenate([v, small], axis=0)
    out = jnp.zeros((group * size,) + v.shape[1:], v.dtype)
    out = lax.dynamic_update_slice_in_dim(out, v, me * size, 0)
    for m in range(1, group):
        got = lax.ppermute(both, axis, partners(axis, m << low))
        out = lax.dynamic_update_slice_in_dim(out, got[:size], (me ^ m) * size, 0)
        small = small + got[size:]
    return out, small


def per_device(byte_ids, lengths, embedding, conv_weight, conv_bias, score_weight, cotangent):
    rows, span = byte_ids.shape
    vocab, width = embedding.shape
    count = span // 16
    seq = lax.axis_size("seq")
    start = (lax.axis_index("seq") * span).reshape(1)

    up = [(i, i + 1) for i in range(seq - 1)]
    left = lax.ppermute(byte_ids, "seq", up)
    right = lax.ppermute(byte_ids, "seq", [(j, i) for i, j in up])
    table_scores, e_high, e_low, ct = prep_call(
        embedding, conv_weight, conv_bias, score_weight, cotangent
    )
    grad_table, weights, id_chunks, hl0, hl1 = table_call(
        start, lengths, byte_ids, left, right, table_scores, conv_weight, ct
    )
    small, *kept = near_call(
        start, lengths, weights, id_chunks, e_high, e_low, conv_weight, conv_bias, score_weight,
        hl0, hl1, cotangent,
    )
    latent = latent_call(kept + [hl0, hl1], cotangent.shape)

    bits = seq.bit_length() - 1
    groups = [("seq", low, min(2, bits - low)) for low in range(0, bits, 2)]
    stages = [("dp", 0, lax.axis_size("dp").bit_length() - 1)] + groups[:-1]
    total = grad_table
    for stage in stages:
        total = scatter_sum(total, *stage)
    size = total.shape[0]
    both = exchange_sum(jnp.concatenate([total, small], axis=0), *groups[-1])
    both, latent = lax.optimization_barrier((both, latent))
    total, small = both[:size], both[size:]
    for stage in reversed(stages):
        total, small = gather_back(total, small, *stage)

    grad_e, grad_w, grad_b, grad_s = pl.pallas_call(
        final_kernel,
        out_shape=(
            jax.ShapeDtypeStruct((vocab, width), F32),
            jax.ShapeDtypeStruct((TAPS, width), F32),
            jax.ShapeDtypeStruct((width,), F32),
            jax.ShapeDtypeStruct((width,), F32),
        ),
        in_specs=vm(4),
        out_specs=vm(4),
        compiler_params=limit(4),
        name="final",
    )(*in_vmem(total, small), *in_hbm(conv_weight, score_weight))
    return latent, grad_e, grad_w, grad_b, grad_s


def solution(mesh):
    placed = (P("dp", "seq"), P("dp"), P(), P(), P(), P(), P("dp", "seq", None))
    return jax.shard_map(
        per_device,
        mesh=mesh,
        in_specs=placed,
        out_specs=(P("dp", "seq", None), P(), P(), P(), P()),
        check_vma=False,
    )
```

time: 132 us -> 77.9 us (0.59)
  Pallas kernels: 81 us -> 41.5 us
  local copies, waits for them, and re-layouts: 7 us -> 1.01 us
  other arithmetic: 5.78 us -> 0.18 us
  waiting for transfers between devices: 16.3 us -> 13.7 us
    pallas_call x3 -> x4, Pallas kernels: 77.7 us -> 39.4 us  [the longest x1 20.3 us: near_call(): pl.pallas_call(near_kernel, out_shape=[pltpu.VMEM((8, width), F32)] + [pl...]
    reshape x5 -> x0, local copies, waits for them, and re-layouts: 4.1 us -> none  [the longest x2 2.53 us: per_device(): bias, scorer = (conv_bias.reshape(1, width), score_weight.reshape(1, width))]
    ppermute x3, waiting for transfers between devices: 9.17 us -> 5.28 us  [exchange_sum(): lax.ppermute(v, axis, partners(axis, m << low))]
    pallas_call x2 -> x0, other arithmetic: 2.54 us -> none  [per_device(): pl.pallas_call(final_kernel, out_shape=(jax.ShapeDtypeStruct((vocab, widt...]
    unnamed x6 -> x2, local copies, waits for them, and re-layouts: 1.48 us -> 0.01 us
  transfers between devices with their start and end apart: 13 -> 13, of which waited for: 6 -> 8; matrix products, arithmetic and copies ran while one was open for 3% -> 0% of each run, Pallas kernels for 43% -> 37%
where the time goes in v2:
time: 77.9 us; the launch traced here: 77.4 us
  Pallas kernels  41.5 us (53%)
  starting transfers between devices  20.2 us (26%)
  waiting for transfers between devices  13.7 us (18%)
  local copies, waits for them, and re-layouts  1.01 us (1%)
  between operations  0.83 us (1%)
    pallas_call x1, Pallas kernels, near_call(): pl.pallas_call(near_kernel, out_shape=[pltpu.VMEM((8, width), F32)] + [pl...  20.3 us
    pallas_call x1, Pallas kernels, table_call(): pl.pallas_call(table_kernel, out_shape=(pltpu.VMEM((vocab, width), F32),...  11.1 us
    ppermute x4, waiting for transfers between devices, gather_back(): got = lax.ppermute(both, axis, partners(axis, m << low))  6.06 us
    ppermute x3, starting transfers between devices, exchange_sum(): lax.ppermute(v, axis, partners(axis, m << low))  5.51 us
    ppermute x3, waiting for transfers between devices, exchange_sum(): lax.ppermute(v, axis, partners(axis, m << low))  5.28 us
    ppermute x4, starting transfers between devices, scatter_sum(): lax.ppermute(part(v, me ^ m, size), axis, partners(axis, m << low))  4.95 us
    ppermute x1, starting transfers between devices, per_device(): left = lax.ppermute(byte_ids, 'seq', up)  4.85 us
    pallas_call x1, Pallas kernels, prep_call(): pl.pallas_call(prep_kernel, out_shape=(pltpu.VMEM((8, vocab), F32), pltpu...  4.12 us
  transfers between devices with their start and end apart: 13, of which 8 were waited for; matrix products, arithmetic and copies ran while one was open for 0% of the time, Pallas kernels for 37%

profile of v2, /device:TPU:0, one launch (start us, length us, event | category | flops | bytes accessed | tf_op | source)
XLA Modules:
  0.0 77.4 jit_solution(2993107691486477760)
XLA Ops:
  0.6 4.8 %collective-permute-start = (s32[16,256]{1,0:T(8,128)}, s32[16,256]{1,0:T(8,128)S(1)}, u32[]{:S(2)}, u32[]{:S(2)}) collective-permute-start(s32[16,256]{1,0:T(8,128)} %ids_ref.1), channel_id=1, source_target_pairs={{0,1},{1,2},{2,3},{3,4},{4,5},{5,6},{6,7},{7,8},{8,9},{9,10},{10,1... | collective-permute-start | bytes 49160 | tf_op jit(solution)/shard_map/ppermute | solution.py:728
  5.5 1.3 %collective-permute-start.1 = (s32[16,256]{1,0:T(8,128)}, s32[16,256]{1,0:T(8,128)S(1)}, u32[]{:S(2)}, u32[]{:S(2)}) collective-permute-start(s32[16,256]{1,0:T(8,128)} %ids_ref.1), channel_id=1, source_target_pairs={{1,0},{2,1},{3,2},{4,3},{5,4},{6,5},{7,6},{8,7},{9,8},{10,9},{11,1... | collective-permute-start | bytes 49160 | tf_op jit(solution)/shard_map/ppermute | solution.py:729
  6.8 4.1 %prep.1 = (f32[8,256]{1,0:T(8,128)S(1)}, bf16[256,768]{1,0:T(8,128)(2,1)S(1)}, bf16[256,768]{1,0:T(8,128)(2,1)S(1)}, f32[16,128,768]{2,1,0:T(8,128)S(1)}) custom-call(f32[256,768]{1,0:T(8,128)} %e_ref.1, f32[4,768]{1,0:T(4,128)} %w_ref.7, f32[768]{0:T(1024)} %b_ref.3, f32[768]{0:T(1024)} %s_ref.5, f32[16,128,768]{2,1,0:T(8,128)} %ct_hbm.3), custom_call_target="tpu_custom_call" | custom-call | flops 100000000 | bytes 1000000 | tf_op jit(solution)/shard_map/prep/pallas_call | solution.py:586
  10.9 0.4 collective-permute-done.1.right_ref
  11.3 11.1 %table_grad.1 = (f32[256,768]{1,0:T(8,128)S(1)}, f32[8,32,128]{2,1,0:T(8,128)S(1)}, s32[48,128]{1,0:T(8,128)S(1)}, bf16[2560,128]{1,0:T(8,128)(2,1)S(1)}, bf16[2560,128]{1,0:T(8,128)(2,1)S(1)}) custom-call(s32[1]{0:T(128)} %bitcast.start_ref, s32[16]{0:T(128)S(1)} %copy-done, s32[16,256]{1,0:T(8,128)} %ids_ref.1, ...), custom_call_target="tpu_custom_call" | custom-call | flops 8000000000 | bytes 20000000 | tf_op jit(solution)/shard_map/table_grad/pallas_call | solution.py:607
  22.4 0.8 %constant_dynamic-slice_fusion.3 = f32[128,768]{1,0:T(8,128)} fusion(f32[256,768]{1,0:T(8,128)S(1)} %get-tuple-element.27, s32[]{:T(128)S(6)} %select_n.25), kind=kLoop, calls=%fused_computation.18 | loop fusion | bytes 786436 | tf_op jit(solution)/shard_map/dynamic_slice | solution.py:687
  23.2 1.9 %collective-permute-done.2 = f32[128,768]{1,0:T(8,128)S(1)} collective-permute-done((f32[128,768]{1,0:T(8,128)}, f32[128,768]{1,0:T(8,128)S(1)}, u32[]{:S(2)}, u32[]{:S(2)}) %collective-permute-start.2) | collective-permute-done | bytes 393248 | tf_op jit(solution)/shard_map/ppermute | solution.py:696
  25.2 4.3 %collective-permute-start.5 = (f32[32,768]{1,0:T(8,128)S(1)}, f32[32,768]{1,0:T(8,128)S(1)}, u32[]{:S(2)}, u32[]{:S(2)}) collective-permute-start(f32[32,768]{1,0:T(8,128)S(1)} %get-tuple-element.46), channel_id=1, source_target_pairs={{0,3},{1,2},{2,1},{3,0},{4,7},{5,6},{6,5},{7,4},{8,11},{9,10},{10,... | collective-permute-start | bytes 294920 | tf_op jit(solution)/shard_map/ppermute | solution.py:696
  29.5 0.6 collective-permute-start.3
  30.2 20.3 %near.1 = (f32[8,768]{1,0:T(8,128)S(1)}, bf16[2176,768]{1,0:T(8,128)(2,1)S(1)}, bf16[2176,768]{1,0:T(8,128)(2,1)S(1)}, bf16[2176,768]{1,0:T(8,128)(2,1)S(1)}, bf16[2176,768]{1,0:T(8,128)(2,1)S(1)}) custom-call(s32[1]{0:T(128)} %bitcast.start_ref, s32[16]{0:T(128)S(1)} %copy-done, f32[8,32,128]{2,1,0:T(8,128)S(1)} %get-tuple-element.28.weights_ref, ...), custom_call_target="tpu_custom_call" | custom-call | flops 16000000000 | bytes 40000000 | tf_op jit(solution)/shard_map/near/pallas_call | solution.py:638
  50.6 4.9 %collective-permute-start.8 = (f32[40,768]{1,0:T(8,128)S(1)}, f32[40,768]{1,0:T(8,128)S(1)}, u32[]{:S(2)}, u32[]{:S(2)}) collective-permute-start(f32[40,768]{1,0:T(8,128)S(1)} %pad_maximum_fusion.1), channel_id=1, source_target_pairs={{0,12},{1,13},{2,14},{3,15},{4,8},{5,9},{6,10},{7,11},{8,4},{9,5},... | collective-permute-start | bytes 368648 | tf_op jit(solution)/shard_map/ppermute | solution.py:702
  55.5 0.6 collective-permute-start.7
  56.1 3.9 %latent.1 = f32[16,128,768]{2,1,0:T(8,128)} custom-call(bf16[2176,768]{1,0:T(8,128)(2,1)S(1)} %get-tuple-element.35.high0, bf16[2176,768]{1,0:T(8,128)(2,1)S(1)} %get-tuple-element.36.low0, bf16[2176,768]{1,0:T(8,128)(2,1)S(1)} %get-tuple-element.37.high1, bf16[2176,768]{1,0:T(8,128)(2,1)S(1)} %get-tuple-element.38.low1, ...), custom_call_target="tpu_custom_call" | custom-call | flops 4000000000 | bytes 10000000 | tf_op jit(solution)/shard_map/latent/pallas_call | solution.py:667
  60.0 1.8 %collective-permute-done.6 = f32[40,768]{1,0:T(8,128)S(1)} collective-permute-done((f32[40,768]{1,0:T(8,128)S(1)}, f32[40,768]{1,0:T(8,128)S(1)}, u32[]{:S(2)}, u32[]{:S(2)}) %collective-permute-start.6) | collective-permute-done | bytes 122912 | tf_op jit(solution)/shard_map/ppermute | solution.py:702
  61.9 3.5 %collective-permute-done.7 = f32[40,768]{1,0:T(8,128)S(1)} collective-permute-done((f32[40,768]{1,0:T(8,128)S(1)}, f32[40,768]{1,0:T(8,128)S(1)}, u32[]{:S(2)}, u32[]{:S(2)}) %collective-permute-start.7) | collective-permute-done | bytes 122912 | tf_op jit(solution)/shard_map/ppermute | solution.py:702
  65.4 0.5 collective-permute-start.9
  65.9 1.7 %collective-permute-start.10 = (f32[40,768]{1,0:T(8,128)S(1)}, f32[40,768]{1,0:T(8,128)S(1)}, u32[]{:S(2)}, u32[]{:S(2)}) collective-permute-start(f32[40,768]{1,0:T(8,128)S(1)} %add_add_fusion), channel_id=1, source_target_pairs={{0,2},{1,3},{2,0},{3,1},{4,6},{5,7},{6,4},{7,5},{8,10},{9,11},{10,... | collective-permute-start | bytes 368648 | tf_op jit(solution)/shard_map/ppermute | solution.py:714
  67.6 1.3 %collective-permute-start.11 = (f32[40,768]{1,0:T(8,128)S(1)}, f32[40,768]{1,0:T(8,128)S(1)}, u32[]{:S(2)}, u32[]{:S(2)}) collective-permute-start(f32[40,768]{1,0:T(8,128)S(1)} %add_add_fusion), channel_id=1, source_target_pairs={{0,3},{1,2},{2,1},{3,0},{4,7},{5,6},{6,5},{7,4},{8,11},{9,10},{10,... | collective-permute-start | bytes 368648 | tf_op jit(solution)/shard_map/ppermute | solution.py:714
  69.0 2.2 %collective-permute-done.9 = f32[40,768]{1,0:T(8,128)S(1)} collective-permute-done((f32[40,768]{1,0:T(8,128)S(1)}, f32[40,768]{1,0:T(8,128)S(1)}, u32[]{:S(2)}, u32[]{:S(2)}) %collective-permute-start.9) | collective-permute-done | bytes 122912 | tf_op jit(solution)/shard_map/ppermute | solution.py:714
  71.2 0.9 %collective-permute-done.10 = f32[40,768]{1,0:T(8,128)S(1)} collective-permute-done((f32[40,768]{1,0:T(8,128)S(1)}, f32[40,768]{1,0:T(8,128)S(1)}, u32[]{:S(2)}, u32[]{:S(2)}) %collective-permute-start.10) | collective-permute-done | bytes 122912 | tf_op jit(solution)/shard_map/ppermute | solution.py:714
  72.1 1.3 %collective-permute-done.11 = f32[40,768]{1,0:T(8,128)S(1)} collective-permute-done((f32[40,768]{1,0:T(8,128)S(1)}, f32[40,768]{1,0:T(8,128)S(1)}, u32[]{:S(2)}, u32[]{:S(2)}) %collective-permute-start.11) | collective-permute-done | bytes 122912 | tf_op jit(solution)/shard_map/ppermute | solution.py:714
  73.5 0.1 collective-permute-start.12
  73.7 1.6 %collective-permute-done.12 = f32[136,768]{1,0:T(8,128)S(1)} collective-permute-done((f32[136,768]{1,0:T(8,128)S(1)}, f32[136,768]{1,0:T(8,128)S(1)}, u32[]{:S(2)}, u32[]{:S(2)}) %collective-permute-start.12) | collective-permute-done | bytes 417824 | tf_op jit(solution)/shard_map/ppermute | solution.py:714
  75.3 2.1 %final.1 = (f32[256,768]{1,0:T(8,128)}, f32[4,768]{1,0:T(4,128)}, f32[768]{0:T(1024)}, f32[768]{0:T(1024)}) custom-call(f32[256,768]{1,0:T(8,128)S(1)} %slice_dynamic-update-slice_fusion.sum_ref, f32[8,768]{1,0:T(8,128)S(1)} %slice_add_fusion.small_ref, f32[4,768]{1,0:T(4,128)} %w_ref.7, f32[768]{0:T(1024)} %s_ref.5), custom_call_target="tpu_custom_call" | custom-call | tf_op jit(solution)/shard_map/final/pallas_call | solution.py:755
  (26 shorter events, 0.4 us)
Async XLA Ops:
  0.6 10.3 %collective-permute-start = (s32[16,256]{1,0:T(8,128)}, s32[16,256]{1,0:T(8,128)S(1)}, u32[]{:S(2)}, u32[]{:S(2)}) collective-permute-start(s32[16,256]{1,0:T(8,128)} %ids_ref.1), channel_id=1, source_target_pairs={{0,1},{1,2},{2,3},{3,4},{4,5},{5,6},{6,7},{7,8},{8,9},{9,10},{10,1... | collective-permute-start | bytes 49160 | tf_op jit(solution)/shard_map/ppermute | solution.py:728
  5.5 5.8 %collective-permute-start.1 = (s32[16,256]{1,0:T(8,128)}, s32[16,256]{1,0:T(8,128)S(1)}, u32[]{:S(2)}, u32[]{:S(2)}) collective-permute-start(s32[16,256]{1,0:T(8,128)} %ids_ref.1), channel_id=1, source_target_pairs={{1,0},{2,1},{3,2},{4,3},{5,4},{6,5},{7,6},{8,7},{9,8},{10,9},{11,1... | collective-permute-start | bytes 49160 | tf_op jit(solution)/shard_map/ppermute | solution.py:729
  6.8 4.5 %copy-start = (s32[16]{0:T(128)S(1)}, s32[16]{0:T(128)}, u32[]{:S(2)}) copy-start(s32[16]{0:T(128)} %len_ref.3) | copy-start | bytes 196
  23.2 1.9 %collective-permute-start.2 = (f32[128,768]{1,0:T(8,128)}, f32[128,768]{1,0:T(8,128)S(1)}, u32[]{:S(2)}, u32[]{:S(2)}) collective-permute-start(f32[128,768]{1,0:T(8,128)} %constant_dynamic-slice_fusion.3), channel_id=1, source_target_pairs={{0,16},{16,0},{1,17},{17,1},{2,18},{18,2},{3,19},{19,3},{4,20},{20... | collective-permute-start | bytes 1179656 | tf_op jit(solution)/shard_map/ppermute | solution.py:696
  25.2 25.3 %collective-permute-start.5 = (f32[32,768]{1,0:T(8,128)S(1)}, f32[32,768]{1,0:T(8,128)S(1)}, u32[]{:S(2)}, u32[]{:S(2)}) collective-permute-start(f32[32,768]{1,0:T(8,128)S(1)} %get-tuple-element.46), channel_id=1, source_target_pairs={{0,3},{1,2},{2,1},{3,0},{4,7},{5,6},{6,5},{7,4},{8,11},{9,10},{10,... | collective-permute-start | bytes 294920 | tf_op jit(solution)/shard_map/ppermute | solution.py:696
  29.5 21.0 %collective-permute-start.4 = (f32[32,768]{1,0:T(8,128)S(1)}, f32[32,768]{1,0:T(8,128)S(1)}, u32[]{:S(2)}, u32[]{:S(2)}) collective-permute-start(f32[32,768]{1,0:T(8,128)S(1)} %get-tuple-element.47), channel_id=1, source_target_pairs={{0,2},{1,3},{2,0},{3,1},{4,6},{5,7},{6,4},{7,5},{8,10},{9,11},{10,... | collective-permute-start | bytes 294920 | tf_op jit(solution)/shard_map/ppermute | solution.py:696
  29.5 21.0 %collective-permute-start.3 = (f32[32,768]{1,0:T(8,128)S(1)}, f32[32,768]{1,0:T(8,128)S(1)}, u32[]{:S(2)}, u32[]{:S(2)}) collective-permute-start(f32[32,768]{1,0:T(8,128)S(1)} %get-tuple-element.45), channel_id=1, source_target_pairs={{0,1},{1,0},{2,3},{3,2},{4,5},{5,4},{6,7},{7,6},{8,9},{9,8},{10,11... | collective-permute-start | bytes 294920 | tf_op jit(solution)/shard_map/ppermute | solution.py:696
  50.6 9.4 %collective-permute-start.8 = (f32[40,768]{1,0:T(8,128)S(1)}, f32[40,768]{1,0:T(8,128)S(1)}, u32[]{:S(2)}, u32[]{:S(2)}) collective-permute-start(f32[40,768]{1,0:T(8,128)S(1)} %pad_maximum_fusion.1), channel_id=1, source_target_pairs={{0,12},{1,13},{2,14},{3,15},{4,8},{5,9},{6,10},{7,11},{8,4},{9,5},... | collective-permute-start | bytes 368648 | tf_op jit(solution)/shard_map/ppermute | solution.py:702
  55.5 6.4 %collective-permute-start.6 = (f32[40,768]{1,0:T(8,128)S(1)}, f32[40,768]{1,0:T(8,128)S(1)}, u32[]{:S(2)}, u32[]{:S(2)}) collective-permute-start(f32[40,768]{1,0:T(8,128)S(1)} %pad_maximum_fusion.1), channel_id=1, source_target_pairs={{0,4},{1,5},{2,6},{3,7},{4,0},{5,1},{6,2},{7,3},{8,12},{9,13},{10,... | collective-permute-start | bytes 368648 | tf_op jit(solution)/shard_map/ppermute | solution.py:702
  55.5 9.8 %collective-permute-start.7 = (f32[40,768]{1,0:T(8,128)S(1)}, f32[40,768]{1,0:T(8,128)S(1)}, u32[]{:S(2)}, u32[]{:S(2)}) collective-permute-start(f32[40,768]{1,0:T(8,128)S(1)} %pad_maximum_fusion.1), channel_id=1, source_target_pairs={{0,8},{1,9},{2,10},{3,11},{4,12},{5,13},{6,14},{7,15},{8,0},{9,1},... | collective-permute-start | bytes 368648 | tf_op jit(solution)/shard_map/ppermute | solution.py:702
  65.4 5.8 %collective-permute-start.9 = (f32[40,768]{1,0:T(8,128)S(1)}, f32[40,768]{1,0:T(8,128)S(1)}, u32[]{:S(2)}, u32[]{:S(2)}) collective-permute-start(f32[40,768]{1,0:T(8,128)S(1)} %add_add_fusion), channel_id=1, source_target_pairs={{0,1},{1,0},{2,3},{3,2},{4,5},{5,4},{6,7},{7,6},{8,9},{9,8},{10,11... | collective-permute-start | bytes 368648 | tf_op jit(solution)/shard_map/ppermute | solution.py:714
  65.9 6.2 %collective-permute-start.10 = (f32[40,768]{1,0:T(8,128)S(1)}, f32[40,768]{1,0:T(8,128)S(1)}, u32[]{:S(2)}, u32[]{:S(2)}) collective-permute-start(f32[40,768]{1,0:T(8,128)S(1)} %add_add_fusion), channel_id=1, source_target_pairs={{0,2},{1,3},{2,0},{3,1},{4,6},{5,7},{6,4},{7,5},{8,10},{9,11},{10,... | collective-permute-start | bytes 368648 | tf_op jit(solution)/shard_map/ppermute | solution.py:714
  67.6 5.8 %collective-permute-start.11 = (f32[40,768]{1,0:T(8,128)S(1)}, f32[40,768]{1,0:T(8,128)S(1)}, u32[]{:S(2)}, u32[]{:S(2)}) collective-permute-start(f32[40,768]{1,0:T(8,128)S(1)} %add_add_fusion), channel_id=1, source_target_pairs={{0,3},{1,2},{2,1},{3,0},{4,7},{5,6},{6,5},{7,4},{8,11},{9,10},{10,... | collective-permute-start | bytes 368648 | tf_op jit(solution)/shard_map/ppermute | solution.py:714
  73.5 1.8 %collective-permute-start.12 = (f32[136,768]{1,0:T(8,128)S(1)}, f32[136,768]{1,0:T(8,128)S(1)}, u32[]{:S(2)}, u32[]{:S(2)}) collective-permute-start(f32[136,768]{1,0:T(8,128)S(1)} %pad_maximum_fusion), channel_id=1, source_target_pairs={{0,16},{16,0},{1,17},{17,1},{2,18},{18,2},{3,19},{19,3},{4,20},{20... | collective-permute-start | bytes 1253384 | tf_op jit(solution)/shard_map/ppermute | solution.py:714

commit v3 on v2

--- a/solution.py
+++ b/solution.py
@@ -11,8 +11,8 @@
 HIGH = lax.Precision.HIGHEST
 ROWS = 16
 TAPS = 4
-TABLE_BATCH, MIX_BATCH, LATENT_BATCH = 4, 2, 4
-RING = 10
+TABLE_BATCH, MIX_BATCH, LATENT_BATCH = 4, 4, 4
+RING = 18
 RELS = (-2, -1, 0, 1, 2, 3)
 NT = (((1,), (1,)), ((), ()))
 TN = (((0,), (0,)), ((), ()))
@@ -224,22 +224,46 @@
     return [(g, list(range(b, b + size))) for g in range(2) for b in range(0, count, size)]
 
 
-def window_grads(ct_ref, hl, d_ref, w, n):
+class Halves:
+    def __init__(self, first, second):
+        self.refs, self.size = (first, second), first.shape[0]
+
+    def parts(self, lo, hi):
+        for ref, base in zip(self.refs, (0, self.size)):
+            a, b = max(lo, base), min(hi, base + self.size)
+            if a < b:
+                yield ref, a - base, b - base, a - lo, b - lo
+
+    def load(self, lo, hi, cols):
+        found = [ref[a:b, cols] for ref, a, b, _, _ in self.parts(lo, hi)]
+        return found[0] if len(found) == 1 else jnp.concatenate(found, axis=0)
+
+    def store(self, lo, value, cols):
+        for ref, a, b, i, j in self.parts(lo, lo + value.shape[0]):
+            ref[a:b, cols] = value[i:j]
+
+
+def window_grads(ct_ref, both_ref, hl, d, w, n):
     wide = jnp.concatenate([hl, hl], axis=1)
     at = 128 * w + 48
-    high, low = split(ct_ref[:, 8 * w : 8 * w + 8, n : n + 256].reshape(64, 256))
+    cols = slice(n, n + 256)
+    high, low = split(ct_ref[:, 8 * w : 8 * w + 8, cols].reshape(64, 256))
+    both_ref[128 * w : 128 * w + 64, cols] = high
+    both_ref[128 * w + 64 : 128 * w + 128, cols] = low
     grads = dot(wide, jnp.concatenate([high, high, low, low], axis=0))
-    d_ref[at : at + 32, n : n + 256] += grads[:32]
-    d_ref[at + 32 : at + 160, n : n + 256] = grads[32:]
+    d.store(at, d.load(at, at + 32, cols) + grads[:32], cols)
+    d.store(at + 32, grads[32:], cols)
 
 
 def table_kernel(
     start_ref, len_ref, ids_ref, left_ref, right_ref, t_ref, w_ref, ct_ref,
-    grad_ref, weights_ref, chunks_ref, hl0, hl1,
+    grad_ref, weights_ref, chunks_ref, hl0, hl1, both0, both1, d00, d01, d10, d11,
     ids_scr, bands_ref, *scratch,
 ):
-    d_refs, oh_refs, high_refs, low_refs = (scratch[2 * i : 2 * i + 2] for i in range(4))
-    hl_refs = (hl0, hl1)
+    oh0, oh1, high_ref, low_ref = scratch
+    oh_refs = (oh0, oh1)
+    hl_refs, both_refs = (hl0, hl1), (both0, both1)
+    ds = (Halves(d00, d01), Halves(d10, d11))
     count = ids_ref.shape[1] // 16
     chunks = count + 1
     vocab = t_ref.shape[1]
@@ -260,9 +284,9 @@
     for g in range(2):
         chunks_ref[g * per : g * per + per, :] = to_chunks(ids[0], ids[1], g)
     width = w_ref.shape[1]
-    for d_ref in d_refs:
-        d_ref[:80, :] = jnp.zeros((80, width), F32)
-        d_ref[-64:, :] = jnp.zeros((64, width), F32)
+    for d in ds:
+        d.store(0, jnp.zeros((80, width), F32), slice(None))
+        d.store(2 * d.size - 64, jnp.zeros((64, width), F32), slice(None))
 
     diagonal = diagonals()
 
@@ -273,12 +297,12 @@
             if not made:
                 made.append(banded(bands_ref, g, w, count, diagonal))
                 hl_refs[g][w * 160 : w * 160 + 160, :] = made[0]
-            window_grads(ct_ref.at[g * 8 : g * 8 + 8], made[0], d_refs[g], w, n)
+            window_grads(ct_ref.at[g * 8 : g * 8 + 8], both_refs[g], made[0], ds[g], w, n)
 
         return [functools.partial(step, n) for n in range(0, width, 256)]
 
-    def part_steps(g, c):
-        d_ref, oh_ref, high_ref, low_ref = (x[g] for x in (d_refs, oh_refs, high_refs, low_refs))
+    def part_steps(g, c, put):
+        d, oh_ref = ds[g], oh_refs[g]
         to = c * 128
         size = 128 if c < count else 64
 
@@ -287,28 +311,30 @@
             oh_ref[:, to : to + 128] = one_hot_t(ids, vocab)
             if size < 128:
                 zero = jnp.zeros((128 - size, width), BF16)
-                high_ref[to + size : to + 128, :] = zero
-                low_ref[to + size : to + 128, :] = zero
+                high_ref[put + size : put + 128, :] = zero
+                low_ref[put + size : put + 128, :] = zero
 
         def step(n):
             cols = slice(n, n + 128)
             taps = [jnp.broadcast_to(w_ref[k : k + 1, cols], (64, 128)) for k in range(TAPS)]
             for i in range(0, size, 64):
-                near = d_ref[to + 24 + i : to + 112 + i, cols]
+                near = d.load(to + 24 + i, to + 112 + i, cols)
                 total = sum(taps[3 - k] * near[8 * k : 8 * k + 64] for k in range(TAPS))
                 high, low = split(total)
-                high_ref[to + i : to + i + 64, cols] = high
-                low_ref[to + i : to + i + 64, cols] = low
+                high_ref[put + i : put + i + 64, cols] = high
+                low_ref[put + i : put + i + 64, cols] = low
 
         return [mark] + [functools.partial(step, n) for n in range(0, width, 128)]
 
-    def sum_steps(g, cs):
+    def sum_steps(g, cs, put):
+        held = slice(put, put + 128 * len(cs))
         at = slice(cs[0] * 128, cs[-1] * 128 + 128)
 
         def step(n):
             cols = slice(n, n + 256)
             oh = oh_refs[g][:, at]
-            total = dot(oh, high_refs[g][at, cols]) + dot(oh, low_refs[g][at, cols])
+            both = jnp.concatenate([high_ref[held, cols], low_ref[held, cols]], axis=0)
+            total = dot(jnp.concatenate([oh, oh], axis=1), both)
             if g == 0 and cs[0] == 0:
                 grad_ref[:, cols] = total
             else:
@@ -317,25 +343,25 @@
         return [functools.partial(step, n) for n in range(0, width, 256)]
 
     stages = [[], [], []]
-    for g, ws in batches(count, min(TABLE_BATCH, count)):
+    for t, (g, ws) in enumerate(batches(count, min(TABLE_BATCH, count))):
         cs = ws + [count] * (ws[-1] == count - 1)
+        put = t % 3 * (TABLE_BATCH + 1) * 128
         stages[0].append(sum((grad_steps(g, w) for w in ws), []))
-        stages[1].append(sum((part_steps(g, c) for c in cs), []))
-        stages[2].append(sum_steps(g, cs))
+        stages[1].append(sum((part_steps(g, c, put + 128 * i) for i, c in enumerate(cs)), []))
+        stages[2].append(sum_steps(g, cs, put))
     run_stages(stages, (0, 1, 2))
 
 
 def near_kernel(
-    start_ref, len_ref, weights_ref, chunks_ref, e_high, e_low, w_ref, b_ref, s_ref, hl0, hl1, ct_hbm,
+    start_ref, len_ref, weights_ref, chunks_ref, e_high, e_low, w_ref, b_ref, s_ref, both0, both1, d00, d01, d10, d11,
     small_ref, high0, low0, high1, low1,
-    near_ref, q_ref, sums_ref, oh0, oh1, d0, d1, x_ref, ct_ref, sem,
+    near_ref, q_ref, sums_ref, oh0, oh1, x_ref,
 ):
-    copy = pltpu.make_async_copy(ct_hbm, ct_ref, sem)
-    copy.start()
-    oh_refs, d_refs, hl_refs = (oh0, oh1), (d0, d1), (hl0, hl1)
+    oh_refs, both_refs = (oh0, oh1), (both0, both1)
+    ds = (Halves(d00, d01), Halves(d10, d11))
     high_refs, low_refs = (high0, high1), (low0, low1)
     padded = weights_ref.shape[1]
-    count = ct_ref.shape[1] // 8
+    count = both0.shape[0] // 128
     chunks = count + 1
     vocab, width = e_high.shape
     start = start_ref[0]
@@ -344,8 +370,6 @@
     near_ref[...] = jnp.zeros_like(near_ref)
     sums_ref[...] = jnp.zeros_like(sums_ref)
     diagonal = diagonals()
-    for d_ref in d_refs:
-        d_ref[48:80, :] = jnp.zeros((32, width), F32)
     bias = line(b_ref)
     turned = chunks_ref[...].astype(F32).T
 
@@ -372,7 +396,8 @@
         def step(n):
             cols = slice(n, n + 256)
             oh = oh_refs[g][at, :]
-            x = dot(oh, e_high[:, cols]) + dot(oh, e_low[:, cols])
+            table = jnp.concatenate([e_high[:, cols], e_low[:, cols]], axis=0)
+            x = dot(jnp.concatenate([oh, oh], axis=1), table)
             for i, c in enumerate(cs):
                 to = slot(g, c)
                 x_ref[to : to + 128, cols] = x[i * 128 : i * 128 + 128]
@@ -380,13 +405,6 @@
         return [functools.partial(mark, c) for c in cs] + [
             functools.partial(step, n) for n in range(0, width, 256)
         ]
-
-    def grad_steps(g, w):
-        def step(n):
-            hl = hl_refs[g][w * 160 : w * 160 + 160, :]
-            window_grads(ct_ref.at[g * 8 : g * 8 + 8], hl, d_refs[g], w, n)
-
-        return [functools.partial(step, n) for n in range(0, width, 256)]
 
     def conv_steps(g, c):
         at = c * 128
@@ -399,7 +417,7 @@
             first = jnp.broadcast_to(bias[:, cols], (step_size, 128))
             sums = [sums_ref[8 * k : 8 * k + 8, cols] for k in range(TAPS + 1)]
             for i in range(at, at + size, step_size):
-                d = d_refs[g][i + 48 : i + 48 + step_size, cols]
+                d = ds[g].load(i + 48, i + 48 + step_size, cols)
                 x = bytes_at(g, c, i - at, step_size + 24, cols)
                 total = first
                 products = [d]
@@ -420,10 +438,17 @@
     def meet_steps(g, w):
         at = slice(w * 128, w * 128 + 160)
 
+        made = []
+
+        def product(n):
+            cols = slice(n, n + 256)
+            ct = both_refs[g][128 * w : 128 * w + 128, cols]
+            wide = jnp.concatenate([high_refs[g][at, cols], low_refs[g][at, cols]], axis=1)
+            both = dot(wide, jnp.concatenate([ct, ct], axis=1), NT)
+            made.append(both if n == 0 else made.pop() + both)
+
         def meet():
-            ct = ct_ref[g * 8 : g * 8 + 8, 8 * w : 8 * w + 8, :].reshape(64, width)
-            ct = jnp.concatenate(split(ct), axis=0)
-            product = dot(high_refs[g][at, :], ct, NT) + dot(low_refs[g][at, :], ct, NT)
+            product = made.pop()
             for i, r in enumerate(RELS):
                 total = jnp.zeros((8, 128), F32)
                 for u in range(8):
@@ -433,17 +458,15 @@
                 found = found + pltpu.roll(found, 64, 1)
                 near_ref[i, 8 + w : 9 + w, g * 64 : g * 64 + 64] = found[:, g * 64 : g * 64 + 64]
 
-        return [meet]
-
-    stages = [[], [], [], []]
+        return [functools.partial(product, n) for n in range(0, width, 256)] + [meet]
+
+    stages = [[], [], []]
     for g, ws in batches(count, MIX_BATCH):
         cs = ws + [count] * (ws[-1] == count - 1)
         stages[0].append(look_up_steps(g, cs))
-        stages[1].append(sum((grad_steps(g, w) for w in ws), []))
-        stages[2].append(sum((conv_steps(g, c) for c in cs), []))
-        stages[3].append(sum((meet_steps(g, w) for w in ws), []))
-    stages[1][0].insert(0, copy.wait)
-    run_stages(stages, (0, 1, 2, 4))
+        stages[1].append(sum((conv_steps(g, c) for c in cs), []))
+        stages[2].append(sum((meet_steps(g, w) for w in ws), []))
+    run_stages(stages, (0, 2, 4))
 
     for k in range(TAPS + 1):
         total = jnp.sum(sums_ref[8 * k : 8 * k + 8, :], axis=0, keepdims=True)
@@ -531,23 +554,39 @@
         copy.wait()
 
 
-def final_kernel(sum_ref, small_ref, w_ref, s_ref, ge_ref, gw_ref, gb_ref, gs_ref):
-    vocab, width = sum_ref.shape
+def final_kernel(stages, place_ref, mine_ref, theirs_ref, w_ref, s_ref, ge_ref, gw_ref, gb_ref, gs_ref):
+    vocab, width = ge_ref.shape
+    places = [(0, None)]
+    size = vocab
+    for i in reversed(range(len(stages))):
+        places = [(low | m << 2 * i, None) for m in range(1 << stages[i][2]) for low, _ in places]
+    for stage in stages:
+        size >>= stage[2]
+    half = len(places) // 2
+    pieces = [(mine_ref, p * (size + 8)) for p in range(half)]
+    pieces += [(theirs_ref, p * (size + 8)) for p in range(half)]
+    small = sum(ref[at + size : at + size + 8, :] for ref, at in pieces)
     hist = []
     for k in range(TAPS):
         at = k * vocab
-        hist.append(small_ref[6 + at // width : 7 + at // width, at % width : at % width + vocab])
+        hist.append(small[6 + at // width : 7 + at // width, at % width : at % width + vocab])
     hist = jnp.concatenate(hist + [jnp.zeros((8 - TAPS, vocab), F32)], axis=0).T
     scaled = w_ref[...] * line(s_ref)
-    columns = [jnp.broadcast_to(hist[:, k : k + 1], (vocab, 128)) for k in range(TAPS)]
-    for n in range(0, width, 128):
-        cols = slice(n, n + 128)
-        ge_ref[:, cols] = sum_ref[:, cols] + sum(
-            columns[k] * scaled[k : k + 1, cols] for k in range(TAPS)
-        )
-    gw_ref[...] = small_ref[0:TAPS, :]
-    gb_ref[...] = small_ref[TAPS : TAPS + 1, :].reshape(width)
-    gs_ref[...] = small_ref[TAPS + 1 : TAPS + 2, :].reshape(width)
+    for k in range(TAPS):
+        turned = jnp.broadcast_to(hist[:, k : k + 1], (vocab, 128))
+        for n in range(0, width, 128):
+            add = turned * scaled[k : k + 1, n : n + 128]
+            ge_ref[:, n : n + 128] = add if k == 0 else ge_ref[:, n : n + 128] + add
+    for (mask, _), (ref, at) in zip(places, pieces):
+        row, rest = 0, vocab
+        for i, stage in enumerate(stages):
+            rest >>= stage[2]
+            row = row + (place_ref[i] ^ ((mask >> 2 * i) & 3)) * rest
+        row = pl.multiple_of(row, 8)
+        ge_ref[pl.ds(row, size), :] += ref[at : at + size, :]
+    gw_ref[...] = small[:TAPS]
+    gb_ref[...] = small[TAPS : TAPS + 1].reshape(width)
+    gs_ref[...] = small[TAPS + 1 : TAPS + 2].reshape(width)
 
 
 def in_vmem(*arrays):
@@ -612,17 +651,19 @@
             pltpu.VMEM((2 * per, 128), I32),
             pltpu.VMEM((160 * count, 128), BF16),
             pltpu.VMEM((160 * count, 128), BF16),
-        ),
+            pltpu.VMEM((128 * count, width), BF16),
+            pltpu.VMEM((128 * count, width), BF16),
+        )
+        + (pltpu.VMEM((d_rows // 2, width), F32),) * 4,
         in_specs=sm(2) + vm(6),
-        out_specs=vm(5),
+        out_specs=vm(11),
         scratch_shapes=[
             pltpu.VMEM((8 + per, 256), I32),
             pltpu.VMEM((12 * count, 128), F32),
         ]
-        + [pltpu.VMEM((d_rows, width), F32)] * 2
         + [pltpu.VMEM((vocab, chunks * 128), BF16)] * 2
-        + [pltpu.VMEM((chunks * 128, width), BF16)] * 4,
-        compiler_params=limit(34),
+        + [pltpu.VMEM((3 * (TABLE_BATCH + 1) * 128, width), BF16)] * 2,
+        compiler_params=limit(12),
         cost_estimate=cost(8 * 10**9, 2 * 10**7),
         name="table_grad",
     )(
@@ -631,14 +672,13 @@
     )
 
 
-def near_call(start, lengths, weights, id_chunks, e_high, e_low, conv_weight, bias, scorer, hl0, hl1, ct):
-    rows, half, width = ct.shape
-    count, chunks, per, d_rows = sizes(2 * half)
-    vocab = e_high.shape[0]
+def near_call(start, lengths, weights, id_chunks, e_high, e_low, conv_weight, bias, scorer, *grads):
+    count, chunks, per, d_rows = sizes(grads[0].shape[0] // 8)
+    vocab, width = e_high.shape
     return pl.pallas_call(
         near_kernel,
         out_shape=[pltpu.VMEM((8, width), F32)] + [pltpu.VMEM((chunks * 128, width), BF16)] * 4,
-        in_specs=sm(2) + vm(9) + [pl.BlockSpec(memory_space=pl.ANY)],
+        in_specs=sm(2) + vm(13),
         out_specs=vm(5),
         scratch_shapes=[
             pltpu.VMEM((6, 8 + per, 128), F32),
@@ -646,18 +686,13 @@
             pltpu.VMEM((8 * (TAPS + 1), width), F32),
         ]
         + [pltpu.VMEM((chunks * 128, vocab), BF16)] * 2
-        + [pltpu.VMEM((d_rows, width), F32)] * 2
-        + [
-            pltpu.VMEM((RING * 128, width), F32),
-            pltpu.VMEM(ct.shape, F32),
-            pltpu.SemaphoreType.DMA(()),
-        ],
-        compiler_params=limit(30),
+        + [pltpu.VMEM((RING * 128, width), F32)],
+        compiler_params=limit(12),
         cost_estimate=cost(16 * 10**9, 4 * 10**7),
         name="near",
     )(
         start, lengths, *in_vmem(weights, id_chunks, e_high, e_low),
-        *in_hbm(conv_weight, bias, scorer), *in_vmem(hl0, hl1), *in_hbm(ct),
+        *in_hbm(conv_weight, bias, scorer), *in_vmem(*grads),
     )
 
 
@@ -683,17 +718,22 @@
     return [(i, i ^ mask) for i in range(lax.axis_size(axis))]
 
 
-def part(v, index, size):
-    return lax.dynamic_slice_in_dim(v, index * size, size, 0)
-
-
-def scatter_sum(v, axis, low, bits):
-    group = 1 << bits
-    size = v.shape[0] // group
-    me = (lax.axis_index(axis) >> low) & (group - 1)
-    total = part(v, me, size)
-    for m in range(1, group):
-        total = total + lax.ppermute(part(v, me ^ m, size), axis, partners(axis, m << low))
+U32 = jnp.uint32
+
+
+def offsets(axis, low, bits, size):
+    me = (lax.axis_index(axis).astype(U32) >> low) & ((1 << bits) - 1)
+    return [(me ^ m) * U32(size) for m in range(1 << bits)]
+
+
+def part(v, at, size):
+    return lax.dynamic_slice(v, (at, U32(0)), (size, v.shape[1]))
+
+
+def scatter_sum(v, places, size, axis, low):
+    total = part(v, places[0], size)
+    for m in range(1, len(places)):
+        total = total + lax.ppermute(part(v, places[m], size), axis, partners(axis, m << low))
     return total
 
 
@@ -703,18 +743,8 @@
     )
 
 
-def gather_back(v, small, axis, low, bits):
-    group = 1 << bits
-    size = v.shape[0]
-    me = (lax.axis_index(axis) >> low) & (group - 1)
-    both = jnp.concatenate([v, small], axis=0)
-    out = jnp.zeros((group * size,) + v.shape[1:], v.dtype)
-    out = lax.dynamic_update_slice_in_dim(out, v, me * size, 0)
-    for m in range(1, group):
-        got = lax.ppermute(both, axis, partners(axis, m << low))
-        out = lax.dynamic_update_slice_in_dim(out, got[:size], (me ^ m) * size, 0)
-        small = small + got[size:]
-    return out, small
+def own_place(axis, low, bits):
+    return (lax.axis_index(axis) >> low) & ((1 << bits) - 1)
 
 
 def per_device(byte_ids, lengths, embedding, conv_weight, conv_bias, score_weight, cotangent):
@@ -724,47 +754,53 @@
     seq = lax.axis_size("seq")
     start = (lax.axis_index("seq") * span).reshape(1)
 
+    bits = seq.bit_length() - 1
+    groups = [("seq", low, min(2, bits - low)) for low in range(0, bits, 2)]
+    stages = [("dp", 0, lax.axis_size("dp").bit_length() - 1)] + groups[:-1]
+    parts, places = [], []
+    for axis, low, wide in stages:
+        parts.append((parts[-1] if parts else vocab) >> wide)
+        places.append(offsets(axis, low, wide, parts[-1]))
+    here = jnp.stack([own_place(*stage) for stage in stages])
+    byte_ids, start, here, places = lax.optimization_barrier((byte_ids, start, here, places))
     up = [(i, i + 1) for i in range(seq - 1)]
     left = lax.ppermute(byte_ids, "seq", up)
     right = lax.ppermute(byte_ids, "seq", [(j, i) for i, j in up])
     table_scores, e_high, e_low, ct = prep_call(
         embedding, conv_weight, conv_bias, score_weight, cotangent
     )
-    grad_table, weights, id_chunks, hl0, hl1 = table_call(
+    grad_table, weights, id_chunks, hl0, hl1, *grads = table_call(
         start, lengths, byte_ids, left, right, table_scores, conv_weight, ct
     )
     small, *kept = near_call(
         start, lengths, weights, id_chunks, e_high, e_low, conv_weight, conv_bias, score_weight,
-        hl0, hl1, cotangent,
+        *grads,
     )
     latent = latent_call(kept + [hl0, hl1], cotangent.shape)
 
-    bits = seq.bit_length() - 1
-    groups = [("seq", low, min(2, bits - low)) for low in range(0, bits, 2)]
-    stages = [("dp", 0, lax.axis_size("dp").bit_length() - 1)] + groups[:-1]
     total = grad_table
-    for stage in stages:
-        total = scatter_sum(total, *stage)
-    size = total.shape[0]
+    for (axis, low, bits), size, at in zip(stages, parts, places):
+        total = scatter_sum(total, at, size, axis, low)
     both = exchange_sum(jnp.concatenate([total, small], axis=0), *groups[-1])
     both, latent = lax.optimization_barrier((both, latent))
-    total, small = both[:size], both[size:]
-    for stage in reversed(stages):
-        total, small = gather_back(total, small, *stage)
+    for axis, low, wide in reversed(stages[1:]):
+        got = [lax.ppermute(both, axis, partners(axis, m << low)) for m in range(1, 1 << wide)]
+        both = jnp.concatenate([both] + got, axis=0)
+    theirs = lax.ppermute(both, "dp", partners("dp", 1))
 
     grad_e, grad_w, grad_b, grad_s = pl.pallas_call(
-        final_kernel,
+        functools.partial(final_kernel, stages),
         out_shape=(
             jax.ShapeDtypeStruct((vocab, width), F32),
             jax.ShapeDtypeStruct((TAPS, width), F32),
             jax.ShapeDtypeStruct((width,), F32),
             jax.ShapeDtypeStruct((width,), F32),
         ),
-        in_specs=vm(4),
+        in_specs=sm(1) + vm(4),
         out_specs=vm(4),
         compiler_params=limit(4),
         name="final",
-    )(*in_vmem(total, small), *in_hbm(conv_weight, score_weight))
+    )(here, *in_vmem(both, theirs), *in_hbm(conv_weight, score_weight))
     return latent, grad_e, grad_w, grad_b, grad_s
 
 

time: 77.9 us -> 75.1 us (0.964)
  Pallas kernels: 41.5 us -> 38.2 us
  local copies, waits for them, and re-layouts: 1.01 us -> 0.12 us
  waiting for transfers between devices: 13.7 us -> 14.5 us
    pallas_call x1, Pallas kernels: 20.3 us -> 16.5 us  [near_call(): pl.pallas_call(near_kernel, out_shape=[pltpu.VMEM((8, width), F32)] + [pl...]
    ppermute x8, waiting for transfers between devices: 8 us -> 9.12 us  [the longest x3 5.55 us: per_device(): lax.ppermute(both, axis, partners(axis, m << low))]
  transfers between devices with their start and end apart: 13 -> 13, of which waited for: 8 -> 5; matrix products, arithmetic and copies ran while one was open for 0% -> 0% of each run, Pallas kernels for 37% -> 33%
where the time goes in v3:
time: 75.1 us; the launch traced here: 74.6 us
  Pallas kernels  38.2 us (51%)
  starting transfers between devices  20.8 us (28%)
  waiting for transfers between devices  14.5 us (19%)
  between operations  0.83 us (1%)
    pallas_call x1, Pallas kernels, near_call(): pl.pallas_call(near_kernel, out_shape=[pltpu.VMEM((8, width), F32)] + [pl...  16.5 us
    pallas_call x1, Pallas kernels, table_call(): pl.pallas_call(table_kernel, out_shape=(pltpu.VMEM((vocab, width), F32),...  11.6 us
    ppermute x3, waiting for transfers between devices, per_device(): lax.ppermute(both, axis, partners(axis, m << low))  5.55 us
    ppermute x1, starting transfers between devices, per_device(): left = lax.ppermute(byte_ids, 'seq', up)  5.48 us
    ppermute x4, starting transfers between devices, scatter_sum(): lax.ppermute(part(v, places[m], size), axis, partners(axis, m << low))  5.47 us
    ppermute x3, waiting for transfers between devices, exchange_sum(): lax.ppermute(v, axis, partners(axis, m << low))  5.35 us
    ppermute x3, starting transfers between devices, exchange_sum(): lax.ppermute(v, axis, partners(axis, m << low))  4.85 us
    pallas_call x1, Pallas kernels, prep_call(): pl.pallas_call(prep_kernel, out_shape=(pltpu.VMEM((8, vocab), F32), pltpu...  4.12 us
  transfers between devices with their start and end apart: 13, of which 5 were waited for; matrix products, arithmetic and copies ran while one was open for 0% of the time, Pallas kernels for 33%

profile of v3, /device:TPU:0, one launch (start us, length us, event | category | flops | bytes accessed | tf_op | source)
XLA Modules:
  0.0 74.6 jit_solution(14170239688372736977)
XLA Ops:
  0.6 0.1 pad_add_fusion.place_ref
  0.7 1.4 %collective-permute-start.1 = (s32[16,256]{1,0:T(8,128)}, s32[16,256]{1,0:T(8,128)S(1)}, u32[]{:S(2)}, u32[]{:S(2)}) collective-permute-start(s32[16,256]{1,0:T(8,128)} %ids_ref), channel_id=1, source_target_pairs={{1,0},{2,1},{3,2},{4,3},{5,4},{6,5},{7,6},{8,7},{9,8},{10,9},{11,1... | collective-permute-start | bytes 49160 | tf_op jit(solution)/shard_map/ppermute | solution.py:768
  2.1 5.5 %collective-permute-start = (s32[16,256]{1,0:T(8,128)}, s32[16,256]{1,0:T(8,128)S(1)}, u32[]{:S(2)}, u32[]{:S(2)}) collective-permute-start(s32[16,256]{1,0:T(8,128)} %ids_ref), channel_id=1, source_target_pairs={{0,1},{1,2},{2,3},{3,4},{4,5},{5,6},{6,7},{7,8},{8,9},{9,10},{10,1... | collective-permute-start | bytes 49160 | tf_op jit(solution)/shard_map/ppermute | solution.py:767
  7.6 4.1 %prep.1 = (f32[8,256]{1,0:T(8,128)S(1)}, bf16[256,768]{1,0:T(8,128)(2,1)S(1)}, bf16[256,768]{1,0:T(8,128)(2,1)S(1)}, f32[16,128,768]{2,1,0:T(8,128)S(1)}) custom-call(f32[256,768]{1,0:T(8,128)} %e_ref.1, f32[4,768]{1,0:T(4,128)} %w_ref.7, f32[768]{0:T(1024)} %b_ref.3, f32[768]{0:T(1024)} %s_ref.5, f32[16,128,768]{2,1,0:T(8,128)} %ct_hbm.1), custom_call_target="tpu_custom_call" | custom-call | flops 100000000 | bytes 1000000 | tf_op jit(solution)/shard_map/prep/pallas_call | solution.py:625
  11.8 11.6 %table_grad.1 = (f32[256,768]{1,0:T(8,128)S(1)}, f32[8,32,128]{2,1,0:T(8,128)S(1)}, s32[48,128]{1,0:T(8,128)S(1)}, bf16[2560,128]{1,0:T(8,128)(2,1)S(1)}, bf16[2...) custom-call(s32[1]{0:T(128)} %bitcast.start_ref, ...), custom_call_target="tpu_custom_call" | custom-call | flops 8000000000 | bytes 20000000 | tf_op jit(solution)/shard_map/table_grad/pallas_call | solution.py:646
  23.4 0.1 collective-permute-start.2
  23.5 1.7 %collective-permute-done.2 = f32[128,768]{1,0:T(8,128)S(1)} collective-permute-done((f32[128,768]{1,0:T(8,128)S(1)}, f32[128,768]{1,0:T(8,128)S(1)}, u32[]{:S(2)}, u32[]{:S(2)}) %collective-permute-start.2) | collective-permute-done | bytes 393248 | tf_op jit(solution)/shard_map/ppermute | solution.py:736
  25.2 0.1 dynamic-slice_add_fusion
  25.3 3.0 %collective-permute-start.3 = (f32[32,768]{1,0:T(8,128)S(1)}, f32[32,768]{1,0:T(8,128)S(1)}, u32[]{:S(2)}, u32[]{:S(2)}) collective-permute-start(f32[32,768]{1,0:T(8,128)S(1)} %get-tuple-element.75), channel_id=1, source_target_pairs={{0,1},{1,0},{2,3},{3,2},{4,5},{5,4},{6,7},{7,6},{8,9},{9,8},{10,11... | collective-permute-start | bytes 294920 | tf_op jit(solution)/shard_map/ppermute | solution.py:736
  28.3 1.9 %collective-permute-start.5 = (f32[32,768]{1,0:T(8,128)S(1)}, f32[32,768]{1,0:T(8,128)S(1)}, u32[]{:S(2)}, u32[]{:S(2)}) collective-permute-start(f32[32,768]{1,0:T(8,128)S(1)} %get-tuple-element.76), channel_id=1, source_target_pairs={{0,3},{1,2},{2,1},{3,0},{4,7},{5,6},{6,5},{7,4},{8,11},{9,10},{10,... | collective-permute-start | bytes 294920 | tf_op jit(solution)/shard_map/ppermute | solution.py:736
  30.2 0.5 collective-permute-start.4
  30.7 16.5 %near.1 = (f32[8,768]{1,0:T(8,128)S(1)}, bf16[2176,768]{1,0:T(8,128)(2,1)S(1)}, bf16[2176,768]{1,0:T(8,128)(2,1)S(1)}, bf16[2176,768]{1,0:T(8,128)(2,1)S(1)}, bf16[2176,768]{1,0:T(8,128)(2,1)S(1)}) custom-call(s32[1]{0:T(128)} %bitcast.start_ref, s32[16]{0:T(128)S(1)} %copy-done, f32[8,32,128]{2,1,0:T(8,128)S(1)} %get-tuple-element.51.weights_ref, ...), custom_call_target="tpu_custom_call" | custom-call | flops 16000000000 | bytes 40000000 | tf_op jit(solution)/shard_map/near/pallas_call | solution.py:678
  47.3 4.2 %collective-permute-start.8 = (f32[40,768]{1,0:T(8,128)S(1)}, f32[40,768]{1,0:T(8,128)S(1)}, u32[]{:S(2)}, u32[]{:S(2)}) collective-permute-start(f32[40,768]{1,0:T(8,128)S(1)} %pad_maximum_fusion), channel_id=1, source_target_pairs={{0,12},{1,13},{2,14},{3,15},{4,8},{5,9},{6,10},{7,11},{8,4},{9,5},... | collective-permute-start | bytes 368648 | tf_op jit(solution)/shard_map/ppermute | solution.py:742
  51.5 0.6 collective-permute-start.6
  52.2 3.8 %latent.1 = f32[16,128,768]{2,1,0:T(8,128)} custom-call(bf16[2176,768]{1,0:T(8,128)(2,1)S(1)} %get-tuple-element.62.high0, bf16[2176,768]{1,0:T(8,128)(2,1)S(1)} %get-tuple-element.63.low0, bf16[2176,768]{1,0:T(8,128)(2,1)S(1)} %get-tuple-element.64.high1, bf16[2176,768]{1,0:T(8,128)(2,1)S(1)} %get-tuple-element.65.low1, ...), custom_call_target="tpu_custom_call" | custom-call | flops 4000000000 | bytes 10000000 | tf_op jit(solution)/shard_map/latent/pallas_call | solution.py:702
  56.0 5.3 %collective-permute-done.7 = f32[40,768]{1,0:T(8,128)S(1)} collective-permute-done((f32[40,768]{1,0:T(8,128)S(1)}, f32[40,768]{1,0:T(8,128)S(1)}, u32[]{:S(2)}, u32[]{:S(2)}) %collective-permute-start.7) | collective-permute-done | bytes 122912 | tf_op jit(solution)/shard_map/ppermute | solution.py:742
  61.4 1.3 %collective-permute-start.9 = (f32[40,768]{1,0:T(8,128)S(1)}, f32[40,768]{1,0:T(8,128)S(1)}, u32[]{:S(2)}, u32[]{:S(2)}) collective-permute-start(f32[40,768]{1,0:T(8,128)S(1)} %add_add_fusion), channel_id=1, source_target_pairs={{0,1},{1,0},{2,3},{3,2},{4,5},{5,4},{6,7},{7,6},{8,9},{9,8},{10,11... | collective-permute-start | bytes 368648 | tf_op jit(solution)/shard_map/ppermute | solution.py:787
  62.7 1.5 %collective-permute-start.11 = (f32[40,768]{1,0:T(8,128)S(1)}, f32[40,768]{1,0:T(8,128)S(1)}, u32[]{:S(2)}, u32[]{:S(2)}) collective-permute-start(f32[40,768]{1,0:T(8,128)S(1)} %add_add_fusion), channel_id=1, source_target_pairs={{0,3},{1,2},{2,1},{3,0},{4,7},{5,6},{6,5},{7,4},{8,11},{9,10},{10,... | collective-permute-start | bytes 368648 | tf_op jit(solution)/shard_map/ppermute | solution.py:787
  64.2 0.8 %collective-permute-start.10 = (f32[40,768]{1,0:T(8,128)S(1)}, f32[40,768]{1,0:T(8,128)S(1)}, u32[]{:S(2)}, u32[]{:S(2)}) collective-permute-start(f32[40,768]{1,0:T(8,128)S(1)} %add_add_fusion), channel_id=1, source_target_pairs={{0,2},{1,3},{2,0},{3,1},{4,6},{5,7},{6,4},{7,5},{8,10},{9,11},{10,... | collective-permute-start | bytes 368648 | tf_op jit(solution)/shard_map/ppermute | solution.py:787
  65.0 2.4 %collective-permute-done.9 = f32[40,768]{1,0:T(8,128)S(1)} collective-permute-done((f32[40,768]{1,0:T(8,128)S(1)}, f32[40,768]{1,0:T(8,128)S(1)}, u32[]{:S(2)}, u32[]{:S(2)}) %collective-permute-start.9) | collective-permute-done | bytes 122912 | tf_op jit(solution)/shard_map/ppermute | solution.py:787
  67.4 3.2 %collective-permute-done.10 = f32[40,768]{1,0:T(8,128)S(1)} collective-permute-done((f32[40,768]{1,0:T(8,128)S(1)}, f32[40,768]{1,0:T(8,128)S(1)}, u32[]{:S(2)}, u32[]{:S(2)}) %collective-permute-start.10) | collective-permute-done | bytes 122912 | tf_op jit(solution)/shard_map/ppermute | solution.py:787
  70.6 0.1 collective-permute-start.12
  70.7 1.9 %collective-permute-done.12.theirs_ref = f32[160,768]{1,0:T(8,128)S(1)} collective-permute-done((f32[160,768]{1,0:T(8,128)S(1)}, f32[160,768]{1,0:T(8,128)S(1)}, u32[]{:S(2)}, u32[]{:S(2)}) %collective-permute-start.12) | collective-permute-done | bytes 491552 | tf_op jit(solution)/shard_map/ppermute | solution.py:789
  72.5 2.1 %final.1 = (f32[256,768]{1,0:T(8,128)}, f32[4,768]{1,0:T(4,128)}, f32[768]{0:T(1024)}, f32[768]{0:T(1024)}) custom-call(s32[2]{0:T(128)S(1)} %pad_add_fusion.place_ref, f32[160,768]{1,0:T(8,128)S(1)} %constant_dynamic-update-slice_fusion.mine_ref, f32[160,768]{1,0:T(8,128)S(1)} %collective-permute-done.12.theirs_ref, f32[4,768]{1,0:T(4,128)} %w_ref.7, f32[768]{0:T(1024)} %s_ref.5), custom_call_target="tpu_custom_call" | custom-call | tf_op jit(solution)/shard_map/final/pallas_call | solution.py:791
  (20 shorter events, 0.2 us)
Async XLA Ops:
  0.7 11.1 %copy-start = (s32[16]{0:T(128)S(1)}, s32[16]{0:T(128)}, u32[]{:S(2)}) copy-start(s32[16]{0:T(128)} %len_ref.3) | copy-start | bytes 196
  0.7 11.0 %collective-permute-start.1 = (s32[16,256]{1,0:T(8,128)}, s32[16,256]{1,0:T(8,128)S(1)}, u32[]{:S(2)}, u32[]{:S(2)}) collective-permute-start(s32[16,256]{1,0:T(8,128)} %ids_ref), channel_id=1, source_target_pairs={{1,0},{2,1},{3,2},{4,3},{5,4},{6,5},{7,6},{8,7},{9,8},{10,9},{11,1... | collective-permute-start | bytes 49160 | tf_op jit(solution)/shard_map/ppermute | solution.py:768
  2.1 9.6 %collective-permute-start = (s32[16,256]{1,0:T(8,128)}, s32[16,256]{1,0:T(8,128)S(1)}, u32[]{:S(2)}, u32[]{:S(2)}) collective-permute-start(s32[16,256]{1,0:T(8,128)} %ids_ref), channel_id=1, source_target_pairs={{0,1},{1,2},{2,3},{3,4},{4,5},{5,6},{6,7},{7,8},{8,9},{9,10},{10,1... | collective-permute-start | bytes 49160 | tf_op jit(solution)/shard_map/ppermute | solution.py:767
  23.4 1.8 %collective-permute-start.2 = (f32[128,768]{1,0:T(8,128)S(1)}, f32[128,768]{1,0:T(8,128)S(1)}, u32[]{:S(2)}, u32[]{:S(2)}) collective-permute-start(f32[128,768]{1,0:T(8,128)S(1)} %constant_dynamic-slice_fusion.3), channel_id=1, source_target_pairs={{0,16},{16,0},{1,17},{17,1},{2,18},{18,2},{3,19},{19,3},{4,20},{20... | collective-permute-start | bytes 1179656 | tf_op jit(solution)/shard_map/ppermute | solution.py:736
  25.3 21.9 %collective-permute-start.3 = (f32[32,768]{1,0:T(8,128)S(1)}, f32[32,768]{1,0:T(8,128)S(1)}, u32[]{:S(2)}, u32[]{:S(2)}) collective-permute-start(f32[32,768]{1,0:T(8,128)S(1)} %get-tuple-element.75), channel_id=1, source_target_pairs={{0,1},{1,0},{2,3},{3,2},{4,5},{5,4},{6,7},{7,6},{8,9},{9,8},{10,11... | collective-permute-start | bytes 294920 | tf_op jit(solution)/shard_map/ppermute | solution.py:736
  28.3 19.0 %collective-permute-start.5 = (f32[32,768]{1,0:T(8,128)S(1)}, f32[32,768]{1,0:T(8,128)S(1)}, u32[]{:S(2)}, u32[]{:S(2)}) collective-permute-start(f32[32,768]{1,0:T(8,128)S(1)} %get-tuple-element.76), channel_id=1, source_target_pairs={{0,3},{1,2},{2,1},{3,0},{4,7},{5,6},{6,5},{7,4},{8,11},{9,10},{10,... | collective-permute-start | bytes 294920 | tf_op jit(solution)/shard_map/ppermute | solution.py:736
  30.2 17.1 %collective-permute-start.4 = (f32[32,768]{1,0:T(8,128)S(1)}, f32[32,768]{1,0:T(8,128)S(1)}, u32[]{:S(2)}, u32[]{:S(2)}) collective-permute-start(f32[32,768]{1,0:T(8,128)S(1)} %get-tuple-element.77), channel_id=1, source_target_pairs={{0,2},{1,3},{2,0},{3,1},{4,6},{5,7},{6,4},{7,5},{8,10},{9,11},{10,... | collective-permute-start | bytes 294920 | tf_op jit(solution)/shard_map/ppermute | solution.py:736
  47.3 8.7 %collective-permute-start.8 = (f32[40,768]{1,0:T(8,128)S(1)}, f32[40,768]{1,0:T(8,128)S(1)}, u32[]{:S(2)}, u32[]{:S(2)}) collective-permute-start(f32[40,768]{1,0:T(8,128)S(1)} %pad_maximum_fusion), channel_id=1, source_target_pairs={{0,12},{1,13},{2,14},{3,15},{4,8},{5,9},{6,10},{7,11},{8,4},{9,5},... | collective-permute-start | bytes 368648 | tf_op jit(solution)/shard_map/ppermute | solution.py:742
  51.5 9.8 %collective-permute-start.7 = (f32[40,768]{1,0:T(8,128)S(1)}, f32[40,768]{1,0:T(8,128)S(1)}, u32[]{:S(2)}, u32[]{:S(2)}) collective-permute-start(f32[40,768]{1,0:T(8,128)S(1)} %pad_maximum_fusion), channel_id=1, source_target_pairs={{0,8},{1,9},{2,10},{3,11},{4,12},{5,13},{6,14},{7,15},{8,0},{9,1},... | collective-permute-start | bytes 368648 | tf_op jit(solution)/shard_map/ppermute | solution.py:742
  51.5 9.8 %collective-permute-start.6 = (f32[40,768]{1,0:T(8,128)S(1)}, f32[40,768]{1,0:T(8,128)S(1)}, u32[]{:S(2)}, u32[]{:S(2)}) collective-permute-start(f32[40,768]{1,0:T(8,128)S(1)} %pad_maximum_fusion), channel_id=1, source_target_pairs={{0,4},{1,5},{2,6},{3,7},{4,0},{5,1},{6,2},{7,3},{8,12},{9,13},{10,... | collective-permute-start | bytes 368648 | tf_op jit(solution)/shard_map/ppermute | solution.py:742
  61.4 6.0 %collective-permute-start.9 = (f32[40,768]{1,0:T(8,128)S(1)}, f32[40,768]{1,0:T(8,128)S(1)}, u32[]{:S(2)}, u32[]{:S(2)}) collective-permute-start(f32[40,768]{1,0:T(8,128)S(1)} %add_add_fusion), channel_id=1, source_target_pairs={{0,1},{1,0},{2,3},{3,2},{4,5},{5,4},{6,7},{7,6},{8,9},{9,8},{10,11... | collective-permute-start | bytes 368648 | tf_op jit(solution)/shard_map/ppermute | solution.py:787
  62.7 7.9 %collective-permute-start.11 = (f32[40,768]{1,0:T(8,128)S(1)}, f32[40,768]{1,0:T(8,128)S(1)}, u32[]{:S(2)}, u32[]{:S(2)}) collective-permute-start(f32[40,768]{1,0:T(8,128)S(1)} %add_add_fusion), channel_id=1, source_target_pairs={{0,3},{1,2},{2,1},{3,0},{4,7},{5,6},{6,5},{7,4},{8,11},{9,10},{10,... | collective-permute-start | bytes 368648 | tf_op jit(solution)/shard_map/ppermute | solution.py:787
  64.2 6.3 %collective-permute-start.10 = (f32[40,768]{1,0:T(8,128)S(1)}, f32[40,768]{1,0:T(8,128)S(1)}, u32[]{:S(2)}, u32[]{:S(2)}) collective-permute-start(f32[40,768]{1,0:T(8,128)S(1)} %add_add_fusion), channel_id=1, source_target_pairs={{0,2},{1,3},{2,0},{3,1},{4,6},{5,7},{6,4},{7,5},{8,10},{9,11},{10,... | collective-permute-start | bytes 368648 | tf_op jit(solution)/shard_map/ppermute | solution.py:787
  70.6 1.9 %collective-permute-start.12 = (f32[160,768]{1,0:T(8,128)S(1)}, f32[160,768]{1,0:T(8,128)S(1)}, u32[]{:S(2)}, u32[]{:S(2)}) collective-permute-start(f32[160,768]{1,0:T(8,128)S(1)} %constant_dynamic-update-slice_fusion.mine_ref), channel_id=1, source_target_pairs={{0,16},{16,0},{1,17},{17,1},{2,18},{18,2},{3,19},{19,3},{4,20},{20... | collective-permute-start | bytes 1474568 | tf_op jit(solution)/shard_map/ppermute | solution.py:789

commit v4 on v3

--- a/solution.py
+++ b/solution.py
@@ -83,9 +83,23 @@
     return jnp.where(lane < 32, pltpu.roll(y, 1, 0), y)[8:]
 
 
-def prep_kernel(e_ref, w_ref, b_ref, s_ref, ct_hbm, t_ref, high_ref, low_ref, ct_ref, sem):
-    copy = pltpu.make_async_copy(ct_hbm, ct_ref, sem)
-    copy.start()
+def prep_kernel(
+    start_hbm, len_hbm, ids_hbm, e_hbm, w_hbm, b_hbm, s_hbm, ct_hbm,
+    t_ref, high_ref, low_ref, even_ref, length_ref, ids_ref, w_ref, b_ref, s_ref, ct_ref,
+    start_ref, len_ref, e_ref, sems,
+):
+    pairs = [
+        (w_hbm, w_ref), (b_hbm, b_ref), (s_hbm, s_ref), (e_hbm, e_ref),
+        (start_hbm, start_ref), (len_hbm, len_ref), (ids_hbm, ids_ref),
+    ]
+    copies = [pltpu.make_async_copy(a, b, sems.at[i]) for i, (a, b) in enumerate(pairs)]
+    for r in range(0, ROWS, 2):
+        rows = pl.ds(r, 2)
+        copies.append(pltpu.make_async_copy(ct_hbm.at[rows], ct_ref.at[rows], sems.at[len(copies)]))
+    for copy in copies:
+        copy.start()
+    for copy in copies[:4]:
+        copy.wait()
     scaled = w_ref[...] * line(s_ref)
     wide = jnp.concatenate([scaled, jnp.zeros_like(scaled)], axis=0)
     t = lax.dot_general(wide, e_ref[...], NT, precision=HIGH, preferred_element_type=F32)
@@ -93,7 +107,9 @@
     row = lax.broadcasted_iota(I32, t.shape, 0)
     t_ref[...] = jnp.where(row == TAPS, b0, t)
     high_ref[...], low_ref[...] = split(e_ref[...])
-    copy.wait()
+    for copy in copies[4:]:
+        copy.wait()
+    even_ref[...], length_ref[...] = geometry(even_ref.shape, start_ref[0], len_ref)
 
 
 def regroup(ids_ref, ids_scr, first, windows):
@@ -117,10 +133,9 @@
             ids_scr[at : at + len(some), g * 128 : g * 128 + 128] = out[: len(some)]
 
 
-def weigh(start, len_ref, ids_scr, t_ref):
+def weigh(even, length, ids_scr, t_ref):
     shape = (ids_scr.shape[0], 128)
     lane = lanes(shape)
-    even, length = geometry(shape, start, len_ref)
     live = [alive(even, length), alive(even + 1, length)]
     ids, terms = [], []
     for e in range(2):
@@ -156,7 +171,7 @@
         parts = [jnp.exp(s - top) for s in scores]
         norm = sum(parts)
         weights.append([p / norm for p in parts])
-    return ids, weights, even, length
+    return ids, weights
 
 
 def spread(values, even):
@@ -256,7 +271,7 @@
 
 
 def table_kernel(
-    start_ref, len_ref, ids_ref, left_ref, right_ref, t_ref, w_ref, ct_ref,
+    even_ref, length_ref, ids_ref, left_ref, right_ref, t_ref, w_ref, ct_ref,
     grad_ref, weights_ref, chunks_ref, hl0, hl1, both0, both1, d00, d01, d10, d11,
     ids_scr, bands_ref, *scratch,
 ):
@@ -267,12 +282,12 @@
     count = ids_ref.shape[1] // 16
     chunks = count + 1
     vocab = t_ref.shape[1]
-    start = start_ref[0]
+    even, length = even_ref[...], length_ref[...]
     ids_scr[...] = jnp.zeros_like(ids_scr)
     regroup(left_ref, ids_scr, 7, [count - 1])
     regroup(ids_ref, ids_scr, 8, list(range(count)))
     regroup(right_ref, ids_scr, 8 + count, [0])
-    ids, weights, even, length = weigh(start, len_ref, ids_scr, t_ref)
+    ids, weights = weigh(even, length, ids_scr, t_ref)
     for e in range(2):
         for b in range(4):
             weights_ref[e * 4 + b] = weights[e][b]
@@ -353,7 +368,7 @@
 
 
 def near_kernel(
-    start_ref, len_ref, weights_ref, chunks_ref, e_high, e_low, w_ref, b_ref, s_ref, both0, both1, d00, d01, d10, d11,
+    even_ref, length_ref, weights_ref, chunks_ref, e_high, e_low, w_ref, b_ref, s_ref, both0, both1, d00, d01, d10, d11,
     small_ref, high0, low0, high1, low1,
     near_ref, q_ref, sums_ref, oh0, oh1, x_ref,
 ):
@@ -364,7 +379,6 @@
     count = both0.shape[0] // 128
     chunks = count + 1
     vocab, width = e_high.shape
-    start = start_ref[0]
     per = chunks_ref.shape[0] // 2
     small_ref[...] = jnp.zeros_like(small_ref)
     near_ref[...] = jnp.zeros_like(near_ref)
@@ -472,7 +486,7 @@
         total = jnp.sum(sums_ref[8 * k : 8 * k + 8, :], axis=0, keepdims=True)
         to = (k + TAPS) % (TAPS + 1)
         small_ref[to : to + 1, :] = total
-    even, length = geometry((padded, 128), start, len_ref)
+    even, length = even_ref[...], length_ref[...]
     weights = [[weights_ref[e * 4 + b] for b in range(4)] for e in range(2)]
     near = {}
     for i, r in enumerate(RELS):
@@ -620,26 +634,38 @@
     return count, chunks, per, (span + 16) * 8
 
 
-def prep_call(*params):
-    vocab, width = params[0].shape
+def prep_call(start, lengths, ids, embedding, conv_weight, bias, scorer, cotangent):
+    vocab, width = embedding.shape
+    count, chunks, per, d_rows = sizes(ids.shape[1])
     return pl.pallas_call(
         prep_kernel,
         out_shape=(
             pltpu.VMEM((8, vocab), F32),
             pltpu.VMEM((vocab, width), BF16),
             pltpu.VMEM((vocab, width), BF16),
-            pltpu.VMEM(params[-1].shape, F32),
+            pltpu.VMEM((8 + per, 128), I32),
+            pltpu.VMEM((8 + per, 128), I32),
+            pltpu.VMEM(ids.shape, I32),
+            pltpu.VMEM(conv_weight.shape, F32),
+            pltpu.VMEM(bias.shape, F32),
+            pltpu.VMEM(scorer.shape, F32),
+            pltpu.VMEM(cotangent.shape, F32),
         ),
-        in_specs=vm(4) + [pl.BlockSpec(memory_space=pl.ANY)],
-        out_specs=vm(4),
-        scratch_shapes=[pltpu.SemaphoreType.DMA(())],
+        in_specs=[pl.BlockSpec(memory_space=pl.ANY)] * 8,
+        out_specs=vm(10),
+        scratch_shapes=[
+            pltpu.SMEM((1,), I32),
+            pltpu.SMEM(lengths.shape, I32),
+            pltpu.VMEM((vocab, width), F32),
+            pltpu.SemaphoreType.DMA((7 + ROWS // 2,)),
+        ],
         compiler_params=limit(4),
         cost_estimate=cost(10**8, 10**6),
         name="prep",
-    )(*in_hbm(*params))
-
-
-def table_call(start, lengths, ids, left, right, table_scores, conv_weight, cotangent):
+    )(*in_hbm(start, lengths, ids, embedding, conv_weight, bias, scorer, cotangent))
+
+
+def table_call(even, length, ids, left, right, table_scores, conv_weight, cotangent):
     rows, half, width = cotangent.shape
     count, chunks, per, d_rows = sizes(2 * half)
     vocab = table_scores.shape[1]
@@ -655,7 +681,7 @@
             pltpu.VMEM((128 * count, width), BF16),
         )
         + (pltpu.VMEM((d_rows // 2, width), F32),) * 4,
-        in_specs=sm(2) + vm(6),
+        in_specs=vm(8),
         out_specs=vm(11),
         scratch_shapes=[
             pltpu.VMEM((8 + per, 256), I32),
@@ -666,19 +692,16 @@
         compiler_params=limit(12),
         cost_estimate=cost(8 * 10**9, 2 * 10**7),
         name="table_grad",
-    )(
-        start, lengths, *in_hbm(ids), *in_vmem(left, right, table_scores),
-        *in_hbm(conv_weight), *in_vmem(cotangent),
-    )
-
-
-def near_call(start, lengths, weights, id_chunks, e_high, e_low, conv_weight, bias, scorer, *grads):
+    )(*in_vmem(even, length, ids, left, right, table_scores, conv_weight, cotangent))
+
+
+def near_call(even, length, weights, id_chunks, e_high, e_low, conv_weight, bias, scorer, *grads):
     count, chunks, per, d_rows = sizes(grads[0].shape[0] // 8)
     vocab, width = e_high.shape
     return pl.pallas_call(
         near_kernel,
         out_shape=[pltpu.VMEM((8, width), F32)] + [pltpu.VMEM((chunks * 128, width), BF16)] * 4,
-        in_specs=sm(2) + vm(13),
+        in_specs=vm(15),
         out_specs=vm(5),
         scratch_shapes=[
             pltpu.VMEM((6, 8 + per, 128), F32),
@@ -690,10 +713,7 @@
         compiler_params=limit(12),
         cost_estimate=cost(16 * 10**9, 4 * 10**7),
         name="near",
-    )(
-        start, lengths, *in_vmem(weights, id_chunks, e_high, e_low),
-        *in_hbm(conv_weight, bias, scorer), *in_vmem(*grads),
-    )
+    )(*in_vmem(even, length, weights, id_chunks, e_high, e_low, conv_weight, bias, scorer, *grads))
 
 
 def latent_call(kept, shape):
@@ -766,15 +786,14 @@
     up = [(i, i + 1) for i in range(seq - 1)]
     left = lax.ppermute(byte_ids, "seq", up)
     right = lax.ppermute(byte_ids, "seq", [(j, i) for i, j in up])
-    table_scores, e_high, e_low, ct = prep_call(
-        embedding, conv_weight, conv_bias, score_weight, cotangent
+    table_scores, e_high, e_low, even, length, ids, taps, bias, scorer, ct = prep_call(
+        start, lengths, byte_ids, embedding, conv_weight, conv_bias, score_weight, cotangent
     )
     grad_table, weights, id_chunks, hl0, hl1, *grads = table_call(
-        start, lengths, byte_ids, left, right, table_scores, conv_weight, ct
+        even, length, ids, left, right, table_scores, taps, ct
     )
     small, *kept = near_call(
-        start, lengths, weights, id_chunks, e_high, e_low, conv_weight, conv_bias, score_weight,
-        *grads,
+        even, length, weights, id_chunks, e_high, e_low, taps, bias, scorer, *grads
     )
     latent = latent_call(kept + [hl0, hl1], cotangent.shape)
 
@@ -800,7 +819,7 @@
         out_specs=vm(4),
         compiler_params=limit(4),
         name="final",
-    )(here, *in_vmem(both, theirs), *in_hbm(conv_weight, score_weight))
+    )(here, *in_vmem(both, theirs, taps, scorer))
     return latent, grad_e, grad_w, grad_b, grad_s
 
 

time: 75.1 us -> 72.8 us (0.969)
  Pallas kernels: 38.2 us -> 36.2 us
  waiting for transfers between devices: 14.5 us -> 13.6 us
  starting transfers between devices: 20.8 us -> 21.6 us
    ppermute x3, starting transfers between devices: 4.85 us -> 5.76 us  [exchange_sum(): lax.ppermute(v, axis, partners(axis, m << low))]
    ppermute x3, waiting for transfers between devices: 5.55 us -> 4.65 us  [per_device(): lax.ppermute(both, axis, partners(axis, m << low))]
    pallas_call x1, Pallas kernels: 4.12 us -> 3.24 us  [prep_call(): pl.pallas_call(prep_kernel, out_shape=(pltpu.VMEM((8, vocab), F32), pltpu...]
  transfers between devices with their start and end apart: 13 -> 13, of which waited for: 5 -> 5; matrix products, arithmetic and copies ran while one was open for 0% -> 0% of each run, Pallas kernels for 33% -> 32%
where the time goes in v4:
time: 72.8 us; the launch traced here: 72.6 us
  Pallas kernels  36.2 us (50%)
  starting transfers between devices  21.6 us (30%)
  waiting for transfers between devices  13.6 us (19%)
  between operations  0.82 us (1%)
    pallas_call x1, Pallas kernels, near_call(): pl.pallas_call(near_kernel, out_shape=[pltpu.VMEM((8, width), F32)] + [pl...  16.2 us
    pallas_call x1, Pallas kernels, table_call(): pl.pallas_call(table_kernel, out_shape=(pltpu.VMEM((vocab, width), F32),...  11 us
    ppermute x3, starting transfers between devices, exchange_sum(): lax.ppermute(v, axis, partners(axis, m << low))  5.76 us
    ppermute x1, starting transfers between devices, per_device(): left = lax.ppermute(byte_ids, 'seq', up)  5.48 us
    ppermute x4, starting transfers between devices, scatter_sum(): lax.ppermute(part(v, places[m], size), axis, partners(axis, m << low))  5.47 us
    ppermute x3, waiting for transfers between devices, exchange_sum(): lax.ppermute(v, axis, partners(axis, m << low))  5.34 us
    ppermute x3, waiting for transfers between devices, per_device(): lax.ppermute(both, axis, partners(axis, m << low))  4.65 us
    pallas_call x1, Pallas kernels, latent_call(): pl.pallas_call(latent_kernel, out_shape=jax.ShapeDtypeStruct(shape, F32),...  3.83 us
  transfers between devices with their start and end apart: 13, of which 5 were waited for; matrix products, arithmetic and copies ran while one was open for 0% of the time, Pallas kernels for 32%

profile of v4, /device:TPU:0, one launch (start us, length us, event | category | flops | bytes accessed | tf_op | source)
XLA Modules:
  0.0 72.6 jit_solution(9200865765097787038)
XLA Ops:
  0.6 0.1 pad_add_fusion.place_ref
  0.7 1.3 %collective-permute-start.1 = (s32[16,256]{1,0:T(8,128)}, s32[16,256]{1,0:T(8,128)S(1)}, u32[]{:S(2)}, u32[]{:S(2)}) collective-permute-start(s32[16,256]{1,0:T(8,128)} %ids_hbm), channel_id=1, source_target_pairs={{1,0},{2,1},{3,2},{4,3},{5,4},{6,5},{7,6},{8,7},{9,8},{10,9},{11,1... | collective-permute-start | bytes 49160 | tf_op jit(solution)/shard_map/ppermute | solution.py:788
  2.0 5.5 %collective-permute-start = (s32[16,256]{1,0:T(8,128)}, s32[16,256]{1,0:T(8,128)S(1)}, u32[]{:S(2)}, u32[]{:S(2)}) collective-permute-start(s32[16,256]{1,0:T(8,128)} %ids_hbm), channel_id=1, source_target_pairs={{0,1},{1,2},{2,3},{3,4},{4,5},{5,6},{6,7},{7,8},{8,9},{9,10},{10,1... | collective-permute-start | bytes 49160 | tf_op jit(solution)/shard_map/ppermute | solution.py:787
  7.5 3.2 %prep.1 = (f32[8,256]{1,0:T(8,128)S(1)}, bf16[256,768]{1,0:T(8,128)(2,1)S(1)}, bf16[256,768]{1,0:T(8,128)(2,1)S(1)}, s32[32,128]{1,0:T(8,128)S(1)}, s32[32,128]{...) custom-call(s32[1]{0:T(128)} %bitcast.start_hbm, ...), custom_call_target="tpu_custom_call" | custom-call | flops 100000000 | bytes 1000000 | tf_op jit(solution)/shard_map/prep/pallas_call | solution.py:640
  10.8 11.0 %table_grad.1 = (f32[256,768]{1,0:T(8,128)S(1)}, f32[8,32,128]{2,1,0:T(8,128)S(1)}, s32[48,128]{1,0:T(8,128)S(1)}, bf16[2560,128]{1,0:T(8,128)(2,1)S(1)}, bf16[2...) custom-call(s32[32,128]{1,0:T(8,128)S(1)} %get-tuple-element.48.even, ...), custom_call_target="tpu_custom_call" | custom-call | flops 8000000000 | bytes 20000000 | tf_op jit(solution)/shard_map/table_grad/pallas_call | solution.py:672
  21.8 0.1 collective-permute-start.2
  21.9 1.7 %collective-permute-done.2 = f32[128,768]{1,0:T(8,128)S(1)} collective-permute-done((f32[128,768]{1,0:T(8,128)S(1)}, f32[128,768]{1,0:T(8,128)S(1)}, u32[]{:S(2)}, u32[]{:S(2)}) %collective-permute-start.2) | collective-permute-done | bytes 393248 | tf_op jit(solution)/shard_map/ppermute | solution.py:756
  23.6 0.1 dynamic-slice_add_fusion
  23.7 3.0 %collective-permute-start.3 = (f32[32,768]{1,0:T(8,128)S(1)}, f32[32,768]{1,0:T(8,128)S(1)}, u32[]{:S(2)}, u32[]{:S(2)}) collective-permute-start(f32[32,768]{1,0:T(8,128)S(1)} %get-tuple-element.87), channel_id=1, source_target_pairs={{0,1},{1,0},{2,3},{3,2},{4,5},{5,4},{6,7},{7,6},{8,9},{9,8},{10,11... | collective-permute-start | bytes 294920 | tf_op jit(solution)/shard_map/ppermute | solution.py:756
  26.7 1.9 %collective-permute-start.5 = (f32[32,768]{1,0:T(8,128)S(1)}, f32[32,768]{1,0:T(8,128)S(1)}, u32[]{:S(2)}, u32[]{:S(2)}) collective-permute-start(f32[32,768]{1,0:T(8,128)S(1)} %get-tuple-element.88), channel_id=1, source_target_pairs={{0,3},{1,2},{2,1},{3,0},{4,7},{5,6},{6,5},{7,4},{8,11},{9,10},{10,... | collective-permute-start | bytes 294920 | tf_op jit(solution)/shard_map/ppermute | solution.py:756
  28.6 0.5 collective-permute-start.4
  29.1 16.2 %near.1 = (f32[8,768]{1,0:T(8,128)S(1)}, bf16[2176,768]{1,0:T(8,128)(2,1)S(1)}, bf16[2176,768]{1,0:T(8,128)(2,1)S(1)}, bf16[2176,768]{1,0:T(8,128)(2,1)S(1)}, bf16[2176,768]{1,0:T(8,128)(2,1)S(1)}) custom-call(s32[32,128]{1,0:T(8,128)S(1)} %get-tuple-element.48.even_ref, s32[32,128]{1,0:T(8,128)S(1)} %get-tuple-element.49.length_ref, ...), custom_call_target="tpu_custom_call" | custom-call | flops 16000000000 | bytes 40000000 | tf_op jit(solution)/shard_map/near/pallas_call | solution.py:701
  45.4 5.1 %collective-permute-start.8 = (f32[40,768]{1,0:T(8,128)S(1)}, f32[40,768]{1,0:T(8,128)S(1)}, u32[]{:S(2)}, u32[]{:S(2)}) collective-permute-start(f32[40,768]{1,0:T(8,128)S(1)} %pad_maximum_fusion), channel_id=1, source_target_pairs={{0,12},{1,13},{2,14},{3,15},{4,8},{5,9},{6,10},{7,11},{8,4},{9,5},... | collective-permute-start | bytes 368648 | tf_op jit(solution)/shard_map/ppermute | solution.py:762
  50.5 0.6 collective-permute-start.6
  51.2 3.8 %latent.1 = f32[16,128,768]{2,1,0:T(8,128)} custom-call(bf16[2176,768]{1,0:T(8,128)(2,1)S(1)} %get-tuple-element.74.high0, bf16[2176,768]{1,0:T(8,128)(2,1)S(1)} %get-tuple-element.75.low0, bf16[2176,768]{1,0:T(8,128)(2,1)S(1)} %get-tuple-element.76.high1, bf16[2176,768]{1,0:T(8,128)(2,1)S(1)} %get-tuple-element.77.low1, ...), custom_call_target="tpu_custom_call" | custom-call | flops 4000000000 | bytes 10000000 | tf_op jit(solution)/shard_map/latent/pallas_call | solution.py:722
  55.0 5.3 %collective-permute-done.7 = f32[40,768]{1,0:T(8,128)S(1)} collective-permute-done((f32[40,768]{1,0:T(8,128)S(1)}, f32[40,768]{1,0:T(8,128)S(1)}, u32[]{:S(2)}, u32[]{:S(2)}) %collective-permute-start.7) | collective-permute-done | bytes 122912 | tf_op jit(solution)/shard_map/ppermute | solution.py:762
  60.4 0.4 collective-permute-start.9
  60.8 1.5 %collective-permute-start.11 = (f32[40,768]{1,0:T(8,128)S(1)}, f32[40,768]{1,0:T(8,128)S(1)}, u32[]{:S(2)}, u32[]{:S(2)}) collective-permute-start(f32[40,768]{1,0:T(8,128)S(1)} %add_add_fusion), channel_id=1, source_target_pairs={{0,3},{1,2},{2,1},{3,0},{4,7},{5,6},{6,5},{7,4},{8,11},{9,10},{10,... | collective-permute-start | bytes 368648 | tf_op jit(solution)/shard_map/ppermute | solution.py:806
  62.3 1.7 %collective-permute-start.10 = (f32[40,768]{1,0:T(8,128)S(1)}, f32[40,768]{1,0:T(8,128)S(1)}, u32[]{:S(2)}, u32[]{:S(2)}) collective-permute-start(f32[40,768]{1,0:T(8,128)S(1)} %add_add_fusion), channel_id=1, source_target_pairs={{0,2},{1,3},{2,0},{3,1},{4,6},{5,7},{6,4},{7,5},{8,10},{9,11},{10,... | collective-permute-start | bytes 368648 | tf_op jit(solution)/shard_map/ppermute | solution.py:806
  64.0 2.1 %collective-permute-done.9 = f32[40,768]{1,0:T(8,128)S(1)} collective-permute-done((f32[40,768]{1,0:T(8,128)S(1)}, f32[40,768]{1,0:T(8,128)S(1)}, u32[]{:S(2)}, u32[]{:S(2)}) %collective-permute-start.9) | collective-permute-done | bytes 122912 | tf_op jit(solution)/shard_map/ppermute | solution.py:806
  66.1 2.5 %collective-permute-done.10 = f32[40,768]{1,0:T(8,128)S(1)} collective-permute-done((f32[40,768]{1,0:T(8,128)S(1)}, f32[40,768]{1,0:T(8,128)S(1)}, u32[]{:S(2)}, u32[]{:S(2)}) %collective-permute-start.10) | collective-permute-done | bytes 122912 | tf_op jit(solution)/shard_map/ppermute | solution.py:806
  68.7 0.1 collective-permute-start.12
  68.8 1.9 %collective-permute-done.12.theirs_ref = f32[160,768]{1,0:T(8,128)S(1)} collective-permute-done((f32[160,768]{1,0:T(8,128)S(1)}, f32[160,768]{1,0:T(8,128)S(1)}, u32[]{:S(2)}, u32[]{:S(2)}) %collective-permute-start.12) | collective-permute-done | bytes 491552 | tf_op jit(solution)/shard_map/ppermute | solution.py:808
  70.6 1.9 %final.1 = (f32[256,768]{1,0:T(8,128)}, f32[4,768]{1,0:T(4,128)}, f32[768]{0:T(1024)}, f32[768]{0:T(1024)}) custom-call(s32[2]{0:T(128)S(1)} %pad_add_fusion.place_ref, f32[160,768]{1,0:T(8,128)S(1)} %constant_dynamic-update-slice_fusion.mine_ref, f32[160,768]{1,0:T(8,128)S(1)} %collective-permute-done.12.theirs_ref, f32[4,768]{1,0:T(4,128)S(1)} %get-tuple-element.52.w_ref, ...), custom_call_target="tpu_custom_call" | custom-call | tf_op jit(solution)/shard_map/final/pallas_call | solution.py:810
  (18 shorter events, 0.2 us)
Async XLA Ops:
  0.7 10.0 %collective-permute-start.1 = (s32[16,256]{1,0:T(8,128)}, s32[16,256]{1,0:T(8,128)S(1)}, u32[]{:S(2)}, u32[]{:S(2)}) collective-permute-start(s32[16,256]{1,0:T(8,128)} %ids_hbm), channel_id=1, source_target_pairs={{1,0},{2,1},{3,2},{4,3},{5,4},{6,5},{7,6},{8,7},{9,8},{10,9},{11,1... | collective-permute-start | bytes 49160 | tf_op jit(solution)/shard_map/ppermute | solution.py:788
  2.0 8.7 %collective-permute-start = (s32[16,256]{1,0:T(8,128)}, s32[16,256]{1,0:T(8,128)S(1)}, u32[]{:S(2)}, u32[]{:S(2)}) collective-permute-start(s32[16,256]{1,0:T(8,128)} %ids_hbm), channel_id=1, source_target_pairs={{0,1},{1,2},{2,3},{3,4},{4,5},{5,6},{6,7},{7,8},{8,9},{9,10},{10,1... | collective-permute-start | bytes 49160 | tf_op jit(solution)/shard_map/ppermute | solution.py:787
  21.8 1.8 %collective-permute-start.2 = (f32[128,768]{1,0:T(8,128)S(1)}, f32[128,768]{1,0:T(8,128)S(1)}, u32[]{:S(2)}, u32[]{:S(2)}) collective-permute-start(f32[128,768]{1,0:T(8,128)S(1)} %constant_dynamic-slice_fusion.3), channel_id=1, source_target_pairs={{0,16},{16,0},{1,17},{17,1},{2,18},{18,2},{3,19},{19,3},{4,20},{20... | collective-permute-start | bytes 1179656 | tf_op jit(solution)/shard_map/ppermute | solution.py:756
  23.7 21.7 %collective-permute-start.3 = (f32[32,768]{1,0:T(8,128)S(1)}, f32[32,768]{1,0:T(8,128)S(1)}, u32[]{:S(2)}, u32[]{:S(2)}) collective-permute-start(f32[32,768]{1,0:T(8,128)S(1)} %get-tuple-element.87), channel_id=1, source_target_pairs={{0,1},{1,0},{2,3},{3,2},{4,5},{5,4},{6,7},{7,6},{8,9},{9,8},{10,11... | collective-permute-start | bytes 294920 | tf_op jit(solution)/shard_map/ppermute | solution.py:756
  26.7 18.7 %collective-permute-start.5 = (f32[32,768]{1,0:T(8,128)S(1)}, f32[32,768]{1,0:T(8,128)S(1)}, u32[]{:S(2)}, u32[]{:S(2)}) collective-permute-start(f32[32,768]{1,0:T(8,128)S(1)} %get-tuple-element.88), channel_id=1, source_target_pairs={{0,3},{1,2},{2,1},{3,0},{4,7},{5,6},{6,5},{7,4},{8,11},{9,10},{10,... | collective-permute-start | bytes 294920 | tf_op jit(solution)/shard_map/ppermute | solution.py:756
  28.6 16.8 %collective-permute-start.4 = (f32[32,768]{1,0:T(8,128)S(1)}, f32[32,768]{1,0:T(8,128)S(1)}, u32[]{:S(2)}, u32[]{:S(2)}) collective-permute-start(f32[32,768]{1,0:T(8,128)S(1)} %get-tuple-element.89), channel_id=1, source_target_pairs={{0,2},{1,3},{2,0},{3,1},{4,6},{5,7},{6,4},{7,5},{8,10},{9,11},{10,... | collective-permute-start | bytes 294920 | tf_op jit(solution)/shard_map/ppermute | solution.py:756
  45.4 9.6 %collective-permute-start.8 = (f32[40,768]{1,0:T(8,128)S(1)}, f32[40,768]{1,0:T(8,128)S(1)}, u32[]{:S(2)}, u32[]{:S(2)}) collective-permute-start(f32[40,768]{1,0:T(8,128)S(1)} %pad_maximum_fusion), channel_id=1, source_target_pairs={{0,12},{1,13},{2,14},{3,15},{4,8},{5,9},{6,10},{7,11},{8,4},{9,5},... | collective-permute-start | bytes 368648 | tf_op jit(solution)/shard_map/ppermute | solution.py:762
  50.5 9.8 %collective-permute-start.7 = (f32[40,768]{1,0:T(8,128)S(1)}, f32[40,768]{1,0:T(8,128)S(1)}, u32[]{:S(2)}, u32[]{:S(2)}) collective-permute-start(f32[40,768]{1,0:T(8,128)S(1)} %pad_maximum_fusion), channel_id=1, source_target_pairs={{0,8},{1,9},{2,10},{3,11},{4,12},{5,13},{6,14},{7,15},{8,0},{9,1},... | collective-permute-start | bytes 368648 | tf_op jit(solution)/shard_map/ppermute | solution.py:762
  50.5 9.8 %collective-permute-start.6 = (f32[40,768]{1,0:T(8,128)S(1)}, f32[40,768]{1,0:T(8,128)S(1)}, u32[]{:S(2)}, u32[]{:S(2)}) collective-permute-start(f32[40,768]{1,0:T(8,128)S(1)} %pad_maximum_fusion), channel_id=1, source_target_pairs={{0,4},{1,5},{2,6},{3,7},{4,0},{5,1},{6,2},{7,3},{8,12},{9,13},{10,... | collective-permute-start | bytes 368648 | tf_op jit(solution)/shard_map/ppermute | solution.py:762
  60.4 5.7 %collective-permute-start.9 = (f32[40,768]{1,0:T(8,128)S(1)}, f32[40,768]{1,0:T(8,128)S(1)}, u32[]{:S(2)}, u32[]{:S(2)}) collective-permute-start(f32[40,768]{1,0:T(8,128)S(1)} %add_add_fusion), channel_id=1, source_target_pairs={{0,1},{1,0},{2,3},{3,2},{4,5},{5,4},{6,7},{7,6},{8,9},{9,8},{10,11... | collective-permute-start | bytes 368648 | tf_op jit(solution)/shard_map/ppermute | solution.py:806
  60.8 7.8 %collective-permute-start.11 = (f32[40,768]{1,0:T(8,128)S(1)}, f32[40,768]{1,0:T(8,128)S(1)}, u32[]{:S(2)}, u32[]{:S(2)}) collective-permute-start(f32[40,768]{1,0:T(8,128)S(1)} %add_add_fusion), channel_id=1, source_target_pairs={{0,3},{1,2},{2,1},{3,0},{4,7},{5,6},{6,5},{7,4},{8,11},{9,10},{10,... | collective-permute-start | bytes 368648 | tf_op jit(solution)/shard_map/ppermute | solution.py:806
  62.3 6.3 %collective-permute-start.10 = (f32[40,768]{1,0:T(8,128)S(1)}, f32[40,768]{1,0:T(8,128)S(1)}, u32[]{:S(2)}, u32[]{:S(2)}) collective-permute-start(f32[40,768]{1,0:T(8,128)S(1)} %add_add_fusion), channel_id=1, source_target_pairs={{0,2},{1,3},{2,0},{3,1},{4,6},{5,7},{6,4},{7,5},{8,10},{9,11},{10,... | collective-permute-start | bytes 368648 | tf_op jit(solution)/shard_map/ppermute | solution.py:806
  68.7 1.9 %collective-permute-start.12 = (f32[160,768]{1,0:T(8,128)S(1)}, f32[160,768]{1,0:T(8,128)S(1)}, u32[]{:S(2)}, u32[]{:S(2)}) collective-permute-start(f32[160,768]{1,0:T(8,128)S(1)} %constant_dynamic-update-slice_fusion.mine_ref), channel_id=1, source_target_pairs={{0,16},{16,0},{1,17},{17,1},{2,18},{18,2},{3,19},{19,3},{4,20},{20... | collective-permute-start | bytes 1474568 | tf_op jit(solution)/shard_map/ppermute | solution.py:808

commit v5 on v4

--- a/solution.py
+++ b/solution.py
@@ -218,13 +218,14 @@
 
 
 def one_hot_t(ids, vocab):
-    return jnp.where(
-        lax.broadcasted_iota(I32, (vocab, 128), 0) == ids, 1.0, 0.0
-    ).astype(BF16)
+    value = lax.broadcasted_iota(I32, (vocab, 128), 0).astype(F32).astype(BF16)
+    match = value == jnp.broadcast_to(ids.astype(F32), (16, 128)).astype(BF16)[:1]
+    return jnp.where(match, jnp.ones((), BF16), jnp.zeros((), BF16))
 
 
 def weave(*parts):
-    order = [((i + 0.5) / len(p), k, step) for k, p in enumerate(parts) for i, step in enumerate(p)]
+    late = [0.9 if k == len(parts) - 2 else 0.0 for k in range(len(parts))]
+    order = [((i + late[k]) / len(p), k, s) for k, p in enumerate(parts) for i, s in enumerate(p)]
     for _, _, step in sorted(order, key=lambda item: item[:2]):
         step()
 
@@ -403,9 +404,12 @@
         at = slice(cs[0] * 128, cs[-1] * 128 + 128)
 
         def mark(c):
-            column = jnp.broadcast_to(turned[:, g * per + c : g * per + c + 1], (128, vocab))
-            found = jnp.where(column == lanes((128, vocab)).astype(F32), 1.0, 0.0)
-            oh_refs[g][c * 128 : c * 128 + 128, :] = found.astype(BF16)
+            column = turned[:, g * per + c : g * per + c + 1]
+            column = jnp.broadcast_to(column, (128, 128)).astype(BF16)
+            for v in range(0, vocab, 128):
+                match = column == (lanes((128, 128)) + v).astype(F32).astype(BF16)
+                found = jnp.where(match, jnp.ones((), BF16), jnp.zeros((), BF16))
+                oh_refs[g][c * 128 : c * 128 + 128, v : v + 128] = found
 
         def step(n):
             cols = slice(n, n + 256)

time: 72.8 us -> 71.8 us (0.986)
  Pallas kernels: 36.2 us -> 35.4 us
    pallas_call x1, Pallas kernels: 16.2 us -> 15.5 us  [near_call(): pl.pallas_call(near_kernel, out_shape=[pltpu.VMEM((8, width), F32)] + [pl...]
where the time goes in v5:
time: 71.8 us; the launch traced here: 71.5 us
  Pallas kernels  35.4 us (49%)
  starting transfers between devices  21.6 us (30%)
  waiting for transfers between devices  13.3 us (19%)
  between operations  0.82 us (1%)
    pallas_call x1, Pallas kernels, near_call(): pl.pallas_call(near_kernel, out_shape=[pltpu.VMEM((8, width), F32)] + [pl...  15.5 us
    pallas_call x1, Pallas kernels, table_call(): pl.pallas_call(table_kernel, out_shape=(pltpu.VMEM((vocab, width), F32),...  10.7 us
    ppermute x3, starting transfers between devices, exchange_sum(): lax.ppermute(v, axis, partners(axis, m << low))  5.75 us
    ppermute x1, starting transfers between devices, per_device(): left = lax.ppermute(byte_ids, 'seq', up)  5.48 us
    ppermute x4, starting transfers between devices, scatter_sum(): lax.ppermute(part(v, places[m], size), axis, partners(axis, m << low))  5.47 us
    ppermute x3, waiting for transfers between devices, exchange_sum(): lax.ppermute(v, axis, partners(axis, m << low))  5.11 us
    ppermute x3, waiting for transfers between devices, per_device(): lax.ppermute(both, axis, partners(axis, m << low))  4.66 us
    pallas_call x1, Pallas kernels, latent_call(): pl.pallas_call(latent_kernel, out_shape=jax.ShapeDtypeStruct(shape, F32),...  4.06 us
  transfers between devices with their start and end apart: 13, of which 5 were waited for; matrix products, arithmetic and copies ran while one was open for 0% of the time, Pallas kernels for 32%

profile of v5, /device:TPU:0, one launch (start us, length us, event | category | flops | bytes accessed | tf_op | source)
XLA Modules:
  0.0 71.5 jit_solution(13939707560514273539)
XLA Ops:
  0.6 0.1 pad_add_fusion.place_ref
  0.7 1.3 %collective-permute-start.1 = (s32[16,256]{1,0:T(8,128)}, s32[16,256]{1,0:T(8,128)S(1)}, u32[]{:S(2)}, u32[]{:S(2)}) collective-permute-start(s32[16,256]{1,0:T(8,128)} %ids_hbm), channel_id=1, source_target_pairs={{1,0},{2,1},{3,2},{4,3},{5,4},{6,5},{7,6},{8,7},{9,8},{10,9},{11,1... | collective-permute-start | bytes 49160 | tf_op jit(solution)/shard_map/ppermute | solution.py:792
  2.0 5.5 %collective-permute-start = (s32[16,256]{1,0:T(8,128)}, s32[16,256]{1,0:T(8,128)S(1)}, u32[]{:S(2)}, u32[]{:S(2)}) collective-permute-start(s32[16,256]{1,0:T(8,128)} %ids_hbm), channel_id=1, source_target_pairs={{0,1},{1,2},{2,3},{3,4},{4,5},{5,6},{6,7},{7,8},{8,9},{9,10},{10,1... | collective-permute-start | bytes 49160 | tf_op jit(solution)/shard_map/ppermute | solution.py:791
  7.5 3.2 %prep.1 = (f32[8,256]{1,0:T(8,128)S(1)}, bf16[256,768]{1,0:T(8,128)(2,1)S(1)}, bf16[256,768]{1,0:T(8,128)(2,1)S(1)}, s32[32,128]{1,0:T(8,128)S(1)}, s32[32,128]{...) custom-call(s32[1]{0:T(128)} %bitcast.start_hbm, ...), custom_call_target="tpu_custom_call" | custom-call | flops 100000000 | bytes 1000000 | tf_op jit(solution)/shard_map/prep/pallas_call | solution.py:644
  10.8 10.7 %table_grad.1 = (f32[256,768]{1,0:T(8,128)S(1)}, f32[8,32,128]{2,1,0:T(8,128)S(1)}, s32[48,128]{1,0:T(8,128)S(1)}, bf16[2560,128]{1,0:T(8,128)(2,1)S(1)}, bf16[2...) custom-call(s32[32,128]{1,0:T(8,128)S(1)} %get-tuple-element.48.even, ...), custom_call_target="tpu_custom_call" | custom-call | flops 8000000000 | bytes 20000000 | tf_op jit(solution)/shard_map/table_grad/pallas_call | solution.py:676
  21.5 0.1 collective-permute-start.2
  21.6 1.7 %collective-permute-done.2 = f32[128,768]{1,0:T(8,128)S(1)} collective-permute-done((f32[128,768]{1,0:T(8,128)S(1)}, f32[128,768]{1,0:T(8,128)S(1)}, u32[]{:S(2)}, u32[]{:S(2)}) %collective-permute-start.2) | collective-permute-done | bytes 393248 | tf_op jit(solution)/shard_map/ppermute | solution.py:760
  23.3 0.1 dynamic-slice_add_fusion
  23.4 3.0 %collective-permute-start.3 = (f32[32,768]{1,0:T(8,128)S(1)}, f32[32,768]{1,0:T(8,128)S(1)}, u32[]{:S(2)}, u32[]{:S(2)}) collective-permute-start(f32[32,768]{1,0:T(8,128)S(1)} %get-tuple-element.87), channel_id=1, source_target_pairs={{0,1},{1,0},{2,3},{3,2},{4,5},{5,4},{6,7},{7,6},{8,9},{9,8},{10,11... | collective-permute-start | bytes 294920 | tf_op jit(solution)/shard_map/ppermute | solution.py:760
  26.4 1.9 %collective-permute-start.5 = (f32[32,768]{1,0:T(8,128)S(1)}, f32[32,768]{1,0:T(8,128)S(1)}, u32[]{:S(2)}, u32[]{:S(2)}) collective-permute-start(f32[32,768]{1,0:T(8,128)S(1)} %get-tuple-element.88), channel_id=1, source_target_pairs={{0,3},{1,2},{2,1},{3,0},{4,7},{5,6},{6,5},{7,4},{8,11},{9,10},{10,... | collective-permute-start | bytes 294920 | tf_op jit(solution)/shard_map/ppermute | solution.py:760
  28.3 0.5 collective-permute-start.4
  28.8 15.5 %near.1 = (f32[8,768]{1,0:T(8,128)S(1)}, bf16[2176,768]{1,0:T(8,128)(2,1)S(1)}, bf16[2176,768]{1,0:T(8,128)(2,1)S(1)}, bf16[2176,768]{1,0:T(8,128)(2,1)S(1)}, bf16[2176,768]{1,0:T(8,128)(2,1)S(1)}) custom-call(s32[32,128]{1,0:T(8,128)S(1)} %get-tuple-element.48.even_ref, s32[32,128]{1,0:T(8,128)S(1)} %get-tuple-element.49.length_ref, ...), custom_call_target="tpu_custom_call" | custom-call | flops 16000000000 | bytes 40000000 | tf_op jit(solution)/shard_map/near/pallas_call | solution.py:705
  44.4 5.1 %collective-permute-start.8 = (f32[40,768]{1,0:T(8,128)S(1)}, f32[40,768]{1,0:T(8,128)S(1)}, u32[]{:S(2)}, u32[]{:S(2)}) collective-permute-start(f32[40,768]{1,0:T(8,128)S(1)} %pad_maximum_fusion), channel_id=1, source_target_pairs={{0,12},{1,13},{2,14},{3,15},{4,8},{5,9},{6,10},{7,11},{8,4},{9,5},... | collective-permute-start | bytes 368648 | tf_op jit(solution)/shard_map/ppermute | solution.py:766
  49.5 0.6 collective-permute-start.6
  50.2 4.1 %latent.1 = f32[16,128,768]{2,1,0:T(8,128)} custom-call(bf16[2176,768]{1,0:T(8,128)(2,1)S(1)} %get-tuple-element.74.high0, bf16[2176,768]{1,0:T(8,128)(2,1)S(1)} %get-tuple-element.75.low0, bf16[2176,768]{1,0:T(8,128)(2,1)S(1)} %get-tuple-element.76.high1, bf16[2176,768]{1,0:T(8,128)(2,1)S(1)} %get-tuple-element.77.low1, ...), custom_call_target="tpu_custom_call" | custom-call | flops 4000000000 | bytes 10000000 | tf_op jit(solution)/shard_map/latent/pallas_call | solution.py:726
  54.3 5.1 %collective-permute-done.7 = f32[40,768]{1,0:T(8,128)S(1)} collective-permute-done((f32[40,768]{1,0:T(8,128)S(1)}, f32[40,768]{1,0:T(8,128)S(1)}, u32[]{:S(2)}, u32[]{:S(2)}) %collective-permute-start.7) | collective-permute-done | bytes 122912 | tf_op jit(solution)/shard_map/ppermute | solution.py:766
  59.4 0.4 collective-permute-start.9
  59.8 1.5 %collective-permute-start.11 = (f32[40,768]{1,0:T(8,128)S(1)}, f32[40,768]{1,0:T(8,128)S(1)}, u32[]{:S(2)}, u32[]{:S(2)}) collective-permute-start(f32[40,768]{1,0:T(8,128)S(1)} %add_add_fusion), channel_id=1, source_target_pairs={{0,3},{1,2},{2,1},{3,0},{4,7},{5,6},{6,5},{7,4},{8,11},{9,10},{10,... | collective-permute-start | bytes 368648 | tf_op jit(solution)/shard_map/ppermute | solution.py:810
  61.3 1.6 %collective-permute-start.10 = (f32[40,768]{1,0:T(8,128)S(1)}, f32[40,768]{1,0:T(8,128)S(1)}, u32[]{:S(2)}, u32[]{:S(2)}) collective-permute-start(f32[40,768]{1,0:T(8,128)S(1)} %add_add_fusion), channel_id=1, source_target_pairs={{0,2},{1,3},{2,0},{3,1},{4,6},{5,7},{6,4},{7,5},{8,10},{9,11},{10,... | collective-permute-start | bytes 368648 | tf_op jit(solution)/shard_map/ppermute | solution.py:810
  63.0 2.1 %collective-permute-done.9 = f32[40,768]{1,0:T(8,128)S(1)} collective-permute-done((f32[40,768]{1,0:T(8,128)S(1)}, f32[40,768]{1,0:T(8,128)S(1)}, u32[]{:S(2)}, u32[]{:S(2)}) %collective-permute-start.9) | collective-permute-done | bytes 122912 | tf_op jit(solution)/shard_map/ppermute | solution.py:810
  65.1 2.5 %collective-permute-done.10 = f32[40,768]{1,0:T(8,128)S(1)} collective-permute-done((f32[40,768]{1,0:T(8,128)S(1)}, f32[40,768]{1,0:T(8,128)S(1)}, u32[]{:S(2)}, u32[]{:S(2)}) %collective-permute-start.10) | collective-permute-done | bytes 122912 | tf_op jit(solution)/shard_map/ppermute | solution.py:810
  67.7 0.1 collective-permute-start.12
  67.8 1.9 %collective-permute-done.12.theirs_ref = f32[160,768]{1,0:T(8,128)S(1)} collective-permute-done((f32[160,768]{1,0:T(8,128)S(1)}, f32[160,768]{1,0:T(8,128)S(1)}, u32[]{:S(2)}, u32[]{:S(2)}) %collective-permute-start.12) | collective-permute-done | bytes 491552 | tf_op jit(solution)/shard_map/ppermute | solution.py:812
  69.6 1.9 %final.1 = (f32[256,768]{1,0:T(8,128)}, f32[4,768]{1,0:T(4,128)}, f32[768]{0:T(1024)}, f32[768]{0:T(1024)}) custom-call(s32[2]{0:T(128)S(1)} %pad_add_fusion.place_ref, f32[160,768]{1,0:T(8,128)S(1)} %constant_dynamic-update-slice_fusion.mine_ref, f32[160,768]{1,0:T(8,128)S(1)} %collective-permute-done.12.theirs_ref, f32[4,768]{1,0:T(4,128)S(1)} %get-tuple-element.52.w_ref, ...), custom_call_target="tpu_custom_call" | custom-call | tf_op jit(solution)/shard_map/final/pallas_call | solution.py:814
  (18 shorter events, 0.2 us)
Async XLA Ops:
  0.7 10.0 %collective-permute-start.1 = (s32[16,256]{1,0:T(8,128)}, s32[16,256]{1,0:T(8,128)S(1)}, u32[]{:S(2)}, u32[]{:S(2)}) collective-permute-start(s32[16,256]{1,0:T(8,128)} %ids_hbm), channel_id=1, source_target_pairs={{1,0},{2,1},{3,2},{4,3},{5,4},{6,5},{7,6},{8,7},{9,8},{10,9},{11,1... | collective-permute-start | bytes 49160 | tf_op jit(solution)/shard_map/ppermute | solution.py:792
  2.0 8.7 %collective-permute-start = (s32[16,256]{1,0:T(8,128)}, s32[16,256]{1,0:T(8,128)S(1)}, u32[]{:S(2)}, u32[]{:S(2)}) collective-permute-start(s32[16,256]{1,0:T(8,128)} %ids_hbm), channel_id=1, source_target_pairs={{0,1},{1,2},{2,3},{3,4},{4,5},{5,6},{6,7},{7,8},{8,9},{9,10},{10,1... | collective-permute-start | bytes 49160 | tf_op jit(solution)/shard_map/ppermute | solution.py:791
  21.5 1.8 %collective-permute-start.2 = (f32[128,768]{1,0:T(8,128)S(1)}, f32[128,768]{1,0:T(8,128)S(1)}, u32[]{:S(2)}, u32[]{:S(2)}) collective-permute-start(f32[128,768]{1,0:T(8,128)S(1)} %constant_dynamic-slice_fusion.3), channel_id=1, source_target_pairs={{0,16},{16,0},{1,17},{17,1},{2,18},{18,2},{3,19},{19,3},{4,20},{20... | collective-permute-start | bytes 1179656 | tf_op jit(solution)/shard_map/ppermute | solution.py:760
  23.4 20.9 %collective-permute-start.3 = (f32[32,768]{1,0:T(8,128)S(1)}, f32[32,768]{1,0:T(8,128)S(1)}, u32[]{:S(2)}, u32[]{:S(2)}) collective-permute-start(f32[32,768]{1,0:T(8,128)S(1)} %get-tuple-element.87), channel_id=1, source_target_pairs={{0,1},{1,0},{2,3},{3,2},{4,5},{5,4},{6,7},{7,6},{8,9},{9,8},{10,11... | collective-permute-start | bytes 294920 | tf_op jit(solution)/shard_map/ppermute | solution.py:760
  26.4 17.9 %collective-permute-start.5 = (f32[32,768]{1,0:T(8,128)S(1)}, f32[32,768]{1,0:T(8,128)S(1)}, u32[]{:S(2)}, u32[]{:S(2)}) collective-permute-start(f32[32,768]{1,0:T(8,128)S(1)} %get-tuple-element.88), channel_id=1, source_target_pairs={{0,3},{1,2},{2,1},{3,0},{4,7},{5,6},{6,5},{7,4},{8,11},{9,10},{10,... | collective-permute-start | bytes 294920 | tf_op jit(solution)/shard_map/ppermute | solution.py:760
  28.3 16.0 %collective-permute-start.4 = (f32[32,768]{1,0:T(8,128)S(1)}, f32[32,768]{1,0:T(8,128)S(1)}, u32[]{:S(2)}, u32[]{:S(2)}) collective-permute-start(f32[32,768]{1,0:T(8,128)S(1)} %get-tuple-element.89), channel_id=1, source_target_pairs={{0,2},{1,3},{2,0},{3,1},{4,6},{5,7},{6,4},{7,5},{8,10},{9,11},{10,... | collective-permute-start | bytes 294920 | tf_op jit(solution)/shard_map/ppermute | solution.py:760
  44.4 9.8 %collective-permute-start.8 = (f32[40,768]{1,0:T(8,128)S(1)}, f32[40,768]{1,0:T(8,128)S(1)}, u32[]{:S(2)}, u32[]{:S(2)}) collective-permute-start(f32[40,768]{1,0:T(8,128)S(1)} %pad_maximum_fusion), channel_id=1, source_target_pairs={{0,12},{1,13},{2,14},{3,15},{4,8},{5,9},{6,10},{7,11},{8,4},{9,5},... | collective-permute-start | bytes 368648 | tf_op jit(solution)/shard_map/ppermute | solution.py:766
  49.5 9.8 %collective-permute-start.7 = (f32[40,768]{1,0:T(8,128)S(1)}, f32[40,768]{1,0:T(8,128)S(1)}, u32[]{:S(2)}, u32[]{:S(2)}) collective-permute-start(f32[40,768]{1,0:T(8,128)S(1)} %pad_maximum_fusion), channel_id=1, source_target_pairs={{0,8},{1,9},{2,10},{3,11},{4,12},{5,13},{6,14},{7,15},{8,0},{9,1},... | collective-permute-start | bytes 368648 | tf_op jit(solution)/shard_map/ppermute | solution.py:766
  49.5 9.8 %collective-permute-start.6 = (f32[40,768]{1,0:T(8,128)S(1)}, f32[40,768]{1,0:T(8,128)S(1)}, u32[]{:S(2)}, u32[]{:S(2)}) collective-permute-start(f32[40,768]{1,0:T(8,128)S(1)} %pad_maximum_fusion), channel_id=1, source_target_pairs={{0,4},{1,5},{2,6},{3,7},{4,0},{5,1},{6,2},{7,3},{8,12},{9,13},{10,... | collective-permute-start | bytes 368648 | tf_op jit(solution)/shard_map/ppermute | solution.py:766
  59.4 5.7 %collective-permute-start.9 = (f32[40,768]{1,0:T(8,128)S(1)}, f32[40,768]{1,0:T(8,128)S(1)}, u32[]{:S(2)}, u32[]{:S(2)}) collective-permute-start(f32[40,768]{1,0:T(8,128)S(1)} %add_add_fusion), channel_id=1, source_target_pairs={{0,1},{1,0},{2,3},{3,2},{4,5},{5,4},{6,7},{7,6},{8,9},{9,8},{10,11... | collective-permute-start | bytes 368648 | tf_op jit(solution)/shard_map/ppermute | solution.py:810
  59.8 7.8 %collective-permute-start.11 = (f32[40,768]{1,0:T(8,128)S(1)}, f32[40,768]{1,0:T(8,128)S(1)}, u32[]{:S(2)}, u32[]{:S(2)}) collective-permute-start(f32[40,768]{1,0:T(8,128)S(1)} %add_add_fusion), channel_id=1, source_target_pairs={{0,3},{1,2},{2,1},{3,0},{4,7},{5,6},{6,5},{7,4},{8,11},{9,10},{10,... | collective-permute-start | bytes 368648 | tf_op jit(solution)/shard_map/ppermute | solution.py:810
  61.3 6.3 %collective-permute-start.10 = (f32[40,768]{1,0:T(8,128)S(1)}, f32[40,768]{1,0:T(8,128)S(1)}, u32[]{:S(2)}, u32[]{:S(2)}) collective-permute-start(f32[40,768]{1,0:T(8,128)S(1)} %add_add_fusion), channel_id=1, source_target_pairs={{0,2},{1,3},{2,0},{3,1},{4,6},{5,7},{6,4},{7,5},{8,10},{9,11},{10,... | collective-permute-start | bytes 368648 | tf_op jit(solution)/shard_map/ppermute | solution.py:810
  67.7 1.9 %collective-permute-start.12 = (f32[160,768]{1,0:T(8,128)S(1)}, f32[160,768]{1,0:T(8,128)S(1)}, u32[]{:S(2)}, u32[]{:S(2)}) collective-permute-start(f32[160,768]{1,0:T(8,128)S(1)} %constant_dynamic-update-slice_fusion.mine_ref), channel_id=1, source_target_pairs={{0,16},{16,0},{1,17},{17,1},{2,18},{18,2},{3,19},{19,3},{4,20},{20... | collective-permute-start | bytes 1474568 | tf_op jit(solution)/shard_map/ppermute | solution.py:812

commit v6 on v5

--- a/solution.py
+++ b/solution.py
@@ -11,7 +11,7 @@
 HIGH = lax.Precision.HIGHEST
 ROWS = 16
 TAPS = 4
-TABLE_BATCH, MIX_BATCH, LATENT_BATCH = 4, 4, 4
+TABLE_BATCH, MIX_BATCH, LATENT_BATCH = 2, 4, 4
 RING = 18
 RELS = (-2, -1, 0, 1, 2, 3)
 NT = (((1,), (1,)), ((), ()))
@@ -590,11 +590,11 @@
         hist.append(small[6 + at // width : 7 + at // width, at % width : at % width + vocab])
     hist = jnp.concatenate(hist + [jnp.zeros((8 - TAPS, vocab), F32)], axis=0).T
     scaled = w_ref[...] * line(s_ref)
-    for k in range(TAPS):
-        turned = jnp.broadcast_to(hist[:, k : k + 1], (vocab, 128))
+    for v in range(0, vocab, 64):
+        turned = [jnp.broadcast_to(hist[v : v + 64, k : k + 1], (64, 128)) for k in range(TAPS)]
         for n in range(0, width, 128):
-            add = turned * scaled[k : k + 1, n : n + 128]
-            ge_ref[:, n : n + 128] = add if k == 0 else ge_ref[:, n : n + 128] + add
+            cols = slice(n, n + 128)
+            ge_ref[v : v + 64, cols] = sum(turned[k] * scaled[k : k + 1, cols] for k in range(TAPS))
     for (mask, _), (ref, at) in zip(places, pieces):
         row, rest = 0, vocab
         for i, stage in enumerate(stages):

time: 71.8 us -> 70.9 us (0.987)
  Pallas kernels: 35.4 us -> 34.6 us
    pallas_call x1, Pallas kernels: 10.7 us -> 9.84 us  [table_call(): pl.pallas_call(table_kernel, out_shape=(pltpu.VMEM((vocab, width), F32),...]
where the time goes in v6:
time: 70.9 us; the launch traced here: 70.6 us
  Pallas kernels  34.6 us (49%)
  starting transfers between devices  21.6 us (30%)
  waiting for transfers between devices  13.3 us (19%)
  between operations  0.82 us (1%)
    pallas_call x1, Pallas kernels, near_call(): pl.pallas_call(near_kernel, out_shape=[pltpu.VMEM((8, width), F32)] + [pl...  15.5 us
    pallas_call x1, Pallas kernels, table_call(): pl.pallas_call(table_kernel, out_shape=(pltpu.VMEM((vocab, width), F32),...  9.84 us
    ppermute x3, starting transfers between devices, exchange_sum(): lax.ppermute(v, axis, partners(axis, m << low))  5.75 us
    ppermute x1, starting transfers between devices, per_device(): left = lax.ppermute(byte_ids, 'seq', up)  5.48 us
    ppermute x4, starting transfers between devices, scatter_sum(): lax.ppermute(part(v, places[m], size), axis, partners(axis, m << low))  5.45 us
    ppermute x3, waiting for transfers between devices, exchange_sum(): lax.ppermute(v, axis, partners(axis, m << low))  5.07 us
    ppermute x3, waiting for transfers between devices, per_device(): lax.ppermute(both, axis, partners(axis, m << low))  4.67 us
    pallas_call x1, Pallas kernels, latent_call(): pl.pallas_call(latent_kernel, out_shape=jax.ShapeDtypeStruct(shape, F32),...  4.1 us
  transfers between devices with their start and end apart: 13, of which 5 were waited for; matrix products, arithmetic and copies ran while one was open for 0% of the time, Pallas kernels for 32%

profile of v6, /device:TPU:0, one launch (start us, length us, event | category | flops | bytes accessed | tf_op | source)
XLA Modules:
  0.0 70.6 jit_solution(14544408346714917481)
XLA Ops:
  0.6 0.1 pad_add_fusion.place_ref
  0.7 1.3 %collective-permute-start.1 = (s32[16,256]{1,0:T(8,128)}, s32[16,256]{1,0:T(8,128)S(1)}, u32[]{:S(2)}, u32[]{:S(2)}) collective-permute-start(s32[16,256]{1,0:T(8,128)} %ids_hbm), channel_id=1, source_target_pairs={{1,0},{2,1},{3,2},{4,3},{5,4},{6,5},{7,6},{8,7},{9,8},{10,9},{11,1... | collective-permute-start | bytes 49160 | tf_op jit(solution)/shard_map/ppermute | solution.py:792
  2.0 5.5 %collective-permute-start = (s32[16,256]{1,0:T(8,128)}, s32[16,256]{1,0:T(8,128)S(1)}, u32[]{:S(2)}, u32[]{:S(2)}) collective-permute-start(s32[16,256]{1,0:T(8,128)} %ids_hbm), channel_id=1, source_target_pairs={{0,1},{1,2},{2,3},{3,4},{4,5},{5,6},{6,7},{7,8},{8,9},{9,10},{10,1... | collective-permute-start | bytes 49160 | tf_op jit(solution)/shard_map/ppermute | solution.py:791
  7.5 3.2 %prep.1 = (f32[8,256]{1,0:T(8,128)S(1)}, bf16[256,768]{1,0:T(8,128)(2,1)S(1)}, bf16[256,768]{1,0:T(8,128)(2,1)S(1)}, s32[32,128]{1,0:T(8,128)S(1)}, s32[32,128]{...) custom-call(s32[1]{0:T(128)} %bitcast.start_hbm, ...), custom_call_target="tpu_custom_call" | custom-call | flops 100000000 | bytes 1000000 | tf_op jit(solution)/shard_map/prep/pallas_call | solution.py:644
  10.8 9.8 %table_grad.1 = (f32[256,768]{1,0:T(8,128)S(1)}, f32[8,32,128]{2,1,0:T(8,128)S(1)}, s32[48,128]{1,0:T(8,128)S(1)}, bf16[2560,128]{1,0:T(8,128)(2,1)S(1)}, bf16[2...) custom-call(s32[32,128]{1,0:T(8,128)S(1)} %get-tuple-element.48.even, ...), custom_call_target="tpu_custom_call" | custom-call | flops 8000000000 | bytes 20000000 | tf_op jit(solution)/shard_map/table_grad/pallas_call | solution.py:676
  20.6 0.1 collective-permute-start.2
  20.7 1.7 %collective-permute-done.2 = f32[128,768]{1,0:T(8,128)S(1)} collective-permute-done((f32[128,768]{1,0:T(8,128)S(1)}, f32[128,768]{1,0:T(8,128)S(1)}, u32[]{:S(2)}, u32[]{:S(2)}) %collective-permute-start.2) | collective-permute-done | bytes 393248 | tf_op jit(solution)/shard_map/ppermute | solution.py:760
  22.4 0.1 dynamic-slice_add_fusion
  22.5 3.0 %collective-permute-start.3 = (f32[32,768]{1,0:T(8,128)S(1)}, f32[32,768]{1,0:T(8,128)S(1)}, u32[]{:S(2)}, u32[]{:S(2)}) collective-permute-start(f32[32,768]{1,0:T(8,128)S(1)} %get-tuple-element.87), channel_id=1, source_target_pairs={{0,1},{1,0},{2,3},{3,2},{4,5},{5,4},{6,7},{7,6},{8,9},{9,8},{10,11... | collective-permute-start | bytes 294920 | tf_op jit(solution)/shard_map/ppermute | solution.py:760
  25.5 1.9 %collective-permute-start.5 = (f32[32,768]{1,0:T(8,128)S(1)}, f32[32,768]{1,0:T(8,128)S(1)}, u32[]{:S(2)}, u32[]{:S(2)}) collective-permute-start(f32[32,768]{1,0:T(8,128)S(1)} %get-tuple-element.88), channel_id=1, source_target_pairs={{0,3},{1,2},{2,1},{3,0},{4,7},{5,6},{6,5},{7,4},{8,11},{9,10},{10,... | collective-permute-start | bytes 294920 | tf_op jit(solution)/shard_map/ppermute | solution.py:760
  27.4 0.5 collective-permute-start.4
  27.9 15.5 %near.1 = (f32[8,768]{1,0:T(8,128)S(1)}, bf16[2176,768]{1,0:T(8,128)(2,1)S(1)}, bf16[2176,768]{1,0:T(8,128)(2,1)S(1)}, bf16[2176,768]{1,0:T(8,128)(2,1)S(1)}, bf16[2176,768]{1,0:T(8,128)(2,1)S(1)}) custom-call(s32[32,128]{1,0:T(8,128)S(1)} %get-tuple-element.48.even_ref, s32[32,128]{1,0:T(8,128)S(1)} %get-tuple-element.49.length_ref, ...), custom_call_target="tpu_custom_call" | custom-call | flops 16000000000 | bytes 40000000 | tf_op jit(solution)/shard_map/near/pallas_call | solution.py:705
  43.5 5.1 %collective-permute-start.8 = (f32[40,768]{1,0:T(8,128)S(1)}, f32[40,768]{1,0:T(8,128)S(1)}, u32[]{:S(2)}, u32[]{:S(2)}) collective-permute-start(f32[40,768]{1,0:T(8,128)S(1)} %pad_maximum_fusion), channel_id=1, source_target_pairs={{0,12},{1,13},{2,14},{3,15},{4,8},{5,9},{6,10},{7,11},{8,4},{9,5},... | collective-permute-start | bytes 368648 | tf_op jit(solution)/shard_map/ppermute | solution.py:766
  48.6 0.6 collective-permute-start.6
  49.3 4.1 %latent.1 = f32[16,128,768]{2,1,0:T(8,128)} custom-call(bf16[2176,768]{1,0:T(8,128)(2,1)S(1)} %get-tuple-element.74.high0, bf16[2176,768]{1,0:T(8,128)(2,1)S(1)} %get-tuple-element.75.low0, bf16[2176,768]{1,0:T(8,128)(2,1)S(1)} %get-tuple-element.76.high1, bf16[2176,768]{1,0:T(8,128)(2,1)S(1)} %get-tuple-element.77.low1, ...), custom_call_target="tpu_custom_call" | custom-call | flops 4000000000 | bytes 10000000 | tf_op jit(solution)/shard_map/latent/pallas_call | solution.py:726
  53.4 5.1 %collective-permute-done.7 = f32[40,768]{1,0:T(8,128)S(1)} collective-permute-done((f32[40,768]{1,0:T(8,128)S(1)}, f32[40,768]{1,0:T(8,128)S(1)}, u32[]{:S(2)}, u32[]{:S(2)}) %collective-permute-start.7) | collective-permute-done | bytes 122912 | tf_op jit(solution)/shard_map/ppermute | solution.py:766
  58.5 0.4 collective-permute-start.9
  58.9 1.5 %collective-permute-start.11 = (f32[40,768]{1,0:T(8,128)S(1)}, f32[40,768]{1,0:T(8,128)S(1)}, u32[]{:S(2)}, u32[]{:S(2)}) collective-permute-start(f32[40,768]{1,0:T(8,128)S(1)} %add_add_fusion), channel_id=1, source_target_pairs={{0,3},{1,2},{2,1},{3,0},{4,7},{5,6},{6,5},{7,4},{8,11},{9,10},{10,... | collective-permute-start | bytes 368648 | tf_op jit(solution)/shard_map/ppermute | solution.py:810
  60.4 1.6 %collective-permute-start.10 = (f32[40,768]{1,0:T(8,128)S(1)}, f32[40,768]{1,0:T(8,128)S(1)}, u32[]{:S(2)}, u32[]{:S(2)}) collective-permute-start(f32[40,768]{1,0:T(8,128)S(1)} %add_add_fusion), channel_id=1, source_target_pairs={{0,2},{1,3},{2,0},{3,1},{4,6},{5,7},{6,4},{7,5},{8,10},{9,11},{10,... | collective-permute-start | bytes 368648 | tf_op jit(solution)/shard_map/ppermute | solution.py:810
  62.1 2.1 %collective-permute-done.9 = f32[40,768]{1,0:T(8,128)S(1)} collective-permute-done((f32[40,768]{1,0:T(8,128)S(1)}, f32[40,768]{1,0:T(8,128)S(1)}, u32[]{:S(2)}, u32[]{:S(2)}) %collective-permute-start.9) | collective-permute-done | bytes 122912 | tf_op jit(solution)/shard_map/ppermute | solution.py:810
  64.2 2.5 %collective-permute-done.10 = f32[40,768]{1,0:T(8,128)S(1)} collective-permute-done((f32[40,768]{1,0:T(8,128)S(1)}, f32[40,768]{1,0:T(8,128)S(1)}, u32[]{:S(2)}, u32[]{:S(2)}) %collective-permute-start.10) | collective-permute-done | bytes 122912 | tf_op jit(solution)/shard_map/ppermute | solution.py:810
  66.8 0.1 collective-permute-start.12
  66.9 1.9 %collective-permute-done.12.theirs_ref = f32[160,768]{1,0:T(8,128)S(1)} collective-permute-done((f32[160,768]{1,0:T(8,128)S(1)}, f32[160,768]{1,0:T(8,128)S(1)}, u32[]{:S(2)}, u32[]{:S(2)}) %collective-permute-start.12) | collective-permute-done | bytes 491552 | tf_op jit(solution)/shard_map/ppermute | solution.py:812
  68.7 1.9 %final.1 = (f32[256,768]{1,0:T(8,128)}, f32[4,768]{1,0:T(4,128)}, f32[768]{0:T(1024)}, f32[768]{0:T(1024)}) custom-call(s32[2]{0:T(128)S(1)} %pad_add_fusion.place_ref, f32[160,768]{1,0:T(8,128)S(1)} %constant_dynamic-update-slice_fusion.mine_ref, f32[160,768]{1,0:T(8,128)S(1)} %collective-permute-done.12.theirs_ref, f32[4,768]{1,0:T(4,128)S(1)} %get-tuple-element.52.w_ref, ...), custom_call_target="tpu_custom_call" | custom-call | tf_op jit(solution)/shard_map/final/pallas_call | solution.py:814
  (18 shorter events, 0.2 us)
Async XLA Ops:
  0.7 10.0 %collective-permute-start.1 = (s32[16,256]{1,0:T(8,128)}, s32[16,256]{1,0:T(8,128)S(1)}, u32[]{:S(2)}, u32[]{:S(2)}) collective-permute-start(s32[16,256]{1,0:T(8,128)} %ids_hbm), channel_id=1, source_target_pairs={{1,0},{2,1},{3,2},{4,3},{5,4},{6,5},{7,6},{8,7},{9,8},{10,9},{11,1... | collective-permute-start | bytes 49160 | tf_op jit(solution)/shard_map/ppermute | solution.py:792
  2.0 8.7 %collective-permute-start = (s32[16,256]{1,0:T(8,128)}, s32[16,256]{1,0:T(8,128)S(1)}, u32[]{:S(2)}, u32[]{:S(2)}) collective-permute-start(s32[16,256]{1,0:T(8,128)} %ids_hbm), channel_id=1, source_target_pairs={{0,1},{1,2},{2,3},{3,4},{4,5},{5,6},{6,7},{7,8},{8,9},{9,10},{10,1... | collective-permute-start | bytes 49160 | tf_op jit(solution)/shard_map/ppermute | solution.py:791
  20.6 1.8 %collective-permute-start.2 = (f32[128,768]{1,0:T(8,128)S(1)}, f32[128,768]{1,0:T(8,128)S(1)}, u32[]{:S(2)}, u32[]{:S(2)}) collective-permute-start(f32[128,768]{1,0:T(8,128)S(1)} %constant_dynamic-slice_fusion.3), channel_id=1, source_target_pairs={{0,16},{16,0},{1,17},{17,1},{2,18},{18,2},{3,19},{19,3},{4,20},{20... | collective-permute-start | bytes 1179656 | tf_op jit(solution)/shard_map/ppermute | solution.py:760
  22.5 20.9 %collective-permute-start.3 = (f32[32,768]{1,0:T(8,128)S(1)}, f32[32,768]{1,0:T(8,128)S(1)}, u32[]{:S(2)}, u32[]{:S(2)}) collective-permute-start(f32[32,768]{1,0:T(8,128)S(1)} %get-tuple-element.87), channel_id=1, source_target_pairs={{0,1},{1,0},{2,3},{3,2},{4,5},{5,4},{6,7},{7,6},{8,9},{9,8},{10,11... | collective-permute-start | bytes 294920 | tf_op jit(solution)/shard_map/ppermute | solution.py:760
  25.5 17.9 %collective-permute-start.5 = (f32[32,768]{1,0:T(8,128)S(1)}, f32[32,768]{1,0:T(8,128)S(1)}, u32[]{:S(2)}, u32[]{:S(2)}) collective-permute-start(f32[32,768]{1,0:T(8,128)S(1)} %get-tuple-element.88), channel_id=1, source_target_pairs={{0,3},{1,2},{2,1},{3,0},{4,7},{5,6},{6,5},{7,4},{8,11},{9,10},{10,... | collective-permute-start | bytes 294920 | tf_op jit(solution)/shard_map/ppermute | solution.py:760
  27.4 16.0 %collective-permute-start.4 = (f32[32,768]{1,0:T(8,128)S(1)}, f32[32,768]{1,0:T(8,128)S(1)}, u32[]{:S(2)}, u32[]{:S(2)}) collective-permute-start(f32[32,768]{1,0:T(8,128)S(1)} %get-tuple-element.89), channel_id=1, source_target_pairs={{0,2},{1,3},{2,0},{3,1},{4,6},{5,7},{6,4},{7,5},{8,10},{9,11},{10,... | collective-permute-start | bytes 294920 | tf_op jit(solution)/shard_map/ppermute | solution.py:760
  43.5 9.9 %collective-permute-start.8 = (f32[40,768]{1,0:T(8,128)S(1)}, f32[40,768]{1,0:T(8,128)S(1)}, u32[]{:S(2)}, u32[]{:S(2)}) collective-permute-start(f32[40,768]{1,0:T(8,128)S(1)} %pad_maximum_fusion), channel_id=1, source_target_pairs={{0,12},{1,13},{2,14},{3,15},{4,8},{5,9},{6,10},{7,11},{8,4},{9,5},... | collective-permute-start | bytes 368648 | tf_op jit(solution)/shard_map/ppermute | solution.py:766
  48.6 9.8 %collective-permute-start.7 = (f32[40,768]{1,0:T(8,128)S(1)}, f32[40,768]{1,0:T(8,128)S(1)}, u32[]{:S(2)}, u32[]{:S(2)}) collective-permute-start(f32[40,768]{1,0:T(8,128)S(1)} %pad_maximum_fusion), channel_id=1, source_target_pairs={{0,8},{1,9},{2,10},{3,11},{4,12},{5,13},{6,14},{7,15},{8,0},{9,1},... | collective-permute-start | bytes 368648 | tf_op jit(solution)/shard_map/ppermute | solution.py:766
  48.6 9.8 %collective-permute-start.6 = (f32[40,768]{1,0:T(8,128)S(1)}, f32[40,768]{1,0:T(8,128)S(1)}, u32[]{:S(2)}, u32[]{:S(2)}) collective-permute-start(f32[40,768]{1,0:T(8,128)S(1)} %pad_maximum_fusion), channel_id=1, source_target_pairs={{0,4},{1,5},{2,6},{3,7},{4,0},{5,1},{6,2},{7,3},{8,12},{9,13},{10,... | collective-permute-start | bytes 368648 | tf_op jit(solution)/shard_map/ppermute | solution.py:766
  58.5 5.7 %collective-permute-start.9 = (f32[40,768]{1,0:T(8,128)S(1)}, f32[40,768]{1,0:T(8,128)S(1)}, u32[]{:S(2)}, u32[]{:S(2)}) collective-permute-start(f32[40,768]{1,0:T(8,128)S(1)} %add_add_fusion), channel_id=1, source_target_pairs={{0,1},{1,0},{2,3},{3,2},{4,5},{5,4},{6,7},{7,6},{8,9},{9,8},{10,11... | collective-permute-start | bytes 368648 | tf_op jit(solution)/shard_map/ppermute | solution.py:810
  58.9 7.8 %collective-permute-start.11 = (f32[40,768]{1,0:T(8,128)S(1)}, f32[40,768]{1,0:T(8,128)S(1)}, u32[]{:S(2)}, u32[]{:S(2)}) collective-permute-start(f32[40,768]{1,0:T(8,128)S(1)} %add_add_fusion), channel_id=1, source_target_pairs={{0,3},{1,2},{2,1},{3,0},{4,7},{5,6},{6,5},{7,4},{8,11},{9,10},{10,... | collective-permute-start | bytes 368648 | tf_op jit(solution)/shard_map/ppermute | solution.py:810
  60.4 6.3 %collective-permute-start.10 = (f32[40,768]{1,0:T(8,128)S(1)}, f32[40,768]{1,0:T(8,128)S(1)}, u32[]{:S(2)}, u32[]{:S(2)}) collective-permute-start(f32[40,768]{1,0:T(8,128)S(1)} %add_add_fusion), channel_id=1, source_target_pairs={{0,2},{1,3},{2,0},{3,1},{4,6},{5,7},{6,4},{7,5},{8,10},{9,11},{10,... | collective-permute-start | bytes 368648 | tf_op jit(solution)/shard_map/ppermute | solution.py:810
  66.8 1.9 %collective-permute-start.12 = (f32[160,768]{1,0:T(8,128)S(1)}, f32[160,768]{1,0:T(8,128)S(1)}, u32[]{:S(2)}, u32[]{:S(2)}) collective-permute-start(f32[160,768]{1,0:T(8,128)S(1)} %constant_dynamic-update-slice_fusion.mine_ref), channel_id=1, source_target_pairs={{0,16},{16,0},{1,17},{17,1},{2,18},{18,2},{3,19},{19,3},{4,20},{20... | collective-permute-start | bytes 1474568 | tf_op jit(solution)/shard_map/ppermute | solution.py:812

commit v7 on v6

--- a/solution.py
+++ b/solution.py
@@ -11,7 +11,7 @@
 HIGH = lax.Precision.HIGHEST
 ROWS = 16
 TAPS = 4
-TABLE_BATCH, MIX_BATCH, LATENT_BATCH = 2, 4, 4
+TABLE_BATCH, MIX_BATCH, LATENT_BATCH = 1, 4, 4
 RING = 18
 RELS = (-2, -1, 0, 1, 2, 3)
 NT = (((1,), (1,)), ((), ()))

time: 70.9 us -> 70.8 us (level)
  no operation moved by 1% of the time
where the time goes in v7:
time: 70.8 us; the launch traced here: 70.5 us
  Pallas kernels  34.4 us (49%)
  starting transfers between devices  21.6 us (31%)
  waiting for transfers between devices  13.3 us (19%)
  between operations  0.82 us (1%)
    pallas_call x1, Pallas kernels, near_call(): pl.pallas_call(near_kernel, out_shape=[pltpu.VMEM((8, width), F32)] + [pl...  15.5 us
    pallas_call x1, Pallas kernels, table_call(): pl.pallas_call(table_kernel, out_shape=(pltpu.VMEM((vocab, width), F32),...  9.75 us
    ppermute x3, starting transfers between devices, exchange_sum(): lax.ppermute(v, axis, partners(axis, m << low))  5.75 us
    ppermute x1, starting transfers between devices, per_device(): left = lax.ppermute(byte_ids, 'seq', up)  5.48 us
    ppermute x4, starting transfers between devices, scatter_sum(): lax.ppermute(part(v, places[m], size), axis, partners(axis, m << low))  5.47 us
    ppermute x3, waiting for transfers between devices, exchange_sum(): lax.ppermute(v, axis, partners(axis, m << low))  5.11 us
    ppermute x3, waiting for transfers between devices, per_device(): lax.ppermute(both, axis, partners(axis, m << low))  4.66 us
    pallas_call x1, Pallas kernels, latent_call(): pl.pallas_call(latent_kernel, out_shape=jax.ShapeDtypeStruct(shape, F32),...  4.06 us
  transfers between devices with their start and end apart: 13, of which 5 were waited for; matrix products, arithmetic and copies ran while one was open for 0% of the time, Pallas kernels for 32%

profile of v7, /device:TPU:0, one launch (start us, length us, event | category | flops | bytes accessed | tf_op | source)
XLA Modules:
  0.0 70.5 jit_solution(11653931706237539913)
XLA Ops:
  0.6 0.1 pad_add_fusion.place_ref
  0.7 1.3 %collective-permute-start.1 = (s32[16,256]{1,0:T(8,128)}, s32[16,256]{1,0:T(8,128)S(1)}, u32[]{:S(2)}, u32[]{:S(2)}) collective-permute-start(s32[16,256]{1,0:T(8,128)} %ids_hbm), channel_id=1, source_target_pairs={{1,0},{2,1},{3,2},{4,3},{5,4},{6,5},{7,6},{8,7},{9,8},{10,9},{11,1... | collective-permute-start | bytes 49160 | tf_op jit(solution)/shard_map/ppermute | solution.py:792
  2.0 5.5 %collective-permute-start = (s32[16,256]{1,0:T(8,128)}, s32[16,256]{1,0:T(8,128)S(1)}, u32[]{:S(2)}, u32[]{:S(2)}) collective-permute-start(s32[16,256]{1,0:T(8,128)} %ids_hbm), channel_id=1, source_target_pairs={{0,1},{1,2},{2,3},{3,4},{4,5},{5,6},{6,7},{7,8},{8,9},{9,10},{10,1... | collective-permute-start | bytes 49160 | tf_op jit(solution)/shard_map/ppermute | solution.py:791
  7.5 3.2 %prep.1 = (f32[8,256]{1,0:T(8,128)S(1)}, bf16[256,768]{1,0:T(8,128)(2,1)S(1)}, bf16[256,768]{1,0:T(8,128)(2,1)S(1)}, s32[32,128]{1,0:T(8,128)S(1)}, s32[32,128]{...) custom-call(s32[1]{0:T(128)} %bitcast.start_hbm, ...), custom_call_target="tpu_custom_call" | custom-call | flops 100000000 | bytes 1000000 | tf_op jit(solution)/shard_map/prep/pallas_call | solution.py:644
  10.8 9.7 %table_grad.1 = (f32[256,768]{1,0:T(8,128)S(1)}, f32[8,32,128]{2,1,0:T(8,128)S(1)}, s32[48,128]{1,0:T(8,128)S(1)}, bf16[2560,128]{1,0:T(8,128)(2,1)S(1)}, bf16[2...) custom-call(s32[32,128]{1,0:T(8,128)S(1)} %get-tuple-element.48.even, ...), custom_call_target="tpu_custom_call" | custom-call | flops 8000000000 | bytes 20000000 | tf_op jit(solution)/shard_map/table_grad/pallas_call | solution.py:676
  20.6 0.1 collective-permute-start.2
  20.6 1.7 %collective-permute-done.2 = f32[128,768]{1,0:T(8,128)S(1)} collective-permute-done((f32[128,768]{1,0:T(8,128)S(1)}, f32[128,768]{1,0:T(8,128)S(1)}, u32[]{:S(2)}, u32[]{:S(2)}) %collective-permute-start.2) | collective-permute-done | bytes 393248 | tf_op jit(solution)/shard_map/ppermute | solution.py:760
  22.3 0.1 dynamic-slice_add_fusion
  22.5 3.0 %collective-permute-start.3 = (f32[32,768]{1,0:T(8,128)S(1)}, f32[32,768]{1,0:T(8,128)S(1)}, u32[]{:S(2)}, u32[]{:S(2)}) collective-permute-start(f32[32,768]{1,0:T(8,128)S(1)} %get-tuple-element.87), channel_id=1, source_target_pairs={{0,1},{1,0},{2,3},{3,2},{4,5},{5,4},{6,7},{7,6},{8,9},{9,8},{10,11... | collective-permute-start | bytes 294920 | tf_op jit(solution)/shard_map/ppermute | solution.py:760
  25.4 1.9 %collective-permute-start.5 = (f32[32,768]{1,0:T(8,128)S(1)}, f32[32,768]{1,0:T(8,128)S(1)}, u32[]{:S(2)}, u32[]{:S(2)}) collective-permute-start(f32[32,768]{1,0:T(8,128)S(1)} %get-tuple-element.88), channel_id=1, source_target_pairs={{0,3},{1,2},{2,1},{3,0},{4,7},{5,6},{6,5},{7,4},{8,11},{9,10},{10,... | collective-permute-start | bytes 294920 | tf_op jit(solution)/shard_map/ppermute | solution.py:760
  27.4 0.5 collective-permute-start.4
  27.9 15.5 %near.1 = (f32[8,768]{1,0:T(8,128)S(1)}, bf16[2176,768]{1,0:T(8,128)(2,1)S(1)}, bf16[2176,768]{1,0:T(8,128)(2,1)S(1)}, bf16[2176,768]{1,0:T(8,128)(2,1)S(1)}, bf16[2176,768]{1,0:T(8,128)(2,1)S(1)}) custom-call(s32[32,128]{1,0:T(8,128)S(1)} %get-tuple-element.48.even_ref, s32[32,128]{1,0:T(8,128)S(1)} %get-tuple-element.49.length_ref, ...), custom_call_target="tpu_custom_call" | custom-call | flops 16000000000 | bytes 40000000 | tf_op jit(solution)/shard_map/near/pallas_call | solution.py:705
  43.4 5.1 %collective-permute-start.8 = (f32[40,768]{1,0:T(8,128)S(1)}, f32[40,768]{1,0:T(8,128)S(1)}, u32[]{:S(2)}, u32[]{:S(2)}) collective-permute-start(f32[40,768]{1,0:T(8,128)S(1)} %pad_maximum_fusion), channel_id=1, source_target_pairs={{0,12},{1,13},{2,14},{3,15},{4,8},{5,9},{6,10},{7,11},{8,4},{9,5},... | collective-permute-start | bytes 368648 | tf_op jit(solution)/shard_map/ppermute | solution.py:766
  48.5 0.6 collective-permute-start.6
  49.2 4.1 %latent.1 = f32[16,128,768]{2,1,0:T(8,128)} custom-call(bf16[2176,768]{1,0:T(8,128)(2,1)S(1)} %get-tuple-element.74.high0, bf16[2176,768]{1,0:T(8,128)(2,1)S(1)} %get-tuple-element.75.low0, bf16[2176,768]{1,0:T(8,128)(2,1)S(1)} %get-tuple-element.76.high1, bf16[2176,768]{1,0:T(8,128)(2,1)S(1)} %get-tuple-element.77.low1, ...), custom_call_target="tpu_custom_call" | custom-call | flops 4000000000 | bytes 10000000 | tf_op jit(solution)/shard_map/latent/pallas_call | solution.py:726
  53.3 5.1 %collective-permute-done.7 = f32[40,768]{1,0:T(8,128)S(1)} collective-permute-done((f32[40,768]{1,0:T(8,128)S(1)}, f32[40,768]{1,0:T(8,128)S(1)}, u32[]{:S(2)}, u32[]{:S(2)}) %collective-permute-start.7) | collective-permute-done | bytes 122912 | tf_op jit(solution)/shard_map/ppermute | solution.py:766
  58.4 0.4 collective-permute-start.9
  58.8 1.5 %collective-permute-start.11 = (f32[40,768]{1,0:T(8,128)S(1)}, f32[40,768]{1,0:T(8,128)S(1)}, u32[]{:S(2)}, u32[]{:S(2)}) collective-permute-start(f32[40,768]{1,0:T(8,128)S(1)} %add_add_fusion), channel_id=1, source_target_pairs={{0,3},{1,2},{2,1},{3,0},{4,7},{5,6},{6,5},{7,4},{8,11},{9,10},{10,... | collective-permute-start | bytes 368648 | tf_op jit(solution)/shard_map/ppermute | solution.py:810
  60.3 1.6 %collective-permute-start.10 = (f32[40,768]{1,0:T(8,128)S(1)}, f32[40,768]{1,0:T(8,128)S(1)}, u32[]{:S(2)}, u32[]{:S(2)}) collective-permute-start(f32[40,768]{1,0:T(8,128)S(1)} %add_add_fusion), channel_id=1, source_target_pairs={{0,2},{1,3},{2,0},{3,1},{4,6},{5,7},{6,4},{7,5},{8,10},{9,11},{10,... | collective-permute-start | bytes 368648 | tf_op jit(solution)/shard_map/ppermute | solution.py:810
  62.0 2.1 %collective-permute-done.9 = f32[40,768]{1,0:T(8,128)S(1)} collective-permute-done((f32[40,768]{1,0:T(8,128)S(1)}, f32[40,768]{1,0:T(8,128)S(1)}, u32[]{:S(2)}, u32[]{:S(2)}) %collective-permute-start.9) | collective-permute-done | bytes 122912 | tf_op jit(solution)/shard_map/ppermute | solution.py:810
  64.1 2.5 %collective-permute-done.10 = f32[40,768]{1,0:T(8,128)S(1)} collective-permute-done((f32[40,768]{1,0:T(8,128)S(1)}, f32[40,768]{1,0:T(8,128)S(1)}, u32[]{:S(2)}, u32[]{:S(2)}) %collective-permute-start.10) | collective-permute-done | bytes 122912 | tf_op jit(solution)/shard_map/ppermute | solution.py:810
  66.7 0.1 collective-permute-start.12
  66.8 1.9 %collective-permute-done.12.theirs_ref = f32[160,768]{1,0:T(8,128)S(1)} collective-permute-done((f32[160,768]{1,0:T(8,128)S(1)}, f32[160,768]{1,0:T(8,128)S(1)}, u32[]{:S(2)}, u32[]{:S(2)}) %collective-permute-start.12) | collective-permute-done | bytes 491552 | tf_op jit(solution)/shard_map/ppermute | solution.py:812
  68.6 1.9 %final.1 = (f32[256,768]{1,0:T(8,128)}, f32[4,768]{1,0:T(4,128)}, f32[768]{0:T(1024)}, f32[768]{0:T(1024)}) custom-call(s32[2]{0:T(128)S(1)} %pad_add_fusion.place_ref, f32[160,768]{1,0:T(8,128)S(1)} %constant_dynamic-update-slice_fusion.mine_ref, f32[160,768]{1,0:T(8,128)S(1)} %collective-permute-done.12.theirs_ref, f32[4,768]{1,0:T(4,128)S(1)} %get-tuple-element.52.w_ref, ...), custom_call_target="tpu_custom_call" | custom-call | tf_op jit(solution)/shard_map/final/pallas_call | solution.py:814
  (18 shorter events, 0.2 us)
Async XLA Ops:
  0.7 10.0 %collective-permute-start.1 = (s32[16,256]{1,0:T(8,128)}, s32[16,256]{1,0:T(8,128)S(1)}, u32[]{:S(2)}, u32[]{:S(2)}) collective-permute-start(s32[16,256]{1,0:T(8,128)} %ids_hbm), channel_id=1, source_target_pairs={{1,0},{2,1},{3,2},{4,3},{5,4},{6,5},{7,6},{8,7},{9,8},{10,9},{11,1... | collective-permute-start | bytes 49160 | tf_op jit(solution)/shard_map/ppermute | solution.py:792
  2.0 8.7 %collective-permute-start = (s32[16,256]{1,0:T(8,128)}, s32[16,256]{1,0:T(8,128)S(1)}, u32[]{:S(2)}, u32[]{:S(2)}) collective-permute-start(s32[16,256]{1,0:T(8,128)} %ids_hbm), channel_id=1, source_target_pairs={{0,1},{1,2},{2,3},{3,4},{4,5},{5,6},{6,7},{7,8},{8,9},{9,10},{10,1... | collective-permute-start | bytes 49160 | tf_op jit(solution)/shard_map/ppermute | solution.py:791
  20.6 1.8 %collective-permute-start.2 = (f32[128,768]{1,0:T(8,128)S(1)}, f32[128,768]{1,0:T(8,128)S(1)}, u32[]{:S(2)}, u32[]{:S(2)}) collective-permute-start(f32[128,768]{1,0:T(8,128)S(1)} %constant_dynamic-slice_fusion.3), channel_id=1, source_target_pairs={{0,16},{16,0},{1,17},{17,1},{2,18},{18,2},{3,19},{19,3},{4,20},{20... | collective-permute-start | bytes 1179656 | tf_op jit(solution)/shard_map/ppermute | solution.py:760
  22.5 20.9 %collective-permute-start.3 = (f32[32,768]{1,0:T(8,128)S(1)}, f32[32,768]{1,0:T(8,128)S(1)}, u32[]{:S(2)}, u32[]{:S(2)}) collective-permute-start(f32[32,768]{1,0:T(8,128)S(1)} %get-tuple-element.87), channel_id=1, source_target_pairs={{0,1},{1,0},{2,3},{3,2},{4,5},{5,4},{6,7},{7,6},{8,9},{9,8},{10,11... | collective-permute-start | bytes 294920 | tf_op jit(solution)/shard_map/ppermute | solution.py:760
  25.4 17.9 %collective-permute-start.5 = (f32[32,768]{1,0:T(8,128)S(1)}, f32[32,768]{1,0:T(8,128)S(1)}, u32[]{:S(2)}, u32[]{:S(2)}) collective-permute-start(f32[32,768]{1,0:T(8,128)S(1)} %get-tuple-element.88), channel_id=1, source_target_pairs={{0,3},{1,2},{2,1},{3,0},{4,7},{5,6},{6,5},{7,4},{8,11},{9,10},{10,... | collective-permute-start | bytes 294920 | tf_op jit(solution)/shard_map/ppermute | solution.py:760
  27.4 16.0 %collective-permute-start.4 = (f32[32,768]{1,0:T(8,128)S(1)}, f32[32,768]{1,0:T(8,128)S(1)}, u32[]{:S(2)}, u32[]{:S(2)}) collective-permute-start(f32[32,768]{1,0:T(8,128)S(1)} %get-tuple-element.89), channel_id=1, source_target_pairs={{0,2},{1,3},{2,0},{3,1},{4,6},{5,7},{6,4},{7,5},{8,10},{9,11},{10,... | collective-permute-start | bytes 294920 | tf_op jit(solution)/shard_map/ppermute | solution.py:760
  43.4 9.8 %collective-permute-start.8 = (f32[40,768]{1,0:T(8,128)S(1)}, f32[40,768]{1,0:T(8,128)S(1)}, u32[]{:S(2)}, u32[]{:S(2)}) collective-permute-start(f32[40,768]{1,0:T(8,128)S(1)} %pad_maximum_fusion), channel_id=1, source_target_pairs={{0,12},{1,13},{2,14},{3,15},{4,8},{5,9},{6,10},{7,11},{8,4},{9,5},... | collective-permute-start | bytes 368648 | tf_op jit(solution)/shard_map/ppermute | solution.py:766
  48.5 9.8 %collective-permute-start.7 = (f32[40,768]{1,0:T(8,128)S(1)}, f32[40,768]{1,0:T(8,128)S(1)}, u32[]{:S(2)}, u32[]{:S(2)}) collective-permute-start(f32[40,768]{1,0:T(8,128)S(1)} %pad_maximum_fusion), channel_id=1, source_target_pairs={{0,8},{1,9},{2,10},{3,11},{4,12},{5,13},{6,14},{7,15},{8,0},{9,1},... | collective-permute-start | bytes 368648 | tf_op jit(solution)/shard_map/ppermute | solution.py:766
  48.5 9.8 %collective-permute-start.6 = (f32[40,768]{1,0:T(8,128)S(1)}, f32[40,768]{1,0:T(8,128)S(1)}, u32[]{:S(2)}, u32[]{:S(2)}) collective-permute-start(f32[40,768]{1,0:T(8,128)S(1)} %pad_maximum_fusion), channel_id=1, source_target_pairs={{0,4},{1,5},{2,6},{3,7},{4,0},{5,1},{6,2},{7,3},{8,12},{9,13},{10,... | collective-permute-start | bytes 368648 | tf_op jit(solution)/shard_map/ppermute | solution.py:766
  58.4 5.7 %collective-permute-start.9 = (f32[40,768]{1,0:T(8,128)S(1)}, f32[40,768]{1,0:T(8,128)S(1)}, u32[]{:S(2)}, u32[]{:S(2)}) collective-permute-start(f32[40,768]{1,0:T(8,128)S(1)} %add_add_fusion), channel_id=1, source_target_pairs={{0,1},{1,0},{2,3},{3,2},{4,5},{5,4},{6,7},{7,6},{8,9},{9,8},{10,11... | collective-permute-start | bytes 368648 | tf_op jit(solution)/shard_map/ppermute | solution.py:810
  58.8 7.8 %collective-permute-start.11 = (f32[40,768]{1,0:T(8,128)S(1)}, f32[40,768]{1,0:T(8,128)S(1)}, u32[]{:S(2)}, u32[]{:S(2)}) collective-permute-start(f32[40,768]{1,0:T(8,128)S(1)} %add_add_fusion), channel_id=1, source_target_pairs={{0,3},{1,2},{2,1},{3,0},{4,7},{5,6},{6,5},{7,4},{8,11},{9,10},{10,... | collective-permute-start | bytes 368648 | tf_op jit(solution)/shard_map/ppermute | solution.py:810
  60.3 6.3 %collective-permute-start.10 = (f32[40,768]{1,0:T(8,128)S(1)}, f32[40,768]{1,0:T(8,128)S(1)}, u32[]{:S(2)}, u32[]{:S(2)}) collective-permute-start(f32[40,768]{1,0:T(8,128)S(1)} %add_add_fusion), channel_id=1, source_target_pairs={{0,2},{1,3},{2,0},{3,1},{4,6},{5,7},{6,4},{7,5},{8,10},{9,11},{10,... | collective-permute-start | bytes 368648 | tf_op jit(solution)/shard_map/ppermute | solution.py:810
  66.7 1.9 %collective-permute-start.12 = (f32[160,768]{1,0:T(8,128)S(1)}, f32[160,768]{1,0:T(8,128)S(1)}, u32[]{:S(2)}, u32[]{:S(2)}) collective-permute-start(f32[160,768]{1,0:T(8,128)S(1)} %constant_dynamic-update-slice_fusion.mine_ref), channel_id=1, source_target_pairs={{0,16},{16,0},{1,17},{17,1},{2,18},{18,2},{3,19},{19,3},{4,20},{20... | collective-permute-start | bytes 1474568 | tf_op jit(solution)/shard_map/ppermute | solution.py:812
